TPU v7x, 32 devices: a whole 2x2x4 slice. The times are simulated.
32 devices in a mesh: dp: 8 (over z, x), tensor: 4 (over y, core).
Axes of the slice: x: 2, y: 2, z: 4, core: 2. Of those that a mesh axis runs over, the one named last changes fastest.
Arguments:
- tokens: bfloat16 [32768, 1536], P(('dp', 'tensor')), may hold values from -6 to 6
- lengths: int32 [8, 4], P('dp'), may hold values from 0 to 4096, as said below
- norm_gain: float32 [1536], replicated, may hold values from 0.1 to 1.9
- w_gate: bfloat16 [1536, 3072], P(None, 'tensor'), may hold values from -0.15625 to 0.15625
- w_value: bfloat16 [1536, 3072], P(None, 'tensor'), may hold values from -0.15625 to 0.15625
- w_shared: bfloat16 [1536, 256], replicated, may hold values from -0.15625 to 0.15625
- w_rate: bfloat16 [1536, 48], P(None, 'tensor'), may hold values from -0.15625 to 0.15625
- conv_value: float32 [3072, 4], P('tensor'), may hold values from -0.5 to 0.5
- value_bias: float32 [3072], P('tensor'), may hold values from -0.5 to 0.5
- conv_shared: float32 [256, 4], replicated, may hold values from -0.5 to 0.5
- shared_bias: float32 [256], replicated, may hold values from -0.5 to 0.5
- rate_bias: float32 [48], P('tensor'), may hold values from -6.9 to -2.3
- decay_log: float32 [48], P('tensor'), may hold values from 0 to 2.77
- skip_gain: float32 [48], P('tensor'), may hold values from 0.25 to 3.75, as said below
- mix_gain: float32 [3072], P('tensor'), may hold values from 0.1 to 1.9
- w_out: bfloat16 [3072, 1536], P('tensor'), may hold values from -0.109375 to 0.109375
- cotangent: bfloat16 [32768, 1536], P(('dp', 'tensor')), may hold values from -6 to 6
Outputs:
- block_out: bfloat16 [32768, 1536], P(('dp', 'tensor'))
- tokens_grad: float32 [32768, 1536], P(('dp', 'tensor'))
- norm_gain_grad: float32 [1536], replicated
- w_gate_grad: float32 [1536, 3072], P('dp', 'tensor')
- w_value_grad: float32 [1536, 3072], P('dp', 'tensor')
- w_shared_grad: float32 [1536, 256], replicated
- w_rate_grad: float32 [1536, 48], P('dp', 'tensor')
- conv_value_grad: float32 [3072, 4], P('tensor')
- value_bias_grad: float32 [3072], P('tensor')
- conv_shared_grad: float32 [256, 4], replicated
- shared_bias_grad: float32 [256], replicated
- rate_bias_grad: float32 [48], P('tensor')
- decay_log_grad: float32 [48], P('tensor')
- skip_gain_grad: float32 [48], P('tensor')
- mix_gain_grad: float32 [3072], P('tensor')
- w_out_grad: float32 [3072, 1536], P('tensor', 'dp')
Inputs may be any that keep to these rules, and one draw needn't show every extreme that they name: Each row lists its sequences' lengths from the first slot; each used entry is 1024 or more and the unused entries are 0 at the end; a row's lengths sum to more than half of 4096 and to 4096 at most; some row holds one sequence of exactly 4096. `skip_gain`: Positive.
All inputs are finite; a program needn't handle non-finite values.
Results may differ from a plain program's by a relative error of at most 0.0079.
Values may be sent and summed in bfloat16 or wider, within the bound.
No kernel may reach another device: no remote copies, remote signals or barrier semaphores. Data moves between devices by JAX's collectives and lax.ppermute only.
A program may use at most 320 MiB of HBM per device.

v0:
```python
from functools import partial

import jax
import jax.numpy as jnp
from jax import lax
from jax.sharding import PartitionSpec as P

D = 1536
GROUP = 256
INNER = 3072


EPS = 1e-05
HIGH = lax.Precision.HIGHEST


def segments_of(lengths_row, position_count):
    ends = jnp.cumsum(lengths_row)
    position = jnp.arange(position_count, dtype=jnp.int32)
    segment = jnp.sum((position[:, None] >= ends[None, :]).astype(jnp.int32), axis=1)
    validity = (position < ends[-1]).astype(jnp.float32)
    return (segment, validity)


def causal_conv(values, weight, offset_bias, segment):
    position_count = values.shape[0]
    taps = weight.shape[1]
    running = values * weight[:, taps - 1] + offset_bias
    for offset in range(1, taps):
        earlier = jnp.pad(values, ((offset, 0), (0, 0)))[:position_count]
        before = jnp.pad(segment, (offset, 0), constant_values=-1)[:position_count]
        running = (
            running
            + jnp.where((before == segment)[:, None], earlier, 0.0) * weight[:, taps - 1 - offset]
        )
    return running


def group_step(carried, block, decay_rate):
    state, last_segment = carried
    inputs, steps, b_block, c_block, segment = block
    length = steps.shape[0]
    head_count = steps.shape[1]
    head_size = inputs.shape[1] // head_count
    head_inputs = inputs.reshape(length, head_count, head_size)
    steps_major = steps.T
    cumulative = jnp.cumsum(steps_major * decay_rate[:, None], axis=1)
    order = jnp.arange(length)
    allowed = ((segment[:, None] == segment[None, :]) & (order[:, None] >= order[None, :]))[
        None, :, :
    ]
    spread = cumulative[:, :, None] - cumulative[:, None, :]
    decays = jnp.where(allowed, jnp.exp(jnp.where(allowed, spread, 0.0)), 0.0)
    scores = jnp.dot(c_block, b_block.T, precision=HIGH)
    weights = decays * scores[None, :, :] * steps_major[:, None, :]
    inside = jnp.einsum("hts,shp->thp", weights, head_inputs, precision=HIGH)
    carries = (segment == last_segment).astype(jnp.float32)
    from_state = jnp.einsum("tn,hpn->thp", c_block, state, precision=HIGH)
    outside = from_state * (jnp.exp(cumulative).T * carries[:, None])[:, :, None]
    end_segment = segment[length - 1]
    tails = (
        jnp.exp(cumulative[:, length - 1 :] - cumulative)
        * (segment == end_segment).astype(jnp.float32)[None, :]
        * steps_major
    )
    fresh = jnp.einsum("shp,sn->hpn", head_inputs * tails.T[:, :, None], b_block, precision=HIGH)
    kept_share = (end_segment == last_segment).astype(jnp.float32)
    state = state * (jnp.exp(cumulative[:, length - 1]) * kept_share)[:, None, None] + fresh
    return ((state, end_segment), (inside + outside).reshape(length, head_count * head_size))


def state_space(inputs, steps, decay_rate, b_rows, c_rows, segment):
    position_count, channel_count = inputs.shape
    head_count = steps.shape[1]
    group_count = position_count // GROUP
    blocks = (
        inputs.reshape(group_count, GROUP, channel_count),
        steps.reshape(group_count, GROUP, head_count),
        b_rows.reshape(group_count, GROUP, b_rows.shape[1]),
        c_rows.reshape(group_count, GROUP, c_rows.shape[1]),
        segment.reshape(group_count, GROUP),
    )
    initial = (
        jnp.zeros((head_count, channel_count // head_count, b_rows.shape[1]), jnp.float32),
        jnp.array(-1, jnp.int32),
    )
    stepper = jax.checkpoint(partial(group_step, decay_rate=decay_rate))
    finished, outputs = lax.scan(stepper, initial, blocks)
    return outputs.reshape(position_count, channel_count)


def row_mixer(
    gate,
    value,
    shared,
    rate,
    segment,
    conv_value,
    value_bias,
    conv_shared,
    shared_bias,
    rate_bias,
    decay_log,
    skip_gain,
):
    head_count = rate.shape[1]
    head_size = value.shape[1] // head_count
    value_act = jax.nn.silu(causal_conv(value, conv_value, value_bias, segment))
    shared_act = jax.nn.silu(causal_conv(shared, conv_shared, shared_bias, segment))
    state_size = shared.shape[1] // 2
    steps = jax.nn.softplus(rate + rate_bias)
    mixed_heads = state_space(
        value_act,
        steps,
        -jnp.exp(decay_log),
        shared_act[:, :state_size],
        shared_act[:, state_size:],
        segment,
    )
    mixed_heads = mixed_heads + jnp.repeat(skip_gain, head_size)[None, :] * value_act
    return mixed_heads * jax.nn.silu(gate)


def shards(
    tokens,
    lengths,
    norm_gain,
    w_gate,
    w_value,
    w_shared,
    w_rate,
    conv_value,
    value_bias,
    conv_shared,
    shared_bias,
    rate_bias,
    decay_log,
    skip_gain,
    mix_gain,
    w_out,
    cotangent,
):
    row_count = lengths.shape[0]
    residual = tokens.astype(jnp.float32)
    inverse_in = lax.rsqrt(jnp.mean(residual * residual, axis=1, keepdims=True) + EPS)
    normed = (residual * inverse_in * norm_gain).astype(jnp.bfloat16)
    gathered = lax.all_gather(normed, "tensor", axis=0, tiled=True)
    all_rows = gathered.shape[0]
    positions = all_rows // row_count
    segment, validity = jax.vmap(partial(segments_of, position_count=positions))(lengths)
    validity = validity.reshape(all_rows, 1)
    gate = jnp.dot(gathered, w_gate, preferred_element_type=jnp.float32)
    value = jnp.dot(gathered, w_value, preferred_element_type=jnp.float32)
    shared = jnp.dot(gathered, w_shared, preferred_element_type=jnp.float32)
    rate = jnp.dot(gathered, w_rate, preferred_element_type=jnp.float32)

    def mixer_all(
        gate_in,
        value_in,
        shared_in,
        rate_in,
        conv_v,
        bias_v,
        conv_s,
        bias_s,
        bias_rate,
        decay_in,
        skip_in,
    ):
        shaped = [
            member.reshape(row_count, positions, member.shape[1])
            for member in (gate_in, value_in, shared_in, rate_in)
        ]
        result = jax.vmap(
            row_mixer, in_axes=(0, 0, 0, 0, 0, None, None, None, None, None, None, None)
        )(
            shaped[0],
            shaped[1],
            shaped[2],
            shaped[3],
            segment,
            conv_v,
            bias_v,
            conv_s,
            bias_s,
            bias_rate,
            decay_in,
            skip_in,
        )
        return result.reshape(all_rows, result.shape[2])

    params = (conv_value, value_bias, conv_shared, shared_bias, rate_bias, decay_log, skip_gain)
    gated = mixer_all(gate, value, shared, rate, *params)
    squares = lax.psum(jnp.sum(gated * gated, axis=1), "tensor")
    inverse_mix = lax.rsqrt(squares[:, None] / INNER + EPS)
    mixed = (gated * inverse_mix * mix_gain * validity).astype(jnp.bfloat16)
    out_terms = lax.psum_scatter(
        jnp.dot(mixed, w_out, preferred_element_type=jnp.float32),
        "tensor",
        scatter_dimension=0,
        tiled=True,
    )
    block_out = (residual + out_terms).astype(jnp.bfloat16)
    back_rows = lax.all_gather(cotangent, "tensor", axis=0, tiled=True)
    back_mixed = lax.dot_general(
        back_rows, w_out, (((1,), (1,)), ((), ())), preferred_element_type=jnp.float32
    )
    grad_out = lax.dot_general(
        mixed, back_rows, (((0,), (0,)), ((), ())), preferred_element_type=jnp.float32
    )
    gated_again, pull_mixer = jax.vjp(mixer_all, gate, value, shared, rate, *params)
    weighted = back_mixed * mix_gain * validity
    dots_local = jnp.sum(weighted * gated_again, axis=1)
    squares_again, dots = lax.psum(
        (jnp.sum(gated_again * gated_again, axis=1), dots_local), "tensor"
    )
    inverse_back = lax.rsqrt(squares_again[:, None] / INNER + EPS)
    grad_mix = jnp.sum(back_mixed * validity * gated_again * inverse_back, axis=0)
    back_gated = (
        weighted * inverse_back
        - gated_again * (inverse_back * inverse_back * inverse_back) * dots[:, None] / INNER
    )
    pulled = pull_mixer(back_gated)
    low_gate = pulled[0].astype(jnp.bfloat16)
    low_value = pulled[1].astype(jnp.bfloat16)
    low_rate = pulled[3].astype(jnp.bfloat16)
    shared_own = lax.psum_scatter(pulled[2], "tensor", scatter_dimension=0, tiled=True).astype(
        jnp.bfloat16
    )
    contract_rows = (((0,), (0,)), ((), ()))
    grad_gate = lax.dot_general(
        gathered, low_gate, contract_rows, preferred_element_type=jnp.float32
    )
    grad_value = lax.dot_general(
        gathered, low_value, contract_rows, preferred_element_type=jnp.float32
    )
    grad_rate = lax.dot_general(
        gathered, low_rate, contract_rows, preferred_element_type=jnp.float32
    )
    grad_shared = lax.dot_general(
        normed, shared_own, contract_rows, preferred_element_type=jnp.float32
    )
    contract_cols = (((1,), (1,)), ((), ()))
    part_gate = lax.dot_general(low_gate, w_gate, contract_cols, preferred_element_type=jnp.float32)
    part_value = lax.dot_general(
        low_value, w_value, contract_cols, preferred_element_type=jnp.float32
    )
    part_rate = lax.dot_general(low_rate, w_rate, contract_cols, preferred_element_type=jnp.float32)
    back_normed = lax.psum_scatter(
        part_gate + part_value + part_rate, "tensor", scatter_dimension=0, tiled=True
    )
    back_normed = back_normed + lax.dot_general(
        shared_own, w_shared, contract_cols, preferred_element_type=jnp.float32
    )
    grad_norm = jnp.sum(back_normed * residual * inverse_in, axis=0)
    scaled = back_normed * norm_gain
    tokens_grad = (
        cotangent.astype(jnp.float32)
        + scaled * inverse_in
        - residual
        * (inverse_in * inverse_in * inverse_in)
        * jnp.sum(scaled * residual, axis=1, keepdims=True)
        / D
    )
    grad_gate, grad_value, grad_rate = (
        lax.psum_scatter(grad_gate, "dp", scatter_dimension=0, tiled=True),
        lax.psum_scatter(grad_value, "dp", scatter_dimension=0, tiled=True),
        lax.psum_scatter(grad_rate, "dp", scatter_dimension=0, tiled=True),
    )
    grad_out = lax.psum_scatter(grad_out, "dp", scatter_dimension=1, tiled=True)
    smalls = lax.psum((pulled[4], pulled[5], pulled[8], pulled[9], pulled[10], grad_mix), "dp")
    shared_sums = lax.psum((grad_shared, pulled[6], pulled[7], grad_norm), ("dp", "tensor"))
    return (
        block_out,
        tokens_grad,
        shared_sums[3],
        grad_gate,
        grad_value,
        shared_sums[0],
        grad_rate,
        smalls[0],
        smalls[1],
        shared_sums[1],
        shared_sums[2],
        smalls[2],
        smalls[3],
        smalls[4],
        smalls[5],
        grad_out,
    )


def solution(mesh):
    in_specs = (
        P(("dp", "tensor"), None),
        P("dp", None),
        P(),
        P(None, "tensor"),
        P(None, "tensor"),
        P(),
        P(None, "tensor"),
        P("tensor", None),
        P("tensor"),
        P(),
        P(),
        P("tensor"),
        P("tensor"),
        P("tensor"),
        P("tensor"),
        P("tensor", None),
        P(("dp", "tensor"), None),
    )
    out_specs = (
        P(("dp", "tensor"), None),
        P(("dp", "tensor"), None),
        P(),
        P("dp", "tensor"),
        P("dp", "tensor"),
        P(),
        P("dp", "tensor"),
        P("tensor", None),
        P("tensor"),
        P(),
        P(),
        P("tensor"),
        P("tensor"),
        P("tensor"),
        P("tensor"),
        P("tensor", "dp"),
    )
    return jax.shard_map(shards, mesh=mesh, in_specs=in_specs, out_specs=out_specs, check_vma=False)
```

profile of v0, /device:TPU:0, one launch (start us, length us, event | category | flops | bytes accessed | tf_op | source)
XLA Modules:
  0.0 3471.0 jit_solution(8506085469276071337)
XLA Ops:
  26.3 74.2 %all-gather.3.cloned.1.call-done = bf16[4096,1536]{1,0:T(8,128)(2,1)} async-done(((bf16[1024,1536]{1,0:T(8,128)(2,1)}), bf16[4096,1536]{1,0:T(8,128)(2,1)}) %all-gather.3.cloned.1.call-update) | async-done | bytes 12582928 | tf_op jit(solution)/shard_map/all_gather | solution.py:147
  116.2 13.1 fusion.220
  129.4 13.4 fusion.160
  142.9 12.6 copy.240
  170.8 423.8 %while.62 = (s32[]{:T(128)}, f32[1,12,64,128]{3,2,1,0:T(8,128)S(1)}, s32[1]{0:T(128)}, f32[16,1,256,768]{3,2,0,1:T(8,128)}, f32[16,1,12,64,128]{4,3,2,1,0:T(8,12...) while((s32[]{:T(128)}, ...), condition=%wide.region_13.14_spmd.clone, body=%wide.region_10.13_spmd.clone.sunk | while | flops 1314245632 | bytes 14795287 | solution.py:88
  600.4 399.6 %while.61 = (s32[]{:T(128)}, f32[1,12,64,128]{3,2,1,0:T(8,128)S(1)}, s32[1]{0:T(128)}, f32[16,1,256,768]{3,2,0,1:T(8,128)}, f32[16,1,256,12]{2,0,3,1:T(8,128)}, ...) while((s32[]{:T(128)}, ...), condition=%wide.region_6.7_spmd.clone, body=%wide.region_3.6_spmd.clone.sunk | while | flops 1314147328 | bytes 14007746 | solution.py:88
  1000.1 36.5 %bitcast_multiply_fusion.21 = (f32[1,4096,768]{2,1,0:T(8,128)}, f32[1,4096,768]{2,1,0:T(8,128)}, f32[4096,768]{1,0:T(8,128)}) fusion(f32[768]{0:T(1024)} %mul.1264, f32[16,1,256,768]{3,2,0,1:T(8,128)} %get-tuple-element.542, f32[1,4096,768]{2,1,0:T(8,128)} %get-tuple-element.1054, f32[16,1,256,768]{3,2,0,1:T(8,128)} %get-tuple-element.541, ...), kind=kOutput, calls=%fused_computation.267 | convolution fusion | flops 9704570880 | bytes 90442752 | tf_op jit(solution)/shard_map/dot_general | solution.py:152
  1042.0 10.7 psum.92
  1058.3 20.6 fusion.152
  1078.9 10.9 all-reduce.29
  1089.7 28.9 fusion.145
  1128.2 1363.0 %while.63 = (s32[]{:T(128)}, f32[12]{0:T(128)}, f32[1,12,64,128]{3,2,1,0:T(8,128)}, f32[16,1,256,768]{3,2,0,1:T(8,128)}, f32[16,1,256,12]{2,0,3,1:T(8,128)}, /*i...) while((s32[]{:T(128)}, f32[12]{0:T(128)}, ...), condition=%wide.region_32.33_spmd.clone, body=%wide.region_18.32_spmd.clone.sunk | while | flops 3038755840 | bytes 36137748 | solution.py:88
  2492.5 12.2 fusion.208
  2509.6 17.2 fusion.176
  2527.6 10.0 fusion.199
  2545.1 35.5 %fusion.207 = (f32[768]{0:T(1024)S(1)}, f32[768]{0:T(1024)S(1)}, f32[768]{0:T(1024)S(1)}, f32[768]{0:T(1024)S(1)}, f32[768]{0:T(1024)S(1)}, /*index=5*/f32[1,4096,768]{2,1,0:T(8,128)S(1)}) fusion(f32[4096,768]{1,0:T(8,128)} %copy-done.1, f32[1,4096,768]{2,1,0:T(8,128)} %bitcast.840, pred[4096]{0:T(1024)(128)(4,1)S(1)} %copy-done.28, ...), kind=kLoop, calls=%fused_computation.373 | loop fusion | flops 72347904 | bytes 75528192 | tf_op jit(solution)/shard_map/transpose(jvp(vmap()))/reduce_sum | solution.py:28
  2585.2 12.8 multiply_select_fusion.1
  2598.0 20.4 fusion.138
  2618.5 33.1 add_add_fusion
  2652.3 20.7 fusion.205
  2678.5 22.3 fusion.203
  2700.9 17.2 fusion.171
  2718.3 16.6 fusion.174
  2735.2 37.7 %all-reduce.28 = (f32[768,4]{0,1:T(4,128)}, f32[768]{0:T(1024)}, f32[12]{0:T(128)}, f32[12]{0:T(128)}, f32[12]{0:T(128)}, /*index=5*/f32[768]{0:T(1024)}) all-reduce(f32[768,4]{0,1:T(4,128)S(1)} %pad_add_fusion, f32[768]{0:T(1024)S(1)} %get-tuple-element.922, f32[12]{0:T(128)S(1)} %copy-done.75, ...), channel_id=1, replica_groups=mesh['dp'=8,'tensor'=4] {'dp'}, use_global_device_ids=true, to_apply=%region_46.47 | all-reduce | flops 4644 | bytes 37152 | tf_op jit(solution)/shard_map/psum | solution.py:271
  2774.5 68.7 %reduce-scatter.12.cloned.1.call-done = f32[1024,1536]{1,0:T(8,128)} async-done(((f32[4096,1536]{1,0:T(8,128)}), f32[1024,1536]{1,0:T(8,128)}) %reduce-scatter.12.cloned.1.call-update) | async-done | bytes 6291472 | tf_op jit(solution)/shard_map/reduce_scatter | solution.py:249
  2850.1 39.6 %all-reduce.27 = (f32[1536]{0:T(1024)}, f32[256,4]{0,1:T(4,128)}, f32[256]{0:T(256)}) all-reduce(f32[1536]{0:T(1024)S(1)} %get-tuple-element.927, f32[256,4]{0,1:T(4,128)S(1)} %pad_add_fusion.1, f32[256]{0:T(256)S(1)} %copy-done.67), channel_id=1, replica_groups=mesh['dp'=8,'tensor'=4] {'dp','tensor'}, use_global_device_ids=true, to_apply=%region_37.38 | all-reduce | flops 2816 | bytes 22528 | tf_op jit(solution)/shard_map/psum | solution.py:272
  2889.6 136.9 %reduce-scatter.10.cloned.1.call-done = f32[1024,1536]{1,0:T(8,128)} async-done(((f32[4096,1536]{1,0:T(8,128)}), f32[1024,1536]{1,0:T(8,128)}) %reduce-scatter.10.cloned.1.call-update) | async-done | bytes 6291472 | tf_op jit(solution)/shard_map/reduce_scatter | solution.py:197
  3026.5 11.0 fusion.167
  3037.4 127.0 %all-reduce.32.cloned.1.call-done = f32[1536,256]{1,0:T(8,128)} async-done(((f32[1536,256]{1,0:T(8,128)}), f32[1536,256]{1,0:T(8,128)}) %all-reduce.32.cloned.1.call-update) | async-done | bytes 1572880 | tf_op jit(solution)/shard_map/psum | solution.py:272
  3164.4 98.5 %reduce-scatter.20.cloned.1.call-done = f32[768,192]{0,1:T(8,128)} async-done(((f32[768,1536]{0,1:T(8,128)}), f32[768,192]{0,1:T(8,128)}) %reduce-scatter.20.cloned.1.call-update) | async-done | bytes 589840 | tf_op jit(solution)/shard_map/reduce_scatter | solution.py:270
  3263.0 99.3 %reduce-scatter.18.cloned.1.call-done = f32[192,768]{1,0:T(8,128)} async-done(((f32[1536,768]{1,0:T(8,128)}), f32[192,768]{1,0:T(8,128)}) %reduce-scatter.18.cloned.1.call-update) | async-done | bytes 589840 | tf_op jit(solution)/shard_map/reduce_scatter | solution.py:267
  3362.2 99.1 %reduce-scatter.16.cloned.1.call-done = f32[192,768]{1,0:T(8,128)} async-done(((f32[1536,768]{1,0:T(8,128)}), f32[192,768]{1,0:T(8,128)}) %reduce-scatter.16.cloned.1.call-update) | async-done | bytes 589840 | tf_op jit(solution)/shard_map/reduce_scatter | solution.py:266
  (3187 shorter events, 2226.6 us)
Async XLA Ops:
  7.2 992.9 %copy-start = (bf16[1536,768]{1,0:T(8,128)(2,1)S(1)}, bf16[1536,768]{1,0:T(8,128)(2,1)}, u32[]{:S(2)}) copy-start(bf16[1536,768]{1,0:T(8,128)(2,1)} %param.26) | copy-start | bytes 7077892
  7.2 93.4 %all-gather.3.cloned.1.call-start = ((), (), s32[]{:S(2)}) async-start(), calls=%async_computation.7 | async-start | bytes 15728640 | tf_op jit(solution)/shard_map/all_gather | solution.py:147
  11.2 89.4 %copy-start.20 = (bf16[1536,256]{1,0:T(8,128)(2,1)S(1)}, bf16[1536,256]{1,0:T(8,128)(2,1)}, u32[]{:S(2)}) copy-start(bf16[1536,256]{1,0:T(8,128)(2,1)} %param.28) | copy-start | bytes 2359300
  15.6 1042.7 %all-gather.5.cloned.1.call-start = ((), (), s32[]{:S(2)}) async-start(), calls=%async_computation.9 | async-start | bytes 15728640 | tf_op jit(solution)/shard_map/all_gather | solution.py:204
  16.3 2656.7 %reduce-scatter.14.cloned.1.call-start = ((), (), s32[]{:S(2)}) async-start(), calls=%async_computation.11 | async-start | bytes 5242880 | tf_op jit(solution)/shard_map/reduce_scatter | solution.py:227
  19.0 110.3 %copy-start.25 = (pred[4096]{0:T(1024)(128)(4,1)}, pred[4096]{0:T(1024)(128)(4,1)S(1)}, u32[]{:S(2)}) copy-start(pred[4096]{0:T(1024)(128)(4,1)S(1)} %get-tuple-element.937) | copy-start | bytes 12292
  19.0 110.3 %copy-start.27 = (pred[4096]{0:T(1024)(128)(4,1)}, pred[4096]{0:T(1024)(128)(4,1)S(1)}, u32[]{:S(2)}) copy-start(pred[4096]{0:T(1024)(128)(4,1)S(1)} %get-tuple-element.938) | copy-start | bytes 12292
  19.1 110.3 %copy-start.29 = (pred[4096]{0:T(1024)(128)(4,1)}, pred[4096]{0:T(1024)(128)(4,1)S(1)}, u32[]{:S(2)}) copy-start(pred[4096]{0:T(1024)(128)(4,1)S(1)} %get-tuple-element.939) | copy-start | bytes 12292
  21.2 108.2 %copy-start.44 = (f32[768]{0:T(1024)}, f32[768]{0:T(1024)S(1)}, u32[]{:S(2)}) copy-start(f32[768]{0:T(1024)S(1)} %get-tuple-element.940) | copy-start | bytes 9220
  1058.3 31.4 copy-start.42
  2509.5 263.4 %reduce-scatter.22.cloned.1.call-start = ((), (), s32[]{:S(2)}) async-start(), calls=%async_computation.16 | async-start | bytes 884736
  2509.5 17.2 copy-start.18
  2509.5 18.1 copy-start.32
  2545.1 40.1 %copy-start.47 = (f32[768]{0:T(1024)S(1)}, f32[768]{0:T(1024)}, u32[]{:S(2)}) copy-start(f32[768]{0:T(1024)} %get-tuple-element.941) | copy-start | bytes 9220
  2545.1 40.1 %copy-start.49 = (f32[768]{0:T(1024)S(1)}, f32[768]{0:T(1024)}, u32[]{:S(2)}) copy-start(f32[768]{0:T(1024)} %get-tuple-element.942) | copy-start | bytes 9220
  2545.1 40.1 %copy-start.51 = (f32[768]{0:T(1024)S(1)}, f32[768]{0:T(1024)}, u32[]{:S(2)}) copy-start(f32[768]{0:T(1024)} %get-tuple-element.943) | copy-start | bytes 9220
  2598.0 245.3 %reduce-scatter.12.cloned.1.call-start = ((), (), s32[]{:S(2)}) async-start(), calls=%async_computation.10 | async-start | bytes 31457280 | tf_op jit(solution)/shard_map/reduce_scatter | solution.py:249
  2651.6 374.9 %reduce-scatter.10.cloned.1.call-start = ((), (), s32[]{:S(2)}) async-start(), calls=%async_computation.8 | async-start | bytes 31457280 | tf_op jit(solution)/shard_map/reduce_scatter | solution.py:197
  2673.0 491.4 %all-reduce.32.cloned.1.call-start = ((), (), s32[]{:S(2)}) async-start(), calls=%async_computation.14 | async-start | bytes 3145728 | tf_op jit(solution)/shard_map/psum | solution.py:272
  2678.4 584.5 %reduce-scatter.20.cloned.1.call-start = ((), (), s32[]{:S(2)}) async-start(), calls=%async_computation.15 | async-start | bytes 5308416 | tf_op jit(solution)/shard_map/reduce_scatter | solution.py:270
  2700.8 661.4 %reduce-scatter.18.cloned.1.call-start = ((), (), s32[]{:S(2)}) async-start(), calls=%async_computation.13 | async-start | bytes 5308416 | tf_op jit(solution)/shard_map/reduce_scatter | solution.py:267
  2718.1 17.0 copy-start.73
  2718.1 54.7 %copy-start.68 = (f32[256]{0:T(256)S(1)}, f32[256]{0:T(256)}, u32[]{:S(2)}) copy-start(f32[256]{0:T(256)} %get-tuple-element.933) | copy-start | bytes 3076
  2718.1 54.7 %copy-start.69 = (f32[256]{0:T(256)S(1)}, f32[256]{0:T(256)}, u32[]{:S(2)}) copy-start(f32[256]{0:T(256)} %get-tuple-element.934) | copy-start | bytes 3076
  2718.2 54.7 %copy-start.70 = (f32[256]{0:T(256)S(1)}, f32[256]{0:T(256)}, u32[]{:S(2)}) copy-start(f32[256]{0:T(256)} %get-tuple-element.935) | copy-start | bytes 3076
  2718.2 54.7 %copy-start.71 = (f32[256]{0:T(256)S(1)}, f32[256]{0:T(256)}, u32[]{:S(2)}) copy-start(f32[256]{0:T(256)} %get-tuple-element.936) | copy-start | bytes 3076
  2718.2 125.1 %copy-start.19 = (f32[1024,256]{1,0:T(8,128)S(1)}, f32[1024,256]{1,0:T(8,128)}, u32[]{:S(2)}) copy-start(f32[1024,256]{1,0:T(8,128)} %reduce-scatter.14.cloned.1.call-done) | copy-start | bytes 3145732
  2718.2 125.1 %copy-start.33 = (f32[1536]{0:T(1024)S(1)}, f32[1536]{0:T(1024)}, u32[]{:S(2)}) copy-start(f32[1536]{0:T(1024)} %param.25) | copy-start | bytes 18436
  2718.2 125.1 %copy-start.37 = (f32[1024]{0:T(1024)S(1)}, f32[1024]{0:T(1024)}, u32[]{:S(2)}) copy-start(f32[1024]{0:T(1024)} %copy-done.36) | copy-start | bytes 12292
  2718.2 743.2 %reduce-scatter.16.cloned.1.call-start = ((), (), s32[]{:S(2)}) async-start(), calls=%async_computation.12 | async-start | bytes 5308416 | tf_op jit(solution)/shard_map/reduce_scatter | solution.py:266
  2774.5 75.5 %copy-start.67 = (f32[256]{0:T(256)S(1)}, f32[256]{0:T(256)}, u32[]{:S(2)}) copy-start(f32[256]{0:T(256)} %get-tuple-element.932) | copy-start | bytes 3076
  2774.5 252.0 %copy-start.52 = (f32[1024]{0:T(1024)S(1)}, f32[1024]{0:T(1024)}, u32[]{:S(2)}) copy-start(f32[1024]{0:T(1024)} %get-tuple-element.1082) | copy-start | bytes 12292
  (389 other events, 2295.6 us)
Sparse Core Ops, SparseCore 0:
  15.7 84.7 all-gather.2
  102.1 82.0 all-gather.4
  2509.6 45.1 reduce-scatter.13
  2598.1 63.1 reduce-scatter.21
  2663.8 179.4 reduce-scatter.11
  2845.9 180.5 reduce-scatter.9
  3032.3 132.0 all-reduce.31
  3168.6 94.2 reduce-scatter.19
  3267.2 95.0 reduce-scatter.17
  3366.3 95.0 reduce-scatter.15
where the time goes:
time: 3520 us; the launch traced here: 3470 us
  matrix products  987 us (28%)
  local copies, waits for them, and re-layouts  872 us (25%)
  other arithmetic  720 us (20%)
  waiting for transfers between devices  705 us (20%)
  blocking collectives  98.8 us (3%)
  loops' own time  72.6 us (2%)
    dot_general x64, matrix products, group_step(): inside = jnp.einsum('hts,shp->thp', weights, head_inputs, precision=HIGH)  349 us
    dynamic_update_slice x176, local copies, waits for them, and re-layouts, state_space(): finished, outputs = lax.scan(stepper, initial, blocks)  224 us
    another operation x501, local copies, waits for them, and re-layouts  210 us
    dot_general x80, matrix products, group_step(): from_state = jnp.einsum('tn,hpn->thp', c_block, state, precision=HIGH)  161 us
    reduce_scatter x1, waiting for transfers between devices, shards(): lax.psum_scatter(jnp.dot(mixed, w_out, preferred_element_type=jnp.float32...  137 us
    dot_general x64, matrix products, group_step(): jnp.einsum('shp,sn->hpn', head_inputs * tails.T[:, :, None], b_block, pre...  132 us
    psum x1, waiting for transfers between devices, shards(): lax.psum((grad_shared, pulled[6], pulled[7], grad_norm), ('dp', 'tensor'))  127 us
    squeeze x96, local copies, waits for them, and re-layouts, state_space(): finished, outputs = lax.scan(stepper, initial, blocks)  117 us
  transfers between devices with their start and end apart: 10, of which 7 were waited for; matrix products, arithmetic and copies ran while one was open for 32% of the time, Pallas kernels for 0%

commit v1 on v0

v1 whole, which is shorter than its diff:
```python
from functools import partial

import jax
import jax.numpy as jnp
import numpy as np
from jax import lax
from jax.experimental import pallas as pl
from jax.experimental.pallas import tpu as pltpu
from jax.sharding import PartitionSpec as P

Q = 128
STATE = 128
HEAD = 64
EPS = 1e-05
LOG2E = 1.4426950408889634
NEVER = -1e30
F32 = jnp.float32
BF16 = jnp.bfloat16
HIGH = lax.Precision.HIGHEST
VMEM_LIMIT = 56 * 1024 * 1024

NN = (((1,), (0,)), ((), ()))
NT = (((1,), (1,)), ((), ()))
TN = (((0,), (0,)), ((), ()))


def dot(a, b, dims=NN, precision=None):
    return lax.dot_general(a, b, dims, precision=precision, preferred_element_type=F32)


def segment_of(scal, position):
    end = scal[0]
    count = (position >= end).astype(jnp.int32)
    for k in range(1, 4):
        end = end + scal[k]
        count = count + (position >= end).astype(jnp.int32)
    return count


def rows_of(scal, group):
    return scal[4] + group * Q + lax.broadcasted_iota(jnp.int32, (Q, 1), 0)


def same_segment(scal, position, other):
    return (segment_of(scal, position) == segment_of(scal, other)).astype(F32)


def masks(scal, group):
    column = rows_of(scal, group)
    first = scal[4] + group * Q
    before = segment_of(scal, first - 1)
    last = segment_of(scal, first + Q - 1)
    segment = segment_of(scal, column)
    carries = (segment == before).astype(F32)
    ending = (segment == last).astype(F32)
    kept = (before == last).astype(F32)
    return carries, ending, kept


def reaches(scal, group):
    first = scal[4] + group * Q
    return (segment_of(scal, first - 1) == segment_of(scal, scal[4] - 1)).astype(F32)


def triangle(scal, group, flipped):
    first = scal[4] + group * Q
    rows = first + lax.broadcasted_iota(jnp.int32, (Q, Q), 0)
    cols = first + lax.broadcasted_iota(jnp.int32, (Q, Q), 1)
    ordered = (rows <= cols) if flipped else (rows >= cols)
    allowed = ordered & (segment_of(scal, rows) == segment_of(scal, cols))
    return jnp.where(allowed, 0.0, NEVER)


def in_first(rows):
    return lax.broadcasted_iota(jnp.int32, (rows, 2 * HEAD), 1) < HEAD


def pair_of(columns, head):
    rows = columns.shape[0]
    first = jnp.broadcast_to(columns[:, head : head + 1], (rows, 2 * HEAD))
    second = jnp.broadcast_to(columns[:, head + 1 : head + 2], (rows, 2 * HEAD))
    return jnp.where(in_first(rows), first, second)


def spread_heads(columns, head, channels):
    return jnp.concatenate(
        [pair_of(columns, head + 2 * p) for p in range(channels // (2 * HEAD))], axis=1
    )


def stacked_heads(member):
    first = in_first(member.shape[0])
    none = jnp.zeros_like(member)
    return jnp.concatenate([jnp.where(first, member, none), jnp.where(first, none, member)], axis=0)


def head_sums(member, picks):
    high = member.astype(BF16)
    rest = (member - high.astype(F32)).astype(BF16)
    return dot(high, picks) + dot(rest, picks)


def sigmoid(v):
    return 1.0 / (1.0 + jnp.exp(-v))


def load_earlier(group, ext, halo, before, current):
    ext[0:8, :] = jnp.where(group == 0, halo[...], before[...])
    ext[8 : 8 + Q, :] = current


def conv_before_act(ext, taps, scal, group):
    column = rows_of(scal, group)
    total = ext[8 : 8 + Q, :] * taps[3:4, :] + taps[4:5, :]
    for j in range(1, 4):
        total = total + (ext[8 - j : 8 - j + Q, :] * same_segment(scal, column, column - j)) * taps[
            3 - j : 4 - j, :
        ]
    return total


def prepare_kernel(
    scal, cur, before, halo, taps, head_rows, bc, bct, steps, logs, logs_t, total, ext, running
):
    group = pl.program_id(0)
    width = bc.shape[1]

    @pl.when(group == 0)
    def _():
        running[...] = jnp.zeros_like(running)

    load_earlier(group, ext, halo, before, cur[:, :width])
    pre = conv_before_act(ext, taps, scal, group)
    act = pre * sigmoid(pre)
    bc[...] = act.astype(BF16)
    bct[...] = jnp.concatenate(
        [act[:, k * STATE : (k + 1) * STATE].T for k in range(width // STATE)], axis=0
    ).astype(BF16)
    raw = cur[:, width:] + head_rows[0:1, :]
    step = jnp.maximum(raw, 0.0) + jnp.log1p(jnp.exp(-jnp.abs(raw)))
    steps[...] = step
    scaled = step * (head_rows[1:2, :] * LOG2E)
    lower = (
        lax.broadcasted_iota(jnp.int32, (Q, Q), 0) >= lax.broadcasted_iota(jnp.int32, (Q, Q), 1)
    ).astype(F32)
    summed = dot(lower, scaled, precision=HIGH)
    logs[...] = summed
    logs_t[0] = summed.T[: logs_t.shape[1]]
    total[...] = running[...]
    running[...] = running[...] + summed[Q - 1 : Q, :]


def states_kernel(
    head, scal, cur, before, halo, taps, steps, logs, bct, total, act_out, slope_out, states, final,
    through, ext, state,
):
    group = pl.program_id(0)
    channels = cur.shape[1]

    @pl.when(group == 0)
    def _():
        state[...] = jnp.zeros_like(state)

    load_earlier(group, ext, halo, before, cur[...])
    pre = conv_before_act(ext, taps, scal, group)
    gate = sigmoid(pre)
    act = (pre * gate).astype(BF16)
    act_out[...] = act
    slope_out[...] = (gate * (1.0 + pre * (1.0 - gate))).astype(BF16)
    _, ending, kept = masks(scal, group)
    summed = spread_heads(logs[...], head, channels)
    last = summed[Q - 1 : Q, :]
    tails = jnp.exp2(last - summed) * ending
    scaled = (act.astype(F32) * spread_heads(steps[...], head, channels)).astype(BF16)
    fresh = dot(bct[:STATE, :], (scaled.astype(F32) * tails).astype(BF16))
    states[0] = state[...].astype(BF16)
    state[...] = state[...] * (jnp.exp2(last) * kept) + fresh

    @pl.when(group == pl.num_programs(0) - 1)
    def _():
        final[...] = state[...]
        ended = spread_heads(total[...] + logs[Q - 1 : Q, :], head, channels)
        through[...] = jnp.exp2(ended) * reaches(scal, group + 1)


def entering(scal, group, head, states, start, total, channels):
    share = jnp.exp2(spread_heads(total[...], head, channels))[0:1] * reaches(scal, group)
    return states[0].astype(F32) + share * start[...]


def scan_kernel(
    head, scal, act, bc, steps, logs, logs_t, total, gate, back, states, start, rows, scanned, stats
):
    group = pl.program_id(0)
    channels = act.shape[1]
    b_map, c_map = bc[:, :STATE], bc[:, STATE:]
    scores = dot(c_map, b_map, NT)
    allowed = triangle(scal, group, False)
    carries, _, _ = masks(scal, group)
    state = entering(scal, group, head, states, start, total, channels).astype(BF16)
    outside = dot(c_map, state)
    valid = (rows_of(scal, group) < scal[0] + scal[1] + scal[2] + scal[3]).astype(F32)
    squares = jnp.zeros((Q, 2 * HEAD), F32)
    inner = jnp.zeros((Q, 2 * HEAD), F32)
    for p in range(channels // (2 * HEAD)):
        part = slice(2 * HEAD * p, 2 * HEAD * (p + 1))
        weights = []
        columns = []
        for h in (head + 2 * p, head + 2 * p + 1):
            column = jnp.broadcast_to(logs[:, h : h + 1], (Q, Q))
            columns.append(column)
            decay = jnp.exp2(column + (allowed - logs_t[0, h : h + 1, :]))
            weights.append((decay * scores).astype(BF16))
        summed = jnp.where(in_first(Q), columns[0], columns[1])
        member = act[:, part].astype(F32)
        scaled = (member * pair_of(steps[...], head + 2 * p)).astype(BF16)
        result = dot(jnp.concatenate(weights, axis=1), stacked_heads(scaled))
        result = result + outside[:, part] * (jnp.exp2(summed) * carries)
        scanned[:, part] = result
        mixed_heads = result + rows[6:7, part] * member
        raw = gate[:, part]
        gated = mixed_heads * (raw * sigmoid(raw))
        squares = squares + gated * gated
        inner = inner + back[:, part] * rows[5:6, part] * gated
    squares = jnp.sum(squares, axis=1, keepdims=True)
    inner = jnp.sum(inner, axis=1, keepdims=True) * valid
    lane = lax.broadcasted_iota(jnp.int32, (Q, Q), 1)
    both = jnp.where(lane == 0, squares, jnp.where(lane == 1, inner, 0.0))
    stats[...] = both.T[:8]


def gate_back_kernel(
    head, inner_channels, scal, scanned, act, gate, back, stats, bct, logs, total, rows, mixed,
    low_gate, back_heads, reach, sums,
):
    group = pl.program_id(0)
    channels = act.shape[1]

    @pl.when(group == 0)
    def _():
        reach[...] = jnp.zeros_like(reach)
        sums[...] = jnp.zeros_like(sums)

    row = lax.broadcasted_iota(jnp.int32, (8, Q), 0)
    inverse_row = lax.rsqrt(stats[...] / inner_channels + EPS)
    both = jnp.concatenate(
        [jnp.where(row == 0, inverse_row, stats[...]), jnp.zeros((Q - 8, Q), F32)], axis=0
    ).T
    inverse, inner = both[:, 0:1], both[:, 1:2]
    valid = (rows_of(scal, group) < scal[0] + scal[1] + scal[2] + scal[3]).astype(F32)
    slope = inverse * inverse * inverse * inner * valid / inner_channels
    inverse_valid = inverse * valid
    carries, _, _ = masks(scal, group)
    gradients = []
    for p in range(channels // (2 * HEAD)):
        part = slice(2 * HEAD * p, 2 * HEAD * (p + 1))
        member = act[:, part].astype(F32)
        mixed_heads = scanned[:, part] + rows[6:7, part] * member
        raw = gate[:, part]
        share = sigmoid(raw)
        opened = raw * share
        gated = mixed_heads * opened
        back_part = back[:, part]
        gain = rows[5:6, part]
        normal = gated * inverse_valid
        mixed[:, part] = (normal * gain).astype(BF16)
        scaled_back = back_part * inverse_valid
        gradient = scaled_back * gain - gated * slope
        low_gate[:, part] = (
            gradient * mixed_heads * (share * (1.0 + raw * (1.0 - share)))
        ).astype(BF16)
        low = (gradient * opened).astype(BF16)
        back_heads[:, part] = low
        wide = low.astype(F32)
        sums[0:1, part] = sums[0:1, part] + jnp.sum(scaled_back * gated, axis=0, keepdims=True)
        sums[1:2, part] = sums[1:2, part] + jnp.sum(wide * member, axis=0, keepdims=True)
        entered = jnp.exp2(pair_of(logs[...], head + 2 * p)) * carries
        gradients.append((wide * entered).astype(BF16))
    share = jnp.exp2(spread_heads(total[...], head, channels))[0:1] * reaches(scal, group)
    reach[...] = reach[...] + share * dot(bct[STATE:, :], jnp.concatenate(gradients, axis=1))


def scan_back_kernel(
    head, scal, act, slope, back_heads, scanned, cur, before, halo, rows, picks, bc, bct, steps,
    logs, logs_t, total, raw_rate, head_rows, states, start, leaving, low_value, back_bc, low_rate,
    sums, head_out, first_rows, last_rows, ext, back_ext, back_state,
):
    turn = pl.program_id(0)
    turns = pl.num_programs(0)
    group = turns - 1 - turn
    channels = act.shape[1]

    @pl.when(turn == 0)
    def _():
        back_state[...] = leaving[...]
        back_ext[Q : Q + 8, :] = jnp.zeros_like(back_ext[Q : Q + 8, :])
        sums[...] = jnp.zeros_like(sums)
        head_out[...] = jnp.zeros_like(head_out)

    b_map, c_map = bc[:, :STATE], bc[:, STATE:]
    scores = dot(b_map, c_map, NT)
    allowed = triangle(scal, group, True)
    carries, ending, kept = masks(scal, group)
    state = entering(scal, group, head, states, start, total, channels)
    state_low = state.astype(BF16)
    leaving_low = back_state[...].astype(BF16)
    from_state = dot(b_map, leaving_low)
    back_scores = jnp.zeros((Q, Q), F32)
    into_state, out_of_state, differences, passed, products = [], [], [], [], []
    for p in range(channels // (2 * HEAD)):
        part = slice(2 * HEAD * p, 2 * HEAD * (p + 1))
        low = back_heads[:, part]
        wide = low.astype(F32)
        member = act[:, part].astype(F32)
        step = pair_of(steps[...], head + 2 * p)
        scaled = (member * step).astype(BF16)
        back_weights = dot(stacked_heads(scaled), low, NT)
        weights, columns = [], []
        for k, h in enumerate((head + 2 * p, head + 2 * p + 1)):
            column = jnp.broadcast_to(logs[:, h : h + 1], (Q, Q))
            columns.append(column)
            decay = jnp.exp2((logs_t[0, h : h + 1, :] + allowed) - column)
            weights.append((decay * scores).astype(BF16))
            back_scores = back_scores + decay * back_weights[k * Q : (k + 1) * Q]
        summed = jnp.where(in_first(Q), columns[0], columns[1])
        last = summed[Q - 1 : Q, :]
        tails = jnp.exp2(last - summed) * ending
        back_scaled = dot(jnp.concatenate(weights, axis=1), stacked_heads(low))
        scaled_wide = scaled.astype(F32)
        from_end = tails * from_state[:, part]
        differences.append(wide * scanned[:, part] - scaled_wide * back_scaled)
        passed.append((scaled_wide * from_end).astype(BF16))
        back_scaled = back_scaled + from_end
        into_state.append((scaled_wide * tails).astype(BF16))
        out_of_state.append((wide * (jnp.exp2(summed) * carries)).astype(BF16))
        products.append((back_scaled * member).astype(BF16))
        back_act = back_scaled * step + rows[6:7, part] * wide
        back_ext[0:Q, part] = back_act * slope[:, part].astype(F32)
    into_state = jnp.concatenate(into_state, axis=1)
    out_of_state = jnp.concatenate(out_of_state, axis=1)
    back_b = dot(back_scores.astype(BF16), c_map) + dot(into_state, leaving_low, NT)
    back_c = dot(back_scores.T.astype(BF16), b_map) + dot(out_of_state, state_low, NT)
    back_bc[:, :STATE] = back_b
    back_bc[:, STATE:] = back_c

    whole = spread_heads(logs[Q - 1 : Q, :], head, channels)
    kept_state = back_state[...] * (jnp.exp2(whole) * kept)
    back_state[...] = kept_state + dot(bct[STATE:, :], out_of_state)
    crossing = jnp.sum(kept_state * state, axis=0, keepdims=True)

    difference = head_sums(jnp.concatenate(differences, axis=1), picks[...])
    before_it = dot(jnp.concatenate(passed, axis=1), picks[...])
    product = dot(jnp.concatenate(products, axis=1), picks[...])
    crossing = head_sums(jnp.broadcast_to(crossing, (8, channels)), picks[...])
    rows_at = lax.broadcasted_iota(jnp.int32, (Q, Q), 0)
    cols_at = lax.broadcasted_iota(jnp.int32, (Q, Q), 1)
    back_logs = (
        dot((rows_at <= cols_at).astype(F32), difference, precision=HIGH)
        + dot((rows_at > cols_at).astype(F32), before_it, precision=HIGH)
        + crossing[0:1, :]
    )
    decays = back_logs * head_rows[1:2, :]
    back_rate = (product + decays) * sigmoid(raw_rate[...] + head_rows[0:1, :])
    low_rate[...] = back_rate.astype(BF16)
    head_out[0:1, :] = head_out[0:1, :] + jnp.sum(back_rate, axis=0, keepdims=True)
    head_out[1:2, :] = head_out[1:2, :] + jnp.sum(decays * steps[...], axis=0, keepdims=True)

    conv_back(group, turn, scal, ext, back_ext, cur[...], before, halo, rows, low_value, sums,
              first_rows, last_rows)


def conv_back(
    group, turn, scal, ext, back_ext, current, before, halo, taps, low, sums, first_rows, last_rows
):
    load_earlier(group, ext, halo, before, current)
    column = rows_of(scal, group)
    now = back_ext[0:Q, :]
    sums[3:4, :] = sums[3:4, :] + jnp.sum(now * ext[8 : 8 + Q, :], axis=0, keepdims=True)
    sums[4:5, :] = sums[4:5, :] + jnp.sum(now, axis=0, keepdims=True)
    total = now * taps[3:4, :]
    for j in range(1, 4):
        tap = slice(3 - j, 4 - j)
        earlier = ext[8 - j : 8 - j + Q, :] * same_segment(scal, column, column - j)
        sums[tap, :] = sums[tap, :] + jnp.sum(now * earlier, axis=0, keepdims=True)
        later = back_ext[j : j + Q, :] * same_segment(scal, column, column + j)
        total = total + later * taps[tap, :]
    low[...] = total.astype(BF16)

    @pl.when(turn == 0)
    def _():
        last_rows[...] = total[Q - 8 : Q, :]

    back_ext[Q : Q + 8, :] = back_ext[0:8, :]

    @pl.when(group == 0)
    def _():
        first_rows[...] = back_ext[0:8, :]


def shared_back_kernel(
    scal, back_bc, back_more, cur, before, halo, taps, low, sums, first_rows, last_rows, ext, back_ext
):
    turn = pl.program_id(0)
    group = pl.num_programs(0) - 1 - turn

    @pl.when(turn == 0)
    def _():
        back_ext[Q : Q + 8, :] = jnp.zeros_like(back_ext[Q : Q + 8, :])
        sums[...] = jnp.zeros_like(sums)

    load_earlier(group, ext, halo, before, cur[...])
    pre = conv_before_act(ext, taps, scal, group)
    gate = sigmoid(pre)
    back_ext[0:Q, :] = (back_bc[...] + back_more[...]) * (gate * (1.0 + pre * (1.0 - gate)))
    conv_back(
        group, turn, scal, ext, back_ext, cur[...], before, halo, taps, low, sums, first_rows, last_rows
    )


def many_dots_kernel(dims, scal, *refs):
    count = len(dims)
    out = refs[2 * count]
    total = dot(refs[0][...], refs[count][...], dims[0])
    for k in range(1, count):
        total = total + dot(refs[k][...], refs[count + k][...], dims[k])
    out[...] = total.astype(out.dtype)


def call(body, grid, in_specs, out_specs, out_shape, scratch, name, flops, args):
    moved = sum(a.size * a.dtype.itemsize for a in args) + sum(
        int(np.prod(o.shape)) * np.dtype(o.dtype).itemsize for o in out_shape
    )
    return pl.pallas_call(
        body,
        grid_spec=pltpu.PrefetchScalarGridSpec(
            num_scalar_prefetch=1,
            grid=(grid,),
            in_specs=in_specs,
            out_specs=out_specs,
            scratch_shapes=scratch,
        ),
        out_shape=out_shape,
        compiler_params=pltpu.CompilerParams(vmem_limit_bytes=VMEM_LIMIT),
        cost_estimate=pl.CostEstimate(flops=flops, bytes_accessed=moved, transcendentals=0),
        name=name,
    )(*args)


def whole(shape):
    return pl.BlockSpec(shape, lambda i, s: tuple(0 for _ in shape))


def shape_of(shape, dtype):
    return jax.ShapeDtypeStruct(shape, dtype)


def many_dots(offset_rows, lefts, rights, dims, rows, dtype, name):
    tile = min(256, rows)
    columns = rights[0].shape[0 if dims[0] == NT else 1]
    scal = (offset_rows // tile).reshape(1).astype(jnp.int32)
    flops = 2 * rows * columns * sum(a.shape[1] for a in lefts)
    return call(
        partial(many_dots_kernel, tuple(dims)),
        rows // tile,
        [pl.BlockSpec((tile, a.shape[1]), lambda i, s: (s[0] + i, 0)) for a in lefts]
        + [whole(b.shape) for b in rights],
        [pl.BlockSpec((tile, columns), lambda i, s: (i, 0))],
        [shape_of((rows, columns), dtype)],
        [],
        name,
        flops,
        (scal, *lefts, *rights),
    )[0]


def solution(mesh):
    tensor = mesh.shape["tensor"]
    copies = mesh.shape["dp"]
    ny = tensor // 2
    nx = ny if copies % ny == 0 else 1
    nz = copies // nx

    def from_y(member, shift):
        pairs = [((((y + shift) % ny) * 2 + c), y * 2 + c) for y in range(ny) for c in range(2)]
        return lax.ppermute(member, "tensor", pairs)

    def next_y(member, step):
        pairs = [
            ((y - step) * 2 + c, y * 2 + c)
            for y in range(ny)
            for c in range(2)
            if 0 <= y - step < ny
        ]
        return lax.ppermute(member, "tensor", pairs)

    def from_core(member):
        return lax.ppermute(member, "tensor", [(t ^ 1, t) for t in range(tensor)])

    def from_x(member, shift):
        pairs = [(z * nx + (x + shift) % nx, z * nx + x) for z in range(nz) for x in range(nx)]
        return lax.ppermute(member, "dp", pairs)

    def from_z(member, shift):
        pairs = [(((z + shift) % nz) * nx + x, z * nx + x) for z in range(nz) for x in range(nx)]
        return lax.ppermute(member, "dp", pairs)

    def sum_rows(member):
        bit = 1
        while bit < copies:
            member = member + lax.ppermute(member, "dp", [(d ^ bit, d) for d in range(copies)])
            bit *= 2
        return member

    def sum_all(member):
        bit = 1
        while bit < tensor:
            member = member + lax.ppermute(member, "tensor", [(t ^ bit, t) for t in range(tensor)])
            bit *= 2
        return sum_rows(member)

    def reduce_blocks(blocks, x, z):
        rows, columns = blocks[0].shape
        each = rows // copies
        half = each // 2
        views = [b.reshape(nz, nx, each, columns) for b in blocks]

        def along_y(parts):
            total = parts[0].astype(F32)
            for j in range(1, ny):
                total = total + from_y(parts[j], ny - j).astype(F32)
            return total

        def along_x(part):
            total = lax.dynamic_index_in_dim(part, x, 1, keepdims=False).astype(F32)
            for k in range(1, nx):
                sent = lax.dynamic_index_in_dim(part, (x + k) % nx, 1, keepdims=False)
                total = total + from_x(sent.astype(BF16), nx - k).astype(F32)
            return total

        first = along_x(along_y([v[:, :, :half] for v in views]).astype(BF16))
        second = along_y([along_x(v[:, :, half:]).astype(BF16) for v in views])
        both = jnp.concatenate([first, second], axis=1).astype(BF16)
        total = lax.dynamic_index_in_dim(both, z, 0, keepdims=False).astype(F32)
        for k in range(1, nz):
            sent = lax.dynamic_index_in_dim(both, (z + k) % nz, 0, keepdims=False)
            total = total + from_z(sent, nz - k).astype(F32)
        return total

    def shards(
        tokens, lengths, norm_gain, w_gate, w_value, w_shared, w_rate, conv_value, value_bias,
        conv_shared, shared_bias, rate_bias, decay_log, skip_gain, mix_gain, w_out, cotangent,
    ):
        index = lax.axis_index("tensor")
        y, core = index // 2, index % 2
        dp = lax.axis_index("dp")
        z, x = dp // nx, dp % nx
        own_rows, width = tokens.shape
        rows = 2 * own_rows
        groups = rows // Q
        channels = w_gate.shape[1]
        heads = w_rate.shape[1]
        inner = channels * tensor
        own_start = core * own_rows
        lanes = 128
        wide_heads = -(-(ny * heads) // 8) * 8
        maps = w_shared.shape[1]
        blocks = range(ny)

        values = [w_value] + [from_y(w_value, j) for j in range(1, ny)]
        gates = [w_gate] + [from_y(w_gate, j) for j in range(1, ny)]
        outs = [w_out] + [from_y(w_out, j) for j in range(1, ny)]
        packed = jnp.concatenate(
            [
                conv_value.T,
                value_bias[None],
                mix_gain[None],
                jnp.repeat(skip_gain, HEAD)[None],
                jnp.concatenate([rate_bias, decay_log, jnp.zeros((channels - 2 * heads,), F32)])[None],
            ],
            axis=0,
        )
        packs = [packed] + [from_y(packed, j) for j in range(1, ny)]
        rate_t = w_rate.T
        rates_t = [rate_t] + [from_y(rate_t, j) for j in range(1, ny)]
        all_rates = jnp.concatenate(
            rates_t + [jnp.zeros((lanes - ny * heads, width), BF16)], axis=0
        )
        w_small = jnp.concatenate([w_shared, all_rates.T], axis=1)
        fill = jnp.zeros((lanes - ny * heads,), F32)
        head_rows = jnp.concatenate(
            [
                jnp.concatenate([p[7, :heads] for p in packs] + [fill])[None],
                jnp.concatenate([-jnp.exp(p[7, heads : 2 * heads]) for p in packs] + [fill])[None],
                jnp.zeros((6, lanes), F32),
            ],
            axis=0,
        )
        shared_taps = jnp.concatenate(
            [conv_shared.T, shared_bias[None], jnp.zeros((3, maps), F32)], axis=0
        )
        scal = jnp.concatenate([lengths[0], (y * rows).reshape(1)]).astype(jnp.int32)

        residual = tokens.astype(F32)
        inverse_in = lax.rsqrt(jnp.mean(residual * residual, axis=1, keepdims=True) + EPS)
        normed_own = (residual * inverse_in * norm_gain).astype(BF16)

        def chip_rows(own):
            other = from_core(own)
            both = lax.dynamic_update_slice(jnp.zeros((rows, width), own.dtype), own, (own_start, 0))
            return lax.dynamic_update_slice(both, other, (own_rows - own_start, 0))

        normed = chip_rows(normed_own)
        back_rows = chip_rows(cotangent)
        halo = next_y(normed[rows - 16 :], 1)

        def group_rows(columns, at=0):
            return pl.BlockSpec((Q, columns), lambda i, s: (i, at))

        def rows_before(columns):
            return pl.BlockSpec((8, columns), lambda i, s: (jnp.maximum(i * (Q // 8) - 1, 0), 0))

        def turned(columns, at=0):
            return pl.BlockSpec((Q, columns), lambda i, s: (groups - 1 - i, at))

        def turned_before(columns):
            return pl.BlockSpec(
                (8, columns), lambda i, s: (jnp.maximum((groups - 1 - i) * (Q // 8) - 1, 0), 0)
            )

        small = dot(normed, w_small)
        small_halo = dot(halo, w_small)[8:]
        bc, bct, steps, logs, logs_t, total = call(
            prepare_kernel,
            groups,
            [
                group_rows(maps + lanes),
                rows_before(maps),
                whole((8, maps)),
                whole((8, maps)),
                whole((8, lanes)),
            ],
            [
                group_rows(maps),
                pl.BlockSpec((maps, Q), lambda i, s: (0, i)),
                group_rows(lanes),
                group_rows(lanes),
                pl.BlockSpec((1, wide_heads, Q), lambda i, s: (i, 0, 0)),
                pl.BlockSpec((8, lanes), lambda i, s: (i, 0)),
            ],
            [
                shape_of((rows, maps), BF16),
                shape_of((maps, rows), BF16),
                shape_of((rows, lanes), F32),
                shape_of((rows, lanes), F32),
                shape_of((groups, wide_heads, Q), F32),
                shape_of((groups * 8, lanes), F32),
            ],
            [pltpu.VMEM((Q + 8, maps), F32), pltpu.VMEM((8, lanes), F32)],
            "prepare",
            rows * 2000,
            (scal, small, small[:, :maps], small_halo[:, :maps], shared_taps, head_rows),
        )

        flops_scan = rows * channels * 2 * 600
        raw_values, value_halos, acts, slopes, states, finals, throughs = [], [], [], [], [], [], []
        for j in blocks:
            raw = dot(normed, values[j])
            raw_halo = dot(halo, values[j])[8:]
            act, slope, state, final, through = call(
                partial(states_kernel, j * heads),
                groups,
                [
                    group_rows(channels),
                    rows_before(channels),
                    whole((8, channels)),
                    whole((8, channels)),
                    group_rows(lanes),
                    group_rows(lanes),
                    pl.BlockSpec((maps, Q), lambda i, s: (0, i)),
                    pl.BlockSpec((8, lanes), lambda i, s: (i, 0)),
                ],
                [
                    group_rows(channels),
                    group_rows(channels),
                    pl.BlockSpec((1, STATE, channels), lambda i, s: (i, 0, 0)),
                    whole((STATE, channels)),
                    whole((8, channels)),
                ],
                [
                    shape_of((rows, channels), BF16),
                    shape_of((rows, channels), BF16),
                    shape_of((groups, STATE, channels), BF16),
                    shape_of((STATE, channels), F32),
                    shape_of((8, channels), F32),
                ],
                [pltpu.VMEM((Q + 8, channels), F32), pltpu.VMEM((STATE, channels), F32)],
                "states",
                flops_scan // 2,
                (scal, raw, raw, raw_halo, packs[j], steps, logs, bct, total),
            )
            raw_values.append(raw)
            value_halos.append(raw_halo)
            acts.append(act)
            slopes.append(slope)
            states.append(state)
            finals.append(final)
            throughs.append(through)

        before = [(j + 1) % ny for j in blocks]
        after = [(j - 1) % ny for j in blocks]
        starts = [next_y(finals[k], 1) for k in before]
        for _ in range(ny - 2):
            starts = [next_y(finals[k] + throughs[k][0:1] * starts[k], 1) for k in before]

        raw_gates, backs, scans, stats = [], [], [], []
        for j in blocks:
            raw_gate = dot(normed, gates[j])
            back = dot(back_rows, outs[j], NT)
            scanned, stat = call(
                partial(scan_kernel, j * heads),
                groups,
                [
                    group_rows(channels),
                    group_rows(maps),
                    group_rows(lanes),
                    group_rows(lanes),
                    pl.BlockSpec((1, wide_heads, Q), lambda i, s: (i, 0, 0)),
                    pl.BlockSpec((8, lanes), lambda i, s: (i, 0)),
                    group_rows(channels),
                    group_rows(channels),
                    pl.BlockSpec((1, STATE, channels), lambda i, s: (i, 0, 0)),
                    whole((STATE, channels)),
                    whole((8, channels)),
                ],
                [group_rows(channels), pl.BlockSpec((8, Q), lambda i, s: (0, i))],
                [shape_of((rows, channels), F32), shape_of((8, rows), F32)],
                [],
                "scan",
                flops_scan,
                (scal, acts[j], bc, steps, logs, logs_t, total, raw_gate, back, states[j], starts[j],
                 packs[j]),
            )
            raw_gates.append(raw_gate)
            backs.append(back)
            scans.append(scanned)
            stats.append(stat)

        stat = sum(stats[1:], stats[0])
        stat = stat + from_core(stat)

        mixeds, low_gates, back_heads, reaching, gate_sums = [], [], [], [], []
        for j in blocks:
            mixed, low_gate, back_head, reach, sums = call(
                partial(gate_back_kernel, j * heads, inner),
                groups,
                [
                    group_rows(channels),
                    group_rows(channels),
                    group_rows(channels),
                    group_rows(channels),
                    pl.BlockSpec((8, Q), lambda i, s: (0, i)),
                    pl.BlockSpec((maps, Q), lambda i, s: (0, i)),
                    group_rows(lanes),
                    pl.BlockSpec((8, lanes), lambda i, s: (i, 0)),
                    whole((8, channels)),
                ],
                [
                    group_rows(channels),
                    group_rows(channels),
                    group_rows(channels),
                    whole((STATE, channels)),
                    whole((8, channels)),
                ],
                [
                    shape_of((rows, channels), BF16),
                    shape_of((rows, channels), BF16),
                    shape_of((rows, channels), BF16),
                    shape_of((STATE, channels), F32),
                    shape_of((8, channels), F32),
                ],
                [],
                "gate_back",
                flops_scan // 2,
                (scal, scans[j], acts[j], raw_gates[j], backs[j], stat, bct, logs, total, packs[j]),
            )
            mixeds.append(mixed)
            low_gates.append(low_gate)
            back_heads.append(back_head)
            reaching.append(reach)
            gate_sums.append(sums)

        leavings = [next_y(reaching[k], -1) for k in after]
        for _ in range(ny - 2):
            leavings = [next_y(reaching[k] + throughs[k][0:1] * leavings[k], -1) for k in after]

        ahead = (1 - core) * own_rows
        sent = many_dots(ahead, mixeds, outs, [NN] * ny, own_rows, BF16, "out_other")
        kept = many_dots(own_start, mixeds, outs, [NN] * ny, own_rows, F32, "out_own")
        block_out = (residual + kept + from_core(sent).astype(F32)).astype(BF16)
        out_blocks = [dot(back_rows, m, TN).astype(BF16) for m in mixeds]
        grad_out = reduce_blocks(out_blocks, x, z).T
        gate_blocks = [dot(normed, low, TN).astype(BF16) for low in low_gates]
        grad_gate = reduce_blocks(gate_blocks, x, z)

        channel = np.arange(channels)
        low_values, back_bcs, low_rates, conv_sums, head_sums_ = [None] * ny, [], [], [None] * ny, []
        for j in reversed(blocks):
            picks = jnp.asarray(
                (np.arange(lanes)[None, :] == (j * heads + channel // HEAD)[:, None]), BF16
            )
            low, back_bc, low_rate, sums, head_out, first_rows, last_rows = call(
                partial(scan_back_kernel, j * heads),
                groups,
                [
                    turned(channels),
                    turned(channels),
                    turned(channels),
                    turned(channels),
                    turned(channels),
                    turned_before(channels),
                    whole((8, channels)),
                    whole((8, channels)),
                    whole((channels, lanes)),
                    turned(maps),
                    pl.BlockSpec((maps, Q), lambda i, s: (0, groups - 1 - i)),
                    turned(lanes),
                    turned(lanes),
                    pl.BlockSpec((1, wide_heads, Q), lambda i, s: (groups - 1 - i, 0, 0)),
                    pl.BlockSpec((8, lanes), lambda i, s: (groups - 1 - i, 0)),
                    turned(lanes, maps // lanes),
                    whole((8, lanes)),
                    pl.BlockSpec((1, STATE, channels), lambda i, s: (groups - 1 - i, 0, 0)),
                    whole((STATE, channels)),
                    whole((STATE, channels)),
                ],
                [
                    turned(channels),
                    turned(maps),
                    turned(lanes),
                    whole((8, channels)),
                    whole((8, lanes)),
                    whole((8, channels)),
                    whole((8, channels)),
                ],
                [
                    shape_of((rows, channels), BF16),
                    shape_of((rows, maps), F32),
                    shape_of((rows, lanes), BF16),
                    shape_of((8, channels), F32),
                    shape_of((8, lanes), F32),
                    shape_of((8, channels), F32),
                    shape_of((8, channels), F32),
                ],
                [
                    pltpu.VMEM((Q + 8, channels), F32),
                    pltpu.VMEM((Q + 8, channels), F32),
                    pltpu.VMEM((STATE, channels), F32),
                ],
                "scan_back",
                flops_scan * 3,
                (scal, acts[j], slopes[j], back_heads[j], scans[j], raw_values[j], raw_values[j],
                 value_halos[j], packs[j], picks, bc, bct, steps, logs, logs_t, total, small, head_rows,
                 states[j], starts[j], leavings[j]),
            )
            low_values[j] = (low, first_rows, last_rows)
            back_bcs.append(back_bc)
            low_rates.append(low_rate)
            conv_sums[j] = sums
            head_sums_.append(head_out)

        firsts = [member[1] for member in low_values]
        low_values = [
            joined(scal, low_values[j][0], firsts[after[j]], low_values[j][2], packs[j], next_y, rows)
            for j in blocks
        ]
        value_blocks = [dot(normed, low, TN).astype(BF16) for low in low_values]
        grad_value = reduce_blocks(value_blocks, x, z)

        back_bc = sum(back_bcs[1:], back_bcs[0])
        low_shared, shared_sums, first_rows, last_rows = call(
            shared_back_kernel,
            groups,
            [
                turned(maps),
                turned(maps),
                turned(maps),
                turned_before(maps),
                whole((8, maps)),
                whole((8, maps)),
            ],
            [turned(maps), whole((8, maps)), whole((8, maps)), whole((8, maps))],
            [
                shape_of((rows, maps), BF16),
                shape_of((8, maps), F32),
                shape_of((8, maps), F32),
                shape_of((8, maps), F32),
            ],
            [pltpu.VMEM((Q + 8, maps), F32), pltpu.VMEM((Q + 8, maps), F32)],
            "shared_back",
            rows * 2000,
            (scal, back_bc, from_core(back_bc), small, small, small_halo[:, :maps], shared_taps),
        )
        low_shared = joined(scal, low_shared, first_rows, last_rows, shared_taps, next_y, rows)
        low_rate = sum(low_rates[1:], low_rates[0])
        shared_own = lax.dynamic_slice(low_shared, (own_start, 0), (own_rows, maps))
        grad_shared = dot(normed_own, shared_own, TN)
        grad_rate_all = dot(normed, low_rate, TN)

        lefts = [low_rate] + low_gates + low_values
        rights = [all_rates.T] + gates + values
        sent = many_dots(ahead, lefts, rights, [NT] * len(lefts), own_rows, BF16, "back_other")
        lefts = [low_shared] + lefts
        rights = [w_shared] + rights
        kept = many_dots(own_start, lefts, rights, [NT] * len(lefts), own_rows, F32, "back_own")
        back_normed = kept + from_core(sent).astype(F32)
        grad_norm = jnp.sum(back_normed * residual * inverse_in, axis=0)
        scaled = back_normed * norm_gain
        tokens_grad = (
            cotangent.astype(F32)
            + scaled * inverse_in
            - residual
            * (inverse_in * inverse_in * inverse_in)
            * jnp.sum(scaled * residual, axis=1, keepdims=True)
            / width
        )

        rate_blocks = [grad_rate_all[:, j * heads : (j + 1) * heads].T for j in blocks]
        grad_rate = rate_blocks[0]
        for j in range(1, ny):
            grad_rate = grad_rate + from_y(rate_blocks[j], ny - j)
        grad_rate = lax.dynamic_slice(
            sum_rows(grad_rate), (0, dp * (width // copies)), (heads, width // copies)
        ).T
        head_out = sum(head_sums_[1:], head_sums_[0])
        smalls = []
        for j in blocks:
            skip = gate_sums[j][1].reshape(heads, HEAD).sum(axis=1)
            own_heads = head_out[:2, j * heads : (j + 1) * heads].reshape(2 * heads)
            line = jnp.concatenate([skip, own_heads, jnp.zeros((channels - 3 * heads,), F32)])
            smalls.append(
                jnp.concatenate(
                    [conv_sums[j][:5], gate_sums[j][:1], line[None], jnp.zeros((1, channels), F32)]
                )
            )
        own = smalls[0]
        for j in range(1, ny):
            own = own + from_y(smalls[j], ny - j)
        own = sum_rows(own)
        shared_sums = jnp.where(core == 0, shared_sums, 0.0)
        alls = jnp.concatenate([shared_sums, grad_norm.reshape(-1, maps)], axis=0)
        alls = sum_all(alls)
        grad_shared = lax.psum(grad_shared, ("dp", "tensor"))
        return (
            block_out,
            tokens_grad,
            alls[8:].reshape(width),
            grad_gate,
            grad_value,
            grad_shared,
            grad_rate,
            own[:4].T,
            own[4],
            alls[:4].T,
            alls[4],
            own[6, heads : 2 * heads],
            own[6, 2 * heads : 3 * heads],
            own[6, :heads],
            own[5],
            grad_out,
        )

    def joined(scal, low, first_rows, last_rows, taps, next_y, rows):
        later = next_y(first_rows, -1)
        last = scal[4] + rows - 1
        out = last_rows
        for back in range(1, 4):
            at = last + 1 - back
            extra = jnp.zeros_like(last_rows[0])
            for j in range(back, 4):
                same = same_segment(scal, at, at + j)
                extra = extra + same * taps[3 - j] * later[j - back]
            out = out.at[8 - back].add(extra)
        return lax.dynamic_update_slice(low, out.astype(BF16), (rows - 8, 0))

    in_specs = (
        P(("dp", "tensor"), None),
        P("dp", None),
        P(),
        P(None, "tensor"),
        P(None, "tensor"),
        P(),
        P(None, "tensor"),
        P("tensor", None),
        P("tensor"),
        P(),
        P(),
        P("tensor"),
        P("tensor"),
        P("tensor"),
        P("tensor"),
        P("tensor", None),
        P(("dp", "tensor"), None),
    )
    out_specs = (
        P(("dp", "tensor"), None),
        P(("dp", "tensor"), None),
        P(),
        P("dp", "tensor"),
        P("dp", "tensor"),
        P(),
        P("dp", "tensor"),
        P("tensor", None),
        P("tensor"),
        P(),
        P(),
        P("tensor"),
        P("tensor"),
        P("tensor"),
        P("tensor"),
        P("tensor", "dp"),
    )
    return jax.shard_map(shards, mesh=mesh, in_specs=in_specs, out_specs=out_specs, check_vma=False)
```

time: 3520 us -> 955 us (0.27); the launches traced: 3470 us -> 946 us
  matrix products: 987 us -> 106 us
  local copies, waits for them, and re-layouts: 872 us -> 48.1 us
  other arithmetic: 720 us -> 61.8 us
  waiting for transfers between devices: 705 us -> 325 us
  Pallas kernels: 0 us -> 301 us
  blocking collectives: 98.8 us -> 0 us
  starting transfers between devices: 0.41 us -> 80.7 us
  loops' own time: 72.6 us -> 0 us
    dot_general x302 -> x18, matrix products: 980 us -> 106 us  [dot(): lax.dot_general(a, b, dims, precision=precision, preferred_element_type=F32)]
    reduce_scatter x6 -> x0, waiting for transfers between devices: 503 us -> none  [the longest x1 137 us: shards(): lax.psum_scatter(jnp.dot(mixed, w_out, preferred_element_type=jnp.float32...]
    mul x308 -> x0, other arithmetic: 322 us -> none  [the longest x64 91 us: group_step(): head_inputs * tails.T[:, :, None]]
    pallas_call x0 -> x14, Pallas kernels: none -> 301 us  [call(): pl.pallas_call(body, grid_spec=pltpu.PrefetchScalarGridSpec(num_scalar_pr...]
    dynamic_update_slice x176 -> x3, local copies, waits for them, and re-layouts: 224 us -> 6.67 us  [the longest x2 6.3 us: chip_rows(): return lax.dynamic_update_slice(both, other, (own_rows - own_start, 0))]
    ppermute x0 -> x56, waiting for transfers between devices: none -> 209 us  [the longest x13 115 us: from_y(): return lax.ppermute(member, 'tensor', pairs)]
    another operation x501 -> x6, local copies, waits for them, and re-layouts: 210 us -> 1.04 us
    another operation x195 -> x6, other arithmetic: 128 us -> 3.84 us
  transfers between devices with their start and end apart: 10 -> 57, of which waited for: 7 -> 22; matrix products, arithmetic and copies ran while one was open for 32% -> 20% of each run, Pallas kernels for 0% -> 27%
where the time goes in v1:
time: 955 us; the launch traced here: 946 us
  waiting for transfers between devices  325 us (34%)
  Pallas kernels  301 us (32%)
  matrix products  106 us (11%)
  starting transfers between devices  80.7 us (8%)
  other arithmetic  61.8 us (6%)
  local copies, waits for them, and re-layouts  48.1 us (5%)
  between operations  22.3 us (2%)
    pallas_call x14, Pallas kernels, call(): pl.pallas_call(body, grid_spec=pltpu.PrefetchScalarGridSpec(num_scalar_pr...  301 us
    psum x1, waiting for transfers between devices, shards(): grad_shared = lax.psum(grad_shared, ('dp', 'tensor'))  116 us
    ppermute x13, waiting for transfers between devices, from_y(): return lax.ppermute(member, 'tensor', pairs)  115 us
    dot_general x18, matrix products, dot(): lax.dot_general(a, b, dims, precision=precision, preferred_element_type=F32)  106 us
    ppermute x8, waiting for transfers between devices, next_y(): return lax.ppermute(member, 'tensor', pairs)  42.5 us
    ppermute x9, waiting for transfers between devices, from_z(): return lax.ppermute(member, 'dp', pairs)  28.4 us
    ppermute x13, starting transfers between devices, from_y(): return lax.ppermute(member, 'tensor', pairs)  24.3 us
    unnamed x157, local copies, waits for them, and re-layouts  20.1 us
  transfers between devices with their start and end apart: 57, of which 22 were waited for; matrix products, arithmetic and copies ran while one was open for 20% of the time, Pallas kernels for 27%

profile of v1, /device:TPU:0, one launch (start us, length us, event | category | flops | bytes accessed | tf_op | source)
XLA Modules:
  0.0 945.6 jit_solution(3044118044277561409)
XLA Ops:
  30.8 42.6 %collective-permute-done.3.taps.rows = f32[8,768]{1,0:T(8,128)} collective-permute-done((f32[8,768]{1,0:T(8,128)}, f32[8,768]{1,0:T(8,128)}, u32[]{:S(2)}, u32[]{:S(2)}) %collective-permute-start.3) | collective-permute-done | bytes 24608 | tf_op jit(solution)/shard_map/ppermute | solution.py:485
  92.6 9.7 %fusion.101.cur.before = f32[2048,768]{1,0:T(8,128)} fusion(bf16[2048,1536]{1,0:T(8,128)(2,1)} %constant_dynamic-update-slice_fusion.5, bf16[1536,768]{1,0:T(8,128)(2,1)} %refs_8_.3), kind=kOutput, calls=%fused_computation.214 | convolution fusion | flops 4831838208 | bytes 14942208 | tf_op jit(solution)/shard_map/dot_general | solution.py:28
  118.7 8.6 fusion.104.cur.before
  144.3 38.7 %collective-permute-done.1 = bf16[16,1536]{1,0:T(8,128)(2,1)S(1)} collective-permute-done((bf16[16,1536]{1,0:T(8,128)(2,1)S(1)}, bf16[16,1536]{1,0:T(8,128)(2,1)S(1)}, u32[]{:S(2)}, u32[]{:S(2)}) %collective-permute-start.1) | collective-permute-done | bytes 49184 | tf_op jit(solution)/shard_map/ppermute | solution.py:494
  183.8 13.5 %prepare.1 = (bf16[2048,256]{1,0:T(8,128)(2,1)}, bf16[256,2048]{1,0:T(8,128)(2,1)}, f32[2048,128]{1,0:T(8,128)}, f32[2048,128]{1,0:T(8,128)}, f32[16,24,128]{2,1,0:T(8,128)}, /*index=5*/f32[128,128]{1,0:T(8,128)}) custom-call(s32[5]{0:T(128)} %pad_add_fusion.scal, f32[2048,384]{1,0:T(8,128)} %copy-done, f32[2048,256]{1,0:T(8,128)} %slice.581.before, ...), custom_call_target="tpu_custom_call" | custom-call | flops 4096000 | bytes 9719828 | tf_op jit(solution)/shard_map/prepare/pallas_call | solution.py:433
  200.0 22.1 %states.2 = (bf16[2048,768]{1,0:T(8,128)(2,1)}, bf16[2048,768]{1,0:T(8,128)(2,1)}, bf16[16,128,768]{2,1,0:T(8,128)(2,1)}, f32[128,768]{1,0:T(8,128)}, f32[8,768]{1,0:T(8,128)}) custom-call(s32[5]{0:T(128)} %pad_add_fusion.scal, f32[2048,768]{1,0:T(8,128)} %fusion.101.cur.before, f32[2048,768]{1,0:T(8,128)} %fusion.101.cur.before, f32[8,768]{1,0:T(8,128)} %fusion.65.halo, ...), custom_call_target="tpu_custom_call" | custom-call | flops 943718400 | bytes 25698324 | tf_op jit(solution)/shard_map/states/pallas_call | solution.py:433
  229.5 21.7 %states.3 = (bf16[2048,768]{1,0:T(8,128)(2,1)}, bf16[2048,768]{1,0:T(8,128)(2,1)}, bf16[16,128,768]{2,1,0:T(8,128)(2,1)}, f32[128,768]{1,0:T(8,128)}, f32[8,768]{1,0:T(8,128)}) custom-call(s32[5]{0:T(128)} %pad_add_fusion.scal, f32[2048,768]{1,0:T(8,128)} %fusion.104.cur.before, f32[2048,768]{1,0:T(8,128)} %fusion.104.cur.before, f32[8,768]{1,0:T(8,128)} %fusion.62.halo, ...), custom_call_target="tpu_custom_call" | custom-call | flops 943718400 | bytes 25698324 | tf_op jit(solution)/shard_map/states/pallas_call | solution.py:433
  252.5 8.6 fusion.106.back
  261.9 20.8 %scan.3 = (f32[2048,768]{1,0:T(8,128)}, f32[8,2048]{1,0:T(8,128)}) custom-call(s32[5]{0:T(128)} %pad_add_fusion.scal, bf16[2048,768]{1,0:T(8,128)(2,1)} %get-tuple-element.181.act, bf16[2048,256]{1,0:T(8,128)(2,1)} %get-tuple-element.175.bc, f32[2048,128]{1,0:T(8,128)} %get-tuple-element.170.steps, f32[2048,128]{1,0:T(8,128)} %get-tuple-element.171.logs, ...), custom_call_target="tpu_custom_call" | custom-call | flops 1887436800 | bytes 29057044 | tf_op jit(solution)/shard_map/scan/pallas_call | solution.py:433
  283.5 20.9 %scan.2 = (f32[2048,768]{1,0:T(8,128)}, f32[8,2048]{1,0:T(8,128)}) custom-call(s32[5]{0:T(128)} %pad_add_fusion.scal, bf16[2048,768]{1,0:T(8,128)(2,1)} %get-tuple-element.174.act, bf16[2048,256]{1,0:T(8,128)(2,1)} %get-tuple-element.175.bc, f32[2048,128]{1,0:T(8,128)} %get-tuple-element.170.steps, f32[2048,128]{1,0:T(8,128)} %get-tuple-element.171.logs, ...), custom_call_target="tpu_custom_call" | custom-call | flops 1887436800 | bytes 29057044 | tf_op jit(solution)/shard_map/scan/pallas_call | solution.py:433
  313.3 20.9 %gate_back.2 = (bf16[2048,768]{1,0:T(8,128)(2,1)}, bf16[2048,768]{1,0:T(8,128)(2,1)}, bf16[2048,768]{1,0:T(8,128)(2,1)}, f32[128,768]{1,0:T(8,128)}, f32[8,768]{1,0:T(8,128)}) custom-call(s32[5]{0:T(128)} %pad_add_fusion.scal, f32[2048,768]{1,0:T(8,128)} %get-tuple-element.179.scanned, bf16[2048,768]{1,0:T(8,128)(2,1)} %get-tuple-element.174.act, ...), custom_call_target="tpu_custom_call" | custom-call | flops 943718400 | bytes 34127892 | tf_op jit(solution)/shard_map/gate_back/pallas_call | solution.py:433
  335.6 20.5 %gate_back.3 = (bf16[2048,768]{1,0:T(8,128)(2,1)}, bf16[2048,768]{1,0:T(8,128)(2,1)}, bf16[2048,768]{1,0:T(8,128)(2,1)}, f32[128,768]{1,0:T(8,128)}, f32[8,768]{1,0:T(8,128)}) custom-call(s32[5]{0:T(128)} %pad_add_fusion.scal, f32[2048,768]{1,0:T(8,128)} %get-tuple-element.186.scanned, bf16[2048,768]{1,0:T(8,128)(2,1)} %get-tuple-element.181.act, ...), custom_call_target="tpu_custom_call" | custom-call | flops 943718400 | bytes 34127892 | tf_op jit(solution)/shard_map/gate_back/pallas_call | solution.py:433
  357.4 7.5 convolution_convert_fusion.4
  381.7 8.4 convolution_convert_fusion
  401.5 9.4 out_other.1
  410.9 9.8 %out_own.1 = f32[1024,1536]{1,0:T(8,128)} custom-call(s32[1]{0:T(128)} %bitcast.scal, bf16[2048,768]{1,0:T(8,128)(2,1)} %get-tuple-element.185.refs_0_, bf16[2048,768]{1,0:T(8,128)(2,1)} %get-tuple-element.187.refs_1_, bf16[768,1536]{1,0:T(8,128)(2,1)} %refs_2_.3, bf16[768,1536]{1,0:T(8,128)(2,1)} %collective-permute-done.8.refs_3_), custom_call_target="tpu_custom_call" | custom-call | flops 4831838208 | bytes 17301508 | tf_op jit(solution)/shard_map/out_own/pallas_call | solution.py:433
  420.7 44.5 %scan_back.2 = (bf16[2048,768]{1,0:T(8,128)(2,1)}, f32[2048,256]{1,0:T(8,128)}, bf16[2048,128]{1,0:T(8,128)(2,1)}, f32[8,768]{1,0:T(8,128)}, f32[8,128]{1,0:T(8,...) custom-call(s32[5]{0:T(128)} %pad_add_fusion.scal, bf16[2048,768]{1,0:T(8,128)(2,1)} %get-tuple-element.181.act, ...), custom_call_target="tpu_custom_call" | custom-call | flops 5662310400 | bytes 45940756 | tf_op jit(solution)/shard_map/scan_back/pallas_call | solution.py:433
  466.5 44.1 %scan_back.3 = (bf16[2048,768]{1,0:T(8,128)(2,1)}, f32[2048,256]{1,0:T(8,128)}, bf16[2048,128]{1,0:T(8,128)(2,1)}, f32[8,768]{1,0:T(8,128)}, f32[8,128]{1,0:T(8,...) custom-call(s32[5]{0:T(128)} %pad_add_fusion.scal, bf16[2048,768]{1,0:T(8,128)(2,1)} %get-tuple-element.174.act, ...), custom_call_target="tpu_custom_call" | custom-call | flops 5662310400 | bytes 45940756 | tf_op jit(solution)/shard_map/scan_back/pallas_call | solution.py:433
  529.1 8.6 convolution_convert_fusion.2
  540.0 8.5 convolution_convert_fusion.3
  551.5 17.1 %back_other.1 = bf16[1024,1536]{1,0:T(8,128)(2,1)} custom-call(s32[1]{0:T(128)} %bitcast.14.scal, bf16[2048,128]{1,0:T(8,128)(2,1)} %copy-done.32, bf16[2048,768]{1,0:T(8,128)(2,1)} %get-tuple-element.201.refs_2_.refs_1_, bf16[2048,768]{1,0:T(8,128)(2,1)} %get-tuple-element.202.refs_3_.refs_2_, bf16[2048,768]{1,0:T(8,128)(2,1)} %copy-done.58, ...), custom_call_target="tpu_custom_call" | custom-call | flops 10066329600 | bytes 26083332 | tf_op jit(solution)/shard_map/back_other/pallas_call | solution.py:433
  581.3 7.0 collective-permute-done.41
  614.3 9.1 collective-permute-done.52
  627.8 20.9 %collective-permute-done.48 = bf16[4,2,96,768]{3,2,0,1:T(8,128)(2,1)S(1)} collective-permute-done((bf16[4,2,96,768]{3,2,0,1:T(8,128)(2,1)S(1)}, bf16[4,2,96,768]{3,2,0,1:T(8,128)(2,1)S(1)}, u32[]{:S(2)}, u32[]{:S(2)}) %collective-permute-start.48) | collective-permute-done | bytes 1179680 | tf_op jit(solution)/shard_map/ppermute | solution.py:485
  650.6 28.5 %collective-permute-done.36 = bf16[4,96,768]{2,1,0:T(8,128)(2,1)S(1)} collective-permute-done((bf16[4,96,768]{2,1,0:T(8,128)(2,1)S(1)}, bf16[4,96,768]{2,1,0:T(8,128)(2,1)S(1)}, u32[]{:S(2)}, u32[]{:S(2)}) %collective-permute-start.36) | collective-permute-done | bytes 589856 | tf_op jit(solution)/shard_map/ppermute | solution.py:485
  687.0 7.0 collective-permute-done.49
  699.5 8.5 collective-permute-done.30
  712.5 17.7 %shared_back.1 = (bf16[2048,256]{1,0:T(8,128)(2,1)}, f32[8,256]{1,0:T(8,128)}, f32[8,256]{1,0:T(8,128)}, f32[8,256]{1,0:T(8,128)}) custom-call(s32[5]{0:T(128)} %pad_add_fusion.scal, f32[2048,256]{1,0:T(8,128)} %copy-done.4, f32[2048,256]{1,0:T(8,128)} %collective-permute-done.14.back_more, f32[2048,384]{1,0:T(8,128)} %copy-done, f32[2048,384]{1,0:T(8,128)} %copy-done, ...), custom_call_target="tpu_custom_call" | custom-call | flops 4096000 | bytes 11575316 | tf_op jit(solution)/shard_map/shared_back/pallas_call | solution.py:433
  745.2 18.4 %back_own.1 = f32[1024,1536]{1,0:T(8,128)} custom-call(s32[1]{0:T(128)} %bitcast.scal, bf16[2048,256]{1,0:T(8,128)(2,1)} %constant_dynamic-update-slice_fusion.2.refs_0_, bf16[2048,128]{1,0:T(8,128)(2,1)} %copy-done.32, bf16[2048,768]{1,0:T(8,128)(2,1)} %get-tuple-element.201.refs_2_.refs_1_, bf16[2048,768]{1,0:T(8,128)(2,1)} %get-tuple-element.202.refs_3_.refs_2_, ...), custom_call_target="tpu_custom_call" | custom-call | flops 10871635968 | bytes 31064068 | tf_op jit(solution)/shard_map/back_own/pallas_call | solution.py:433
  780.3 17.7 %collective-permute-done.38 = bf16[192,768]{1,0:T(8,128)(2,1)S(1)} collective-permute-done((bf16[192,768]{1,0:T(8,128)(2,1)S(1)}, bf16[192,768]{1,0:T(8,128)(2,1)S(1)}, u32[]{:S(2)}, u32[]{:S(2)}) %collective-permute-start.38) | collective-permute-done | bytes 294944 | tf_op jit(solution)/shard_map/ppermute | solution.py:505
  805.8 12.8 %fusion.7 = (f32[1024,1536]{1,0:T(8,128)}, bf16[1024,1536]{1,0:T(8,128)(2,1)}) fusion(bf16[1024,1536]{1,0:T(8,128)(2,1)S(1)} %copy-done.2, bf16[1024,1536]{1,0:T(8,128)(2,1)} %param.53, f32[1024]{0:T(1024)S(1)} %get-tuple-element.217, f32[1024]{0:T(1024)S(1)} %copy-done.47, f32[1536]{0:T(1024)S(1)} %copy-done.36, f32[1024]{0:T(1024)S(1)} %copy-done.38, ...), kind=kLoop, calls=%fused_computation.13 | loop fusion | flops 23592960 | bytes 34621440 | tf_op jit(solution)/shard_map/sub | solution.py:919
  820.4 115.6 %all-reduce.2.cloned.1.call-done = f32[1536,256]{1,0:T(8,128)} async-done(((f32[1536,256]{1,0:T(8,128)}), f32[1536,256]{1,0:T(8,128)}) %all-reduce.2.cloned.1.call-update) | async-done | bytes 1572880 | tf_op jit(solution)/shard_map/psum | solution.py:952
  (411 shorter events, 253.7 us)
Async XLA Ops:
  7.2 928.8 %all-reduce.2.cloned.1.call-start = ((), (), s32[]{:S(2)}) async-start(), calls=%async_computation | async-start | bytes 3145728 | tf_op jit(solution)/shard_map/psum | solution.py:952
  17.5 67.5 %collective-permute-start = (bf16[1024,1536]{1,0:T(8,128)(2,1)}, bf16[1024,1536]{1,0:T(8,128)(2,1)}, u32[]{:S(2)}, u32[]{:S(2)}) collective-permute-start(bf16[1024,1536]{1,0:T(8,128)(2,1)} %get-tuple-element.221), channel_id=1, source_target_pairs={{1,0},{0,1},{3,2},{2,3},{5,4},{4,5},{7,6},{6,7},{9,8},{8,9},{11,10... | collective-permute-start | bytes 9437192 | tf_op jit(solution)/shard_map/ppermute | solution.py:497
  18.0 100.7 %collective-permute-start.5 = (bf16[1536,768]{1,0:T(8,128)(2,1)}, bf16[1536,768]{1,0:T(8,128)(2,1)}, u32[]{:S(2)}, u32[]{:S(2)}) collective-permute-start(bf16[1536,768]{1,0:T(8,128)(2,1)} %refs_8_.3), channel_id=1, source_target_pairs={{2,0},{3,1},{0,2},{1,3},{6,4},{7,5},{4,6},{5,7},{10,8},{11,9},{8,1... | collective-permute-start | bytes 7077896 | tf_op jit(solution)/shard_map/ppermute | solution.py:485
  21.4 52.0 %collective-permute-start.3 = (f32[8,768]{1,0:T(8,128)}, f32[8,768]{1,0:T(8,128)}, u32[]{:S(2)}, u32[]{:S(2)}) collective-permute-start(f32[8,768]{1,0:T(8,128)} %concatenate.74.taps.rows), channel_id=1, source_target_pairs={{2,0},{3,1},{0,2},{1,3},{6,4},{7,5},{4,6},{5,7},{10,8},{11,9},{8,1... | collective-permute-start | bytes 73736 | tf_op jit(solution)/shard_map/ppermute | solution.py:485
  22.5 59.4 %collective-permute-start.2 = (bf16[12,1536]{0,1:T(8,128)(2,1)S(1)}, bf16[12,1536]{0,1:T(8,128)(2,1)}, u32[]{:S(2)}, u32[]{:S(2)}) collective-permute-start(bf16[12,1536]{0,1:T(8,128)(2,1)S(1)} %bitcast.206), channel_id=1, source_target_pairs={{2,0},{3,1},{0,2},{1,3},{6,4},{7,5},{4,6},{5,7},{10,8},{11,9},{8,1... | collective-permute-start | bytes 110600 | tf_op jit(solution)/shard_map/ppermute | solution.py:485
  24.6 84.7 %collective-permute-start.4 = (bf16[1024,1536]{1,0:T(8,128)(2,1)S(1)}, bf16[1024,1536]{1,0:T(8,128)(2,1)}, u32[]{:S(2)}, u32[]{:S(2)}) collective-permute-start(bf16[1024,1536]{1,0:T(8,128)(2,1)S(1)} %copy-done.3), channel_id=1, source_target_pairs={{1,0},{0,1},{3,2},{2,3},{5,4},{4,5},{7,6},{6,7},{9,8},{8,9},{11,10... | collective-permute-start | bytes 9437192 | tf_op jit(solution)/shard_map/ppermute | solution.py:497
  73.5 58.9 %collective-permute-start.7 = (bf16[1536,768]{1,0:T(8,128)(2,1)}, bf16[1536,768]{1,0:T(8,128)(2,1)S(1)}, u32[]{:S(2)}, u32[]{:S(2)}) collective-permute-start(bf16[1536,768]{1,0:T(8,128)(2,1)} %refs_6_.3), channel_id=1, source_target_pairs={{2,0},{3,1},{0,2},{1,3},{6,4},{7,5},{4,6},{5,7},{10,8},{11,9},{8,1... | collective-permute-start | bytes 7077896 | tf_op jit(solution)/shard_map/ppermute | solution.py:485
  81.9 170.6 %collective-permute-start.8 = (bf16[768,1536]{1,0:T(8,128)(2,1)}, bf16[768,1536]{1,0:T(8,128)(2,1)}, u32[]{:S(2)}, u32[]{:S(2)}) collective-permute-start(bf16[768,1536]{1,0:T(8,128)(2,1)} %refs_2_.3), channel_id=1, source_target_pairs={{2,0},{3,1},{0,2},{1,3},{6,4},{7,5},{4,6},{5,7},{10,8},{11,9},{8,1... | collective-permute-start | bytes 7077896 | tf_op jit(solution)/shard_map/ppermute | solution.py:485
  89.9 93.1 %collective-permute-start.1 = (bf16[16,1536]{1,0:T(8,128)(2,1)S(1)}, bf16[16,1536]{1,0:T(8,128)(2,1)S(1)}, u32[]{:S(2)}, u32[]{:S(2)}) collective-permute-start(bf16[16,1536]{1,0:T(8,128)(2,1)S(1)} %slice.579), channel_id=1, source_target_pairs={{0,2},{1,3},{4,6},{5,7},{8,10},{9,11},{12,14},{13,15},{16,18},{17,... | collective-permute-start | bytes 147464 | tf_op jit(solution)/shard_map/ppermute | solution.py:494
  222.2 39.0 %collective-permute-start.9 = (f32[128,768]{1,0:T(8,128)}, f32[128,768]{1,0:T(8,128)S(1)}, u32[]{:S(2)}, u32[]{:S(2)}) collective-permute-start(f32[128,768]{1,0:T(8,128)} %get-tuple-element.183), channel_id=1, source_target_pairs={{0,2},{1,3},{4,6},{5,7},{8,10},{9,11},{12,14},{13,15},{16,18},{17,... | collective-permute-start | bytes 1179656 | tf_op jit(solution)/shard_map/ppermute | solution.py:494
  251.2 31.5 %collective-permute-start.6 = (f32[128,768]{1,0:T(8,128)}, f32[128,768]{1,0:T(8,128)S(1)}, u32[]{:S(2)}, u32[]{:S(2)}) collective-permute-start(f32[128,768]{1,0:T(8,128)} %get-tuple-element.178), channel_id=1, source_target_pairs={{0,2},{1,3},{4,6},{5,7},{8,10},{9,11},{12,14},{13,15},{16,18},{17,... | collective-permute-start | bytes 1179656 | tf_op jit(solution)/shard_map/ppermute | solution.py:494
  334.3 86.4 %collective-permute-start.12 = (f32[128,768]{1,0:T(8,128)}, f32[128,768]{1,0:T(8,128)}, u32[]{:S(2)}, u32[]{:S(2)}) collective-permute-start(f32[128,768]{1,0:T(8,128)} %get-tuple-element.190), channel_id=1, source_target_pairs={{2,0},{3,1},{6,4},{7,5},{10,8},{11,9},{14,12},{15,13},{18,16},{19,... | collective-permute-start | bytes 1179656 | tf_op jit(solution)/shard_map/ppermute | solution.py:494
  356.1 110.5 %collective-permute-start.13 = (f32[128,768]{1,0:T(8,128)}, f32[128,768]{1,0:T(8,128)}, u32[]{:S(2)}, u32[]{:S(2)}) collective-permute-start(f32[128,768]{1,0:T(8,128)} %get-tuple-element.194), channel_id=1, source_target_pairs={{2,0},{3,1},{6,4},{7,5},{10,8},{11,9},{14,12},{15,13},{18,16},{19,... | collective-permute-start | bytes 1179656 | tf_op jit(solution)/shard_map/ppermute | solution.py:494
  366.2 259.0 %collective-permute-start.24 = (bf16[4,2,96,768]{3,2,0,1:T(8,128)(2,1)}, bf16[4,2,96,768]{3,2,0,1:T(8,128)(2,1)}, u32[]{:S(2)}, u32[]{:S(2)}) collective-permute-start(bf16[4,2,96,768]{3,2,0,1:T(8,128)(2,1)} %copy.49), channel_id=1, source_target_pairs={{2,0},{3,1},{0,2},{1,3},{6,4},{7,5},{4,6},{5,7},{10,8},{11,9},{8,1... | collective-permute-start | bytes 3538952 | tf_op jit(solution)/shard_map/ppermute | solution.py:485
  376.8 212.0 %collective-permute-start.27 = (bf16[4,96,768]{2,1,0:T(8,128)(2,1)}, bf16[4,96,768]{2,1,0:T(8,128)(2,1)}, u32[]{:S(2)}, u32[]{:S(2)}) collective-permute-start(bf16[4,96,768]{2,1,0:T(8,128)(2,1)} %dynamic-slice_bitcast_fusion.6), channel_id=1, source_target_pairs={{4,0},{0,4},{12,8},{8,12},{20,16},{16,20},{28,24},{24,28},{5,1},{1... | collective-permute-start | bytes 1769480 | tf_op jit(solution)/shard_map/ppermute | solution.py:501
  379.1 219.2 %collective-permute-start.26 = (bf16[4,96,768]{2,1,0:T(8,128)(2,1)}, bf16[4,96,768]{2,1,0:T(8,128)(2,1)}, u32[]{:S(2)}, u32[]{:S(2)}) collective-permute-start(bf16[4,96,768]{2,1,0:T(8,128)(2,1)} %dynamic-slice_bitcast_fusion.7), channel_id=1, source_target_pairs={{4,0},{0,4},{12,8},{8,12},{20,16},{16,20},{28,24},{24,28},{5,1},{1... | collective-permute-start | bytes 1769480 | tf_op jit(solution)/shard_map/ppermute | solution.py:501
  465.2 53.8 %collective-permute-start.16 = (f32[8,768]{1,0:T(8,128)}, f32[8,768]{1,0:T(8,128)}, u32[]{:S(2)}, u32[]{:S(2)}) collective-permute-start(f32[8,768]{1,0:T(8,128)} %get-tuple-element.205), channel_id=1, source_target_pairs={{2,0},{3,1},{6,4},{7,5},{10,8},{11,9},{14,12},{15,13},{18,16},{19,... | collective-permute-start | bytes 73736 | tf_op jit(solution)/shard_map/ppermute | solution.py:494
  519.0 54.2 %collective-permute-start.40 = (f32[12,1536]{1,0:T(8,128)S(1)}, f32[12,1536]{1,0:T(8,128)S(1)}, u32[]{:S(2)}, u32[]{:S(2)}) collective-permute-start(f32[12,1536]{1,0:T(8,128)S(1)} %slice_bitcast_fusion), channel_id=1, source_target_pairs={{2,0},{3,1},{0,2},{1,3},{6,4},{7,5},{4,6},{5,7},{10,8},{11,9},{8,1... | collective-permute-start | bytes 221192 | tf_op jit(solution)/shard_map/ppermute | solution.py:485
  523.8 24.9 %collective-permute-start.44 = (f32[8,768]{1,0:T(8,128)}, f32[8,768]{1,0:T(8,128)}, u32[]{:S(2)}, u32[]{:S(2)}) collective-permute-start(f32[8,768]{1,0:T(8,128)} %maximum_maximum_fusion), channel_id=1, source_target_pairs={{2,0},{3,1},{0,2},{1,3},{6,4},{7,5},{4,6},{5,7},{10,8},{11,9},{8,1... | collective-permute-start | bytes 73736 | tf_op jit(solution)/shard_map/ppermute | solution.py:485
  604.5 44.2 %collective-permute-start.48 = (bf16[4,2,96,768]{3,2,0,1:T(8,128)(2,1)S(1)}, bf16[4,2,96,768]{3,2,0,1:T(8,128)(2,1)S(1)}, u32[]{:S(2)}, u32[]{:S(2)}) collective-permute-start(bf16[4,2,96,768]{3,2,0,1:T(8,128)(2,1)S(1)} %copy-done.28), channel_id=1, source_target_pairs={{2,0},{3,1},{0,2},{1,3},{6,4},{7,5},{4,6},{5,7},{10,8},{11,9},{8,1... | collective-permute-start | bytes 3538952 | tf_op jit(solution)/shard_map/ppermute | solution.py:485
  610.8 101.7 %collective-permute-start.14 = (f32[2048,256]{1,0:T(8,128)S(1)}, f32[2048,256]{1,0:T(8,128)}, u32[]{:S(2)}, u32[]{:S(2)}) collective-permute-start(f32[2048,256]{1,0:T(8,128)S(1)} %add.704.back_bc), channel_id=1, source_target_pairs={{1,0},{0,1},{3,2},{2,3},{5,4},{4,5},{7,6},{6,7},{9,8},{8,9},{11,10... | collective-permute-start | bytes 6291464 | tf_op jit(solution)/shard_map/ppermute | solution.py:497
  612.6 73.2 %collective-permute-start.32 = (bf16[4,2,96,768]{3,2,0,1:T(8,128)(2,1)S(1)}, bf16[4,2,96,768]{3,2,0,1:T(8,128)(2,1)S(1)}, u32[]{:S(2)}, u32[]{:S(2)}) collective-permute-start(bf16[4,2,96,768]{3,2,0,1:T(8,128)(2,1)S(1)} %copy.57), channel_id=1, source_target_pairs={{2,0},{3,1},{0,2},{1,3},{6,4},{7,5},{4,6},{5,7},{10,8},{11,9},{8,1... | collective-permute-start | bytes 3538952 | tf_op jit(solution)/shard_map/ppermute | solution.py:485
  623.4 27.1 %collective-permute-start.34 = (bf16[4,96,768]{2,1,0:T(8,128)(2,1)S(1)}, bf16[4,96,768]{2,1,0:T(8,128)(2,1)S(1)}, u32[]{:S(2)}, u32[]{:S(2)}) collective-permute-start(bf16[4,96,768]{2,1,0:T(8,128)(2,1)S(1)} %dynamic-slice_bitcast_fusion.4), channel_id=1, source_target_pairs={{4,0},{0,4},{12,8},{8,12},{20,16},{16,20},{28,24},{24,28},{5,1},{1... | collective-permute-start | bytes 1769480 | tf_op jit(solution)/shard_map/ppermute | solution.py:501
  625.2 54.0 %collective-permute-start.36 = (bf16[4,96,768]{2,1,0:T(8,128)(2,1)S(1)}, bf16[4,96,768]{2,1,0:T(8,128)(2,1)S(1)}, u32[]{:S(2)}, u32[]{:S(2)}) collective-permute-start(bf16[4,96,768]{2,1,0:T(8,128)(2,1)S(1)} %fusion.18), channel_id=1, source_target_pairs={{2,0},{3,1},{0,2},{1,3},{6,4},{7,5},{4,6},{5,7},{10,8},{11,9},{8,1... | collective-permute-start | bytes 1769480 | tf_op jit(solution)/shard_map/ppermute | solution.py:485
  648.7 32.5 %collective-permute-start.25 = (bf16[4,96,768]{2,1,0:T(8,128)(2,1)S(1)}, bf16[4,96,768]{2,1,0:T(8,128)(2,1)S(1)}, u32[]{:S(2)}, u32[]{:S(2)}) collective-permute-start(bf16[4,96,768]{2,1,0:T(8,128)(2,1)S(1)} %dynamic-slice_bitcast_fusion.8), channel_id=1, source_target_pairs={{4,0},{0,4},{12,8},{8,12},{20,16},{16,20},{28,24},{24,28},{5,1},{1... | collective-permute-start | bytes 1769480 | tf_op jit(solution)/shard_map/ppermute | solution.py:501
  650.6 113.0 %collective-permute-start.18 = (bf16[1024,1536]{1,0:T(8,128)(2,1)}, bf16[1024,1536]{1,0:T(8,128)(2,1)}, u32[]{:S(2)}, u32[]{:S(2)}) collective-permute-start(bf16[1024,1536]{1,0:T(8,128)(2,1)} %back_other.1), channel_id=1, source_target_pairs={{1,0},{0,1},{3,2},{2,3},{5,4},{4,5},{7,6},{6,7},{9,8},{8,9},{11,10... | collective-permute-start | bytes 9437192 | tf_op jit(solution)/shard_map/ppermute | solution.py:497
  707.9 97.8 %collective-permute-start.11 = (bf16[1024,1536]{1,0:T(8,128)(2,1)}, bf16[1024,1536]{1,0:T(8,128)(2,1)}, u32[]{:S(2)}, u32[]{:S(2)}) collective-permute-start(bf16[1024,1536]{1,0:T(8,128)(2,1)} %out_other.1), channel_id=1, source_target_pairs={{1,0},{0,1},{3,2},{2,3},{5,4},{4,5},{7,6},{6,7},{9,8},{8,9},{11,10... | collective-permute-start | bytes 9437192 | tf_op jit(solution)/shard_map/ppermute | solution.py:497
  708.0 62.3 %collective-permute-start.55 = (bf16[192,768]{1,0:T(8,128)(2,1)}, bf16[192,768]{1,0:T(8,128)(2,1)}, u32[]{:S(2)}, u32[]{:S(2)}) collective-permute-start(bf16[192,768]{1,0:T(8,128)(2,1)} %get-tuple-element.238), channel_id=1, source_target_pairs={{8,0},{12,4},{16,8},{20,12},{24,16},{28,20},{0,24},{4,28},{9,1},{1... | collective-permute-start | bytes 884744 | tf_op jit(solution)/shard_map/ppermute | solution.py:505
  709.2 62.9 %collective-permute-start.54 = (bf16[192,768]{1,0:T(8,128)(2,1)}, bf16[192,768]{1,0:T(8,128)(2,1)}, u32[]{:S(2)}, u32[]{:S(2)}) collective-permute-start(bf16[192,768]{1,0:T(8,128)(2,1)} %get-tuple-element.237), channel_id=1, source_target_pairs={{16,0},{20,4},{24,8},{28,12},{0,16},{4,20},{8,24},{12,28},{17,1},{... | collective-permute-start | bytes 884744 | tf_op jit(solution)/shard_map/ppermute | solution.py:505
  735.9 37.0 %collective-permute-start.53 = (bf16[192,768]{1,0:T(8,128)(2,1)S(1)}, bf16[192,768]{1,0:T(8,128)(2,1)}, u32[]{:S(2)}, u32[]{:S(2)}) collective-permute-start(bf16[192,768]{1,0:T(8,128)(2,1)S(1)} %get-tuple-element.236), channel_id=1, source_target_pairs={{24,0},{28,4},{0,8},{4,12},{8,16},{12,20},{16,24},{20,28},{25,1},{... | collective-permute-start | bytes 884744 | tf_op jit(solution)/shard_map/ppermute | solution.py:505
  772.2 25.9 %collective-permute-start.38 = (bf16[192,768]{1,0:T(8,128)(2,1)S(1)}, bf16[192,768]{1,0:T(8,128)(2,1)S(1)}, u32[]{:S(2)}, u32[]{:S(2)}) collective-permute-start(bf16[192,768]{1,0:T(8,128)(2,1)S(1)} %get-tuple-element.240), channel_id=1, source_target_pairs={{16,0},{20,4},{24,8},{28,12},{0,16},{4,20},{8,24},{12,28},{17,1},{... | collective-permute-start | bytes 884744 | tf_op jit(solution)/shard_map/ppermute | solution.py:505
  772.2 25.8 %collective-permute-start.37 = (bf16[192,768]{1,0:T(8,128)(2,1)S(1)}, bf16[192,768]{1,0:T(8,128)(2,1)S(1)}, u32[]{:S(2)}, u32[]{:S(2)}) collective-permute-start(bf16[192,768]{1,0:T(8,128)(2,1)S(1)} %get-tuple-element.239), channel_id=1, source_target_pairs={{24,0},{28,4},{0,8},{4,12},{8,16},{12,20},{16,24},{20,28},{25,1},{... | collective-permute-start | bytes 884744 | tf_op jit(solution)/shard_map/ppermute | solution.py:505
  (101 other events, 1604.0 us)
Sparse Core Ops, SparseCore 0:
  803.8 132.0 all-reduce.1

commit v2 on v1

v2 whole, which is shorter than its diff:
```python
from functools import partial

import jax
import jax.numpy as jnp
import numpy as np
from jax import lax
from jax.experimental import pallas as pl
from jax.experimental.pallas import tpu as pltpu
from jax.sharding import PartitionSpec as P

Q = 128
STATE = 128
HEAD = 64
EPS = 1e-05
LOG2E = 1.4426950408889634
NEVER = -1e30
F32 = jnp.float32
BF16 = jnp.bfloat16
HIGH = lax.Precision.HIGHEST
VMEM_LIMIT = 56 * 1024 * 1024
STEP_ROWS = 512

NN = (((1,), (0,)), ((), ()))
NT = (((1,), (1,)), ((), ()))
TN = (((0,), (0,)), ((), ()))


def dot(a, b, dims=NN, precision=None):
    return lax.dot_general(a, b, dims, precision=precision, preferred_element_type=F32)


STEP, LOG, MARK, RISE = 0, 32, 64, 96
CARRIES, ENDING, VALID, SEGMENT = MARK, MARK + 1, MARK + 2, MARK + 3
EARLIER, LATER = MARK + 3, MARK + 6


def loop(count, body):
    def step(k, carry):
        body(k)
        return carry

    lax.fori_loop(0, count, step, 0, unroll=True)


def group_of(ref, k):
    return ref.at[pl.ds(pl.multiple_of(k * Q, Q), Q), :]


def lane_group_of(ref, k):
    return ref.at[:, pl.ds(pl.multiple_of(k * Q, Q), Q)]


def segment_of(scal, position):
    end = scal[0]
    count = (position >= end).astype(jnp.int32)
    for k in range(1, 4):
        end = end + scal[k]
        count = count + (position >= end).astype(jnp.int32)
    return count


def same_segment(scal, position, other):
    return (segment_of(scal, position) == segment_of(scal, other)).astype(F32)


def kept(scal, group):
    first = scal[4] + group * Q
    return same_segment(scal, first - 1, first + Q - 1)


def reaches(scal, group):
    return same_segment(scal, scal[4] + group * Q - 1, scal[4] - 1)


def triangle(cols, rows, flipped):
    first = lax.broadcasted_iota(jnp.int32, (Q, Q), 0)
    second = lax.broadcasted_iota(jnp.int32, (Q, Q), 1)
    ordered = (first <= second) if flipped else (first >= second)
    allowed = ordered & (cols[:, SEGMENT : SEGMENT + 1] == rows[LOG : LOG + 1, :])
    return jnp.where(allowed, 0.0, NEVER)


def in_first(rows):
    return lax.broadcasted_iota(jnp.int32, (rows, 2 * HEAD), 1) < HEAD


def pair_of(columns, lane):
    rows = columns.shape[0]
    first = jnp.broadcast_to(columns[:, lane : lane + 1], (rows, 2 * HEAD))
    second = jnp.broadcast_to(columns[:, lane + 1 : lane + 2], (rows, 2 * HEAD))
    return jnp.where(in_first(rows), first, second)


def spread_heads(columns, lane, channels):
    return jnp.concatenate(
        [pair_of(columns, lane + 2 * p) for p in range(channels // (2 * HEAD))], axis=1
    )


def stacked_heads(member):
    first = in_first(member.shape[0])
    none = jnp.zeros_like(member)
    return jnp.concatenate([jnp.where(first, member, none), jnp.where(first, none, member)], axis=0)


def split_sum(member, picks):
    high = member.astype(BF16)
    rest = (member - high.astype(F32)).astype(BF16)
    return dot(high, picks) + dot(rest, picks)


def in_order(member, ordered):
    first = member.astype(BF16).astype(F32)
    rest = member - first
    second = rest.astype(BF16).astype(F32)
    parts = first + pltpu.roll(second, 32, 1) + pltpu.roll(rest - second, 64, 1)
    total = dot(ordered.astype(BF16), parts.astype(BF16))
    return total + pltpu.roll(total, 96, 1) + pltpu.roll(total, 64, 1)


def sigmoid(v):
    return 0.5 * jnp.tanh(0.5 * v) + 0.5


def conv_before_act(ext, taps, cols):
    total = ext[8 : 8 + Q, :] * taps[3:4, :] + taps[4:5, :]
    for j in range(1, 4):
        same = cols[:, EARLIER + j : EARLIER + j + 1]
        total = total + (ext[8 - j : 8 - j + Q, :] * same) * taps[3 - j : 4 - j, :]
    return total


def follow(group, ext, halo, current):
    @pl.when(group == 0)
    def _():
        ext[0:8, :] = halo[8:16, :].astype(F32)

    @pl.when(group > 0)
    def _():
        ext[0:8, :] = ext[Q : Q + 8, :]

    ext[8 : 8 + Q, :] = current.astype(F32)


def prepare_kernel(
    subs, scal, shared, rates, halo, taps, head_rows, bc_out, bct_out, cols_out, rows_out, total_out,
    ext, running,
):
    @pl.when(pl.program_id(0) == 0)
    def _():
        running[...] = jnp.zeros_like(running)

    def body(k):
        group = pl.program_id(0) * subs + k
        bc, cols = group_of(bc_out, k), group_of(cols_out, k)
        bct, rows = lane_group_of(bct_out, k), rows_out.at[k]
        width = bc.shape[1]
        raw = group_of(rates, k)[...] + head_rows[0:1, :]
        step = jnp.maximum(raw, 0.0) + jnp.log1p(jnp.exp(-jnp.abs(raw)))
        scaled = step * (head_rows[1:2, :] * LOG2E)
        at = lax.broadcasted_iota(jnp.int32, (Q, Q), 0)
        lane = lax.broadcasted_iota(jnp.int32, (Q, Q), 1)
        summed = in_order(jnp.where(lane < 32, scaled, 0.0), (at >= lane).astype(F32))
        first = scal[4] + group * Q
        position = first + at[:, 0:1]
        segment = segment_of(scal, position)
        marks = {
            CARRIES: segment == segment_of(scal, first - 1),
            ENDING: segment == segment_of(scal, first + Q - 1),
            VALID: position < scal[0] + scal[1] + scal[2] + scal[3],
        }
        for j in range(1, 4):
            marks[EARLIER + j] = segment == segment_of(scal, position - j)
            marks[LATER + j] = segment == segment_of(scal, position + j)
        member = jnp.where(lane == SEGMENT, segment.astype(F32), 0.0)
        for mark, found in marks.items():
            member = jnp.where(lane == mark, found.astype(F32), member)
        member = jnp.where(lane < LOG, step, member)
        member = jnp.where((lane >= LOG) & (lane < MARK), pltpu.roll(summed, LOG, 1), member)
        member = jnp.where(lane >= RISE, pltpu.roll(sigmoid(raw), RISE, 1), member)
        cols[...] = member
        across = member.T
        rows[0:LOG, :] = across[LOG:MARK]
        rows[LOG : LOG + 8, :] = across[SEGMENT : SEGMENT + 8]
        total_out[pl.ds(pl.multiple_of(k * 8, 8), 8), :] = running[...]
        running[...] = running[...] + summed[Q - 1 : Q, :]

        follow(group, ext, halo, group_of(shared, k)[...])
        pre = conv_before_act(ext, taps, cols)
        act = pre * sigmoid(pre)
        bc[...] = act.astype(BF16)
        bct[...] = jnp.concatenate(
            [act[:, m * STATE : (m + 1) * STATE].T for m in range(width // STATE)], axis=0
        ).astype(BF16)

    loop(subs, body)


def states_kernel(
    subs, head, scal, raw, halo, taps, cols_in, bct_in, total, act_out, slope_out, states, final,
    through, ext, state,
):
    channels = raw.shape[1]

    @pl.when(pl.program_id(0) == 0)
    def _():
        state[...] = jnp.zeros_like(state)

    def body(k):
        group = pl.program_id(0) * subs + k
        cols, bct = group_of(cols_in, k), lane_group_of(bct_in, k)
        follow(group, ext, halo, group_of(raw, k)[...])
        pre = conv_before_act(ext, taps, cols)
        gate = sigmoid(pre)
        act = (pre * gate).astype(BF16)
        group_of(act_out, k)[...] = act
        group_of(slope_out, k)[...] = (gate * (1.0 + pre * (1.0 - gate))).astype(BF16)
        summed = spread_heads(cols[...], LOG + head, channels)
        last = summed[Q - 1 : Q, :]
        tails = jnp.exp2(last - summed) * cols[:, ENDING : ENDING + 1]
        scaled = (act.astype(F32) * spread_heads(cols[...], STEP + head, channels)).astype(BF16)
        fresh = dot(bct[:STATE, :], (scaled.astype(F32) * tails).astype(BF16))
        states[k] = state[...].astype(BF16)
        state[...] = state[...] * (jnp.exp2(last) * kept(scal, group)) + fresh

    loop(subs, body)

    @pl.when(pl.program_id(0) == pl.num_programs(0) - 1)
    def _():
        final[...] = state[...]
        at = (subs - 1) * 8
        ended = total[at : at + 8, :] + pltpu.roll(cols_in[subs * Q - 8 : subs * Q, :], 128 - LOG, 1)[7:8]
        through[...] = jnp.exp2(spread_heads(ended, head, channels)) * reaches(
            scal, pl.num_programs(0) * subs
        )


def total_share(scal, group, head, total, k, channels):
    here = total[pl.ds(pl.multiple_of(k * 8, 8), 8), :]
    return jnp.exp2(spread_heads(here, head, channels))[0:1] * reaches(scal, group)


def scan_kernel(
    subs, head, scal, act_in, bc_in, cols_in, rows_in, total, gate_in, back_in, states, start, taps,
    scanned_out, stats_out,
):
    channels = act_in.shape[1]

    def body(k):
        group = pl.program_id(0) * subs + k
        act, bc, cols = group_of(act_in, k), group_of(bc_in, k), group_of(cols_in, k)
        gate, back, rows = group_of(gate_in, k), group_of(back_in, k), rows_in.at[k]
        scanned = group_of(scanned_out, k)
        b_map, c_map = bc[:, :STATE], bc[:, STATE:]
        scores = dot(c_map, b_map, NT)
        allowed = triangle(cols, rows, False)
        carries = cols[:, CARRIES : CARRIES + 1]
        share = total_share(scal, group, head, total, k, channels)
        state = (states[k].astype(F32) + share * start[...]).astype(BF16)
        outside = dot(c_map, state)
        squares = jnp.zeros((Q, 2 * HEAD), F32)
        inner = jnp.zeros((Q, 2 * HEAD), F32)
        for p in range(channels // (2 * HEAD)):
            part = slice(2 * HEAD * p, 2 * HEAD * (p + 1))
            weights = []
            columns = []
            for h in (head + 2 * p, head + 2 * p + 1):
                column = jnp.broadcast_to(cols[:, LOG + h : LOG + h + 1], (Q, Q))
                columns.append(column)
                decay = jnp.exp2(column + (allowed - rows[h : h + 1, :]))
                weights.append((decay * scores).astype(BF16))
            summed = jnp.where(in_first(Q), columns[0], columns[1])
            member = act[:, part].astype(F32)
            scaled = (member * pair_of(cols[...], STEP + head + 2 * p)).astype(BF16)
            result = dot(jnp.concatenate(weights, axis=1), stacked_heads(scaled))
            result = result + outside[:, part] * (jnp.exp2(summed) * carries)
            scanned[:, part] = result
            mixed_heads = result + taps[6:7, part] * member
            raw = gate[:, part].astype(F32)
            gated = mixed_heads * (raw * sigmoid(raw))
            squares = squares + gated * gated
            inner = inner + back[:, part].astype(F32) * taps[5:6, part] * gated
        squares = jnp.sum(squares, axis=1, keepdims=True)
        inner = jnp.sum(inner, axis=1, keepdims=True) * cols[:, VALID : VALID + 1]
        lane = lax.broadcasted_iota(jnp.int32, (Q, Q), 1)
        both = jnp.where(lane == 0, squares, jnp.where(lane == 1, inner, 0.0))
        lane_group_of(stats_out, k)[...] = both.T[:8]

    loop(subs, body)


def gate_back_kernel(
    subs, head, inner_channels, scal, scanned_in, act_in, gate_in, back_in, stats_in, bct_in, cols_in,
    total, taps, mixed_out, low_gate_out, back_heads_out, reach, sums,
):
    channels = act_in.shape[1]

    @pl.when(pl.program_id(0) == 0)
    def _():
        reach[...] = jnp.zeros_like(reach)
        sums[...] = jnp.zeros_like(sums)

    def body(k):
        group = pl.program_id(0) * subs + k
        scanned, act, gate = group_of(scanned_in, k), group_of(act_in, k), group_of(gate_in, k)
        back, cols, stats = group_of(back_in, k), group_of(cols_in, k), lane_group_of(stats_in, k)
        mixed, low_gate = group_of(mixed_out, k), group_of(low_gate_out, k)
        back_heads, bct = group_of(back_heads_out, k), lane_group_of(bct_in, k)
        row = lax.broadcasted_iota(jnp.int32, (8, Q), 0)
        inverse_row = lax.rsqrt(stats[...] / inner_channels + EPS)
        both = jnp.concatenate(
            [jnp.where(row == 0, inverse_row, stats[...]), jnp.zeros((Q - 8, Q), F32)], axis=0
        ).T
        inverse, inner = both[:, 0:1], both[:, 1:2]
        valid, carries = cols[:, VALID : VALID + 1], cols[:, CARRIES : CARRIES + 1]
        slope = inverse * inverse * inverse * inner * valid / inner_channels
        inverse_valid = inverse * valid
        gradients = []
        for p in range(channels // (2 * HEAD)):
            part = slice(2 * HEAD * p, 2 * HEAD * (p + 1))
            member = act[:, part].astype(F32)
            mixed_heads = scanned[:, part] + taps[6:7, part] * member
            raw = gate[:, part].astype(F32)
            share = sigmoid(raw)
            opened = raw * share
            gated = mixed_heads * opened
            gain = taps[5:6, part]
            mixed[:, part] = (gated * inverse_valid * gain).astype(BF16)
            scaled_back = back[:, part].astype(F32) * inverse_valid
            gradient = scaled_back * gain - gated * slope
            low_gate[:, part] = (gradient * mixed_heads * (share + opened * (1.0 - share))).astype(BF16)
            low = (gradient * opened).astype(BF16)
            back_heads[:, part] = low
            wide = low.astype(F32)
            sums[0:1, part] = sums[0:1, part] + jnp.sum(scaled_back * gated, axis=0, keepdims=True)
            sums[1:2, part] = sums[1:2, part] + jnp.sum(wide * member, axis=0, keepdims=True)
            entered = jnp.exp2(pair_of(cols[...], LOG + head + 2 * p)) * carries
            gradients.append((wide * entered).astype(BF16))
        share = total_share(scal, group, head, total, k, channels)
        reach[...] = reach[...] + share * dot(bct[STATE:, :], jnp.concatenate(gradients, axis=1))

    loop(subs, body)


def first_sent_back(scal, later, taps):
    row = lax.broadcasted_iota(jnp.int32, (16, 1), 0)
    out = jnp.zeros((16, later.shape[1]), F32)
    for back in range(1, 4):
        at = scal[4] - back
        extra = jnp.zeros((1, later.shape[1]), F32)
        for j in range(back, 4):
            same = same_segment(scal, at, at + j)
            extra = extra + same * taps[3 - j : 4 - j, :] * later[j - back : j - back + 1, :]
        out = jnp.where(row == 16 - back, extra, out)
    return out


def scan_back_kernel(
    subs, head, scal, act_in, slope_in, heads_in, scanned_in, raw, before, halo, taps, picks, bc_in,
    bct_in, cols_in, rows_in, total, head_rows, states, start, leaving, low_out, back_bc_out,
    low_rate_out, sums, head_out, first_rows, last_rows, ext, back_ext, back_state, difference,
):
    turn = pl.program_id(0)
    turns = pl.num_programs(0) - 1
    channels = act_in.shape[1]

    @pl.when(turn == 0)
    def _():
        back_state[...] = leaving[...]
        back_ext[Q : Q + 8, :] = jnp.zeros_like(back_ext[Q : Q + 8, :])
        sums[...] = jnp.zeros_like(sums)
        head_out[...] = jnp.zeros_like(head_out)

    def body(count):
        k = subs - 1 - count
        group = (turns - 1 - turn) * subs + k
        act, slope, back_heads = group_of(act_in, k), group_of(slope_in, k), group_of(heads_in, k)
        scanned, bc, cols = group_of(scanned_in, k), group_of(bc_in, k), group_of(cols_in, k)
        bct, rows, back_bc = lane_group_of(bct_in, k), rows_in.at[k], group_of(back_bc_out, k)
        b_map, c_map = bc[:, :STATE], bc[:, STATE:]
        scores = dot(b_map, c_map, NT)
        allowed = triangle(cols, rows, True)
        carries, ending = cols[:, CARRIES : CARRIES + 1], cols[:, ENDING : ENDING + 1]
        share = total_share(scal, group, head, total, k, channels)
        state = states[k].astype(F32) + share * start[...]
        state_low = state.astype(BF16)
        leaving_low = back_state[...].astype(BF16)
        from_state = dot(b_map, leaving_low)
        back_scores = jnp.zeros((Q, Q), F32)
        into_state, out_of_state, passed, products = [], [], [], []
        for p in range(channels // (2 * HEAD)):
            part = slice(2 * HEAD * p, 2 * HEAD * (p + 1))
            low = back_heads[:, part]
            wide = low.astype(F32)
            member = act[:, part].astype(F32)
            step = pair_of(cols[...], STEP + head + 2 * p)
            scaled = (member * step).astype(BF16)
            back_weights = dot(stacked_heads(scaled), low, NT)
            weights, columns = [], []
            for m, h in enumerate((head + 2 * p, head + 2 * p + 1)):
                column = jnp.broadcast_to(cols[:, LOG + h : LOG + h + 1], (Q, Q))
                columns.append(column)
                decay = jnp.exp2((rows[h : h + 1, :] + allowed) - column)
                weights.append((decay * scores).astype(BF16))
                back_scores = back_scores + decay * back_weights[m * Q : (m + 1) * Q]
            summed = jnp.where(in_first(Q), columns[0], columns[1])
            last = summed[Q - 1 : Q, :]
            tails = jnp.exp2(last - summed) * ending
            back_scaled = dot(jnp.concatenate(weights, axis=1), stacked_heads(low))
            scaled_wide = scaled.astype(F32)
            from_end = tails * from_state[:, part]
            difference[:, part] = wide * scanned[:, part] - scaled_wide * back_scaled
            passed.append((scaled_wide * from_end).astype(BF16))
            back_scaled = back_scaled + from_end
            into_state.append((scaled_wide * tails).astype(BF16))
            out_of_state.append((wide * (jnp.exp2(summed) * carries)).astype(BF16))
            products.append((back_scaled * member).astype(BF16))
            back_act = back_scaled * step + taps[6:7, part] * wide
            back_ext[0:Q, part] = back_act * slope[:, part].astype(F32)
        into_state = jnp.concatenate(into_state, axis=1)
        out_of_state = jnp.concatenate(out_of_state, axis=1)
        back_b = dot(back_scores.astype(BF16), c_map) + dot(into_state, leaving_low, NT)
        back_c = dot(back_scores.T.astype(BF16), b_map) + dot(out_of_state, state_low, NT)
        back_bc[:, :STATE] = back_b
        back_bc[:, STATE:] = back_c

        whole_group = spread_heads(cols[Q - 1 : Q, :], LOG + head, channels)
        kept_state = back_state[...] * (jnp.exp2(whole_group) * kept(scal, group))
        back_state[...] = kept_state + dot(bct[STATE:, :], out_of_state)
        crossing = jnp.sum(kept_state * state, axis=0, keepdims=True)
        difference[Q - 1 : Q, :] = difference[Q - 1 : Q, :] + crossing

        product = dot(jnp.concatenate(products, axis=1), picks[...])
        at = lax.broadcasted_iota(jnp.int32, (Q, Q), 0)
        lane = lax.broadcasted_iota(jnp.int32, (Q, Q), 1)
        before_it = dot(jnp.concatenate(passed, axis=1), picks[...])
        back_logs = in_order(split_sum(difference[...], picks[...]), at <= lane) + dot(
            (at > lane).astype(BF16), before_it.astype(BF16)
        )
        decays = jnp.where(lane < LOG, back_logs * head_rows[1:2, :], 0.0)
        back_rate = (product + decays) * pltpu.roll(cols[...], 128 - RISE, 1)
        back_rate = jnp.where(lane < LOG, back_rate, 0.0)
        group_of(low_rate_out, k)[...] = back_rate.astype(BF16)
        head_out[0:1, :] = head_out[0:1, :] + jnp.sum(back_rate, axis=0, keepdims=True)
        head_out[1:2, :] = head_out[1:2, :] + jnp.sum(decays * cols[...], axis=0, keepdims=True)

        conv_back(turn, k, ext, back_ext, raw, before, halo, taps, cols, group_of(low_out, k), sums,
                  first_rows, last_rows, group)

    @pl.when(turn < turns)
    def _():
        loop(subs, body)

    @pl.when(turn == turns)
    def _():
        low_rate_out[...] = jnp.zeros_like(low_rate_out)
        low_out[...] = jnp.zeros_like(low_out)
        low_out[0:16, :] = first_sent_back(scal, first_rows, taps).astype(BF16)


def conv_back(
    turn, k, ext, back_ext, raw, before, halo, taps, cols, low, sums, first_rows, last_rows, group
):
    start = pl.multiple_of(jnp.maximum(k * Q - 16, 0), 16)
    earlier = jnp.where(group == 0, halo[...], before[...])
    earlier = jnp.where(k == 0, earlier, raw[pl.ds(start, 16), :])
    ext[0:8, :] = earlier[8:16].astype(F32)
    ext[8 : 8 + Q, :] = group_of(raw, k)[...].astype(F32)
    now = back_ext[0:Q, :]
    sums[3:4, :] = sums[3:4, :] + jnp.sum(now * ext[8 : 8 + Q, :], axis=0, keepdims=True)
    sums[4:5, :] = sums[4:5, :] + jnp.sum(now, axis=0, keepdims=True)
    total = now * taps[3:4, :]
    for j in range(1, 4):
        tap = slice(3 - j, 4 - j)
        earlier = ext[8 - j : 8 - j + Q, :] * cols[:, EARLIER + j : EARLIER + j + 1]
        sums[tap, :] = sums[tap, :] + jnp.sum(now * earlier, axis=0, keepdims=True)
        later = back_ext[j : j + Q, :] * cols[:, LATER + j : LATER + j + 1]
        total = total + later * taps[tap, :]
    low[...] = total.astype(BF16)

    @pl.when((turn == 0) & (k == raw.shape[0] // Q - 1))
    def _():
        last_rows[...] = total[Q - 8 : Q, :]

    back_ext[Q : Q + 8, :] = back_ext[0:8, :]
    first_rows[...] = back_ext[0:8, :]


def shared_back_kernel(
    subs, scal, back_bc, back_more, raw, before, halo, taps, cols_in, low_out, sums, first_rows,
    last_rows, ext, back_ext,
):
    turn = pl.program_id(0)
    turns = pl.num_programs(0) - 1

    @pl.when(turn == 0)
    def _():
        back_ext[Q : Q + 8, :] = jnp.zeros_like(back_ext[Q : Q + 8, :])
        sums[...] = jnp.zeros_like(sums)

    def body(count):
        k = subs - 1 - count
        group = (turns - 1 - turn) * subs + k
        cols = group_of(cols_in, k)
        start = pl.multiple_of(jnp.maximum(k * Q - 16, 0), 16)
        earlier = jnp.where(group == 0, halo[...], before[...])
        earlier = jnp.where(k == 0, earlier, raw[pl.ds(start, 16), :])
        ext[0:8, :] = earlier[8:16].astype(F32)
        ext[8 : 8 + Q, :] = group_of(raw, k)[...].astype(F32)
        pre = conv_before_act(ext, taps, cols)
        gate = sigmoid(pre)
        back = group_of(back_bc, k)[...] + group_of(back_more, k)[...]
        back_ext[0:Q, :] = back * (gate * (1.0 + pre * (1.0 - gate)))
        conv_back(turn, k, ext, back_ext, raw, before, halo, taps, cols, group_of(low_out, k), sums,
                  first_rows, last_rows, group)

    @pl.when(turn < turns)
    def _():
        loop(subs, body)

    @pl.when(turn == turns)
    def _():
        low_out[...] = jnp.zeros_like(low_out)
        low_out[0:16, :] = first_sent_back(scal, first_rows, taps).astype(BF16)


def joined(scal, low, later, last_rows, taps, rows):
    sent = []
    for back in range(3, 0, -1):
        at = scal[4] + rows - back
        extra = jnp.zeros_like(later[0])
        for j in range(back, 4):
            extra = extra + same_segment(scal, at, at + j) * taps[3 - j] * later[j - back]
        sent.append(extra)
    out = last_rows + jnp.concatenate([jnp.zeros((5, later.shape[1]), F32), jnp.stack(sent)])
    return lax.dynamic_update_slice(low, out.astype(BF16), (rows - 8, 0))


def split_blocks(member, count):
    return jnp.split(member, count, axis=0)


def chip_rows_kernel(tiles, scal, own, other, out):
    mine = pl.program_id(0) // tiles == scal[0]
    out[...] = jnp.where(mine, own[...], other[...])


def normed_rows_kernel(tiles, scal, own, other, halo, gain, out):
    def normed(member):
        wide = member.astype(F32)
        inverse = lax.rsqrt(jnp.mean(wide * wide, axis=1, keepdims=True) + EPS)
        return (wide * inverse * gain[...]).astype(BF16)

    step = pl.program_id(0)

    @pl.when(step < 2 * tiles)
    def _():
        out[...] = normed(jnp.where(step // tiles == scal[0], own[...], other[...]))

    @pl.when(step == 2 * tiles)
    def _():
        out[...] = jnp.zeros_like(out)
        out[0:16, :] = normed(halo[...])


def chip_rows(core, own, other, halo=None, gain=None):
    rows, width = own.shape
    tile = min(512, rows)
    tiles = rows // tile

    def at(first):
        return pl.BlockSpec((tile, width), lambda i, s: (jnp.clip(i - first(s) * tiles, 0, tiles - 1), 0))

    specs = [at(lambda s: s[0]), at(lambda s: 1 - s[0])]
    args = [core.reshape(1).astype(jnp.int32), own, other]
    body, extra = partial(chip_rows_kernel, tiles), 0
    if gain is not None:
        body, extra = partial(normed_rows_kernel, tiles), 1
        specs += [whole(halo.shape), whole((1, width))]
        args += [halo, gain.reshape(1, width)]
    return call(
        body,
        2 * tiles + extra,
        specs,
        [pl.BlockSpec((tile, width), lambda i, s: (i, 0))],
        [shape_of((2 * rows + extra * Q, width), BF16)],
        [],
        "chip_rows",
        rows * width * 8,
        tuple(args),
    )[0]


def many_dots_kernel(dims, scal, *refs):
    count = len(dims)
    out = refs[2 * count]
    total = dot(refs[0][...], refs[count][...], dims[0])
    for k in range(1, count):
        total = total + dot(refs[k][...], refs[count + k][...], dims[k])
    out[...] = total.astype(out.dtype)


def call(body, grid, in_specs, out_specs, out_shape, scratch, name, flops, args):
    moved = sum(a.size * a.dtype.itemsize for a in args) + sum(
        int(np.prod(o.shape)) * np.dtype(o.dtype).itemsize for o in out_shape
    )
    return pl.pallas_call(
        body,
        grid_spec=pltpu.PrefetchScalarGridSpec(
            num_scalar_prefetch=1,
            grid=(grid,),
            in_specs=in_specs,
            out_specs=out_specs,
            scratch_shapes=scratch,
        ),
        out_shape=out_shape,
        compiler_params=pltpu.CompilerParams(vmem_limit_bytes=VMEM_LIMIT),
        cost_estimate=pl.CostEstimate(flops=10**6, bytes_accessed=10**5, transcendentals=0),
        name=name,
    )(*args)


def whole(shape):
    return pl.BlockSpec(shape, lambda i, s: tuple(0 for _ in shape))


def after(member, *deps):
    return lax.optimization_barrier((member, *deps))[0]


class Order:
    def __init__(self):
        self.last = None

    def hold(self, member):
        return member if self.last is None else after(member, self.last)

    def holds(self, members):
        members = [self.hold(m) for m in members]
        self.last = after(self.last, *members)
        return members

    def done(self, member):
        self.last = member
        return member


def shape_of(shape, dtype):
    return jax.ShapeDtypeStruct(shape, dtype)


def many_dots(offset_rows, lefts, rights, dims, rows, dtype, name):
    tile = min(256, rows)
    columns = rights[0].shape[0 if dims[0] == NT else 1]
    scal = (offset_rows // tile).reshape(1).astype(jnp.int32)
    flops = 2 * rows * columns * sum(a.shape[1] for a in lefts)
    return call(
        partial(many_dots_kernel, tuple(dims)),
        rows // tile,
        [pl.BlockSpec((tile, a.shape[1]), lambda i, s: (s[0] + i, 0)) for a in lefts]
        + [whole(b.shape) for b in rights],
        [pl.BlockSpec((tile, columns), lambda i, s: (i, 0))],
        [shape_of((rows, columns), dtype)],
        [],
        name,
        flops,
        (scal, *lefts, *rights),
    )[0]


def solution(mesh):
    tensor = mesh.shape["tensor"]
    copies = mesh.shape["dp"]
    ny = tensor // 2
    nx = ny if copies % ny == 0 else 1
    nz = copies // nx

    def from_y(member, shift):
        pairs = [((((y + shift) % ny) * 2 + c), y * 2 + c) for y in range(ny) for c in range(2)]
        return lax.ppermute(member, "tensor", pairs)

    def next_y(member, step):
        pairs = [
            ((y - step) * 2 + c, y * 2 + c)
            for y in range(ny)
            for c in range(2)
            if 0 <= y - step < ny
        ]
        return lax.ppermute(member, "tensor", pairs)

    def from_core(member):
        return lax.ppermute(member, "tensor", [(t ^ 1, t) for t in range(tensor)])

    def from_x(member, shift):
        pairs = [(z * nx + (x + shift) % nx, z * nx + x) for z in range(nz) for x in range(nx)]
        return lax.ppermute(member, "dp", pairs)

    def from_z(member, shift):
        pairs = [(((z + shift) % nz) * nx + x, z * nx + x) for z in range(nz) for x in range(nx)]
        return lax.ppermute(member, "dp", pairs)

    def sum_rows(member):
        bit = 1
        while bit < copies:
            member = member + lax.ppermute(member, "dp", [(d ^ bit, d) for d in range(copies)])
            bit *= 2
        return member

    def sum_row_group(member):
        bit = 1
        while bit < tensor:
            member = member + lax.ppermute(member, "tensor", [(t ^ bit, t) for t in range(tensor)])
            bit *= 2
        return member

    def ways_x(member, x):
        kept = lax.dynamic_index_in_dim(member, x, 1, keepdims=False)
        got = []
        for k in range(1, nx):
            sent = lax.dynamic_index_in_dim(member, (x + k) % nx, 1, keepdims=False)
            got.append(from_x(sent.astype(BF16), nx - k))
        return [kept] + got

    def ways_z(member, z, bit):
        parts = member.reshape(-1, 2, *member.shape[-2:])
        own = (z // bit) % 2
        kept = lax.dynamic_index_in_dim(parts, own, 1, keepdims=False)
        sent = lax.dynamic_index_in_dim(parts, 1 - own, 1, keepdims=False)
        pairs = [((p ^ bit) * nx + x, p * nx + x) for p in range(nz) for x in range(nx)]
        return [kept, lax.ppermute(sent.astype(BF16), "dp", pairs)]

    def summed(parts):
        total = parts[0].astype(F32)
        for part in parts[1:]:
            total = total + part.astype(F32)
        return total

    def gather_rows(member, x, z):
        member = member[None]
        bit = nz // 2
        while bit >= 1:
            pairs = [((p ^ bit) * nx + q, p * nx + q) for p in range(nz) for q in range(nx)]
            other = lax.ppermute(member, "dp", pairs)
            high = (z // bit) % 2 == 1
            member = jnp.stack([jnp.where(high, other, member), jnp.where(high, member, other)], axis=1)
            member = member.reshape(-1, *member.shape[2:])
            bit //= 2
        parts = jnp.stack([member] + [from_x(member, k) for k in range(1, nx)])
        parts = [lax.dynamic_index_in_dim(parts, (k - x) % nx, 0, False) for k in range(nx)]
        return jnp.stack(parts, axis=1).reshape(-1, member.shape[-1])

    def shards(
        tokens, lengths, norm_gain, w_gate, w_value, w_shared, w_rate, conv_value, value_bias,
        conv_shared, shared_bias, rate_bias, decay_log, skip_gain, mix_gain, w_out, cotangent,
    ):
        index = lax.axis_index("tensor")
        y, core = index // 2, index % 2
        dp = lax.axis_index("dp")
        z, x = dp // nx, dp % nx
        own_rows, width = tokens.shape
        rows = 2 * own_rows
        groups = rows // Q
        channels = w_gate.shape[1]
        heads = w_rate.shape[1]
        inner = channels * tensor
        own_start = core * own_rows
        lanes = 128
        maps = w_shared.shape[1]
        blocks = range(ny)

        halo_one = next_y(tokens[own_rows - 16 :], 1)
        tokens_other = from_core(tokens)
        halo = jnp.where(core == 1, halo_one, from_core(halo_one))
        packed = jnp.concatenate(
            [
                conv_value.T,
                value_bias[None],
                mix_gain[None],
                jnp.repeat(skip_gain, HEAD)[None],
                jnp.concatenate([rate_bias, decay_log, jnp.zeros((channels - 2 * heads,), F32)])[None],
                w_rate.T.astype(F32).reshape(-1, channels),
            ],
            axis=0,
        )
        packed = after(packed, halo_one)
        packs = [packed] + [from_y(packed, j) for j in range(1, ny)]

        order = Order()

        def own_part(weight):
            part = weight.shape[0] // nx
            return lax.dynamic_slice(weight, (x * part, 0), (part, weight.shape[1]))

        def fetched(member, dep):
            member = after(member, dep)
            return [from_y(member, j) for j in range(1, ny)]

        def from_parts(weight, pieces):
            part = weight.shape[0] // nx
            found = [weight]
            for piece in pieces:
                full = lax.dynamic_update_slice(weight, piece, (x * part, 0))
                for k in range(1, nx):
                    got = from_x(piece, k)
                    full = lax.dynamic_update_slice(full, got, ((x + k) % nx * part, 0))
                found.append(full)
            return found

        back_other = from_core(after(cotangent, tokens_other))
        value_parts = fetched(own_part(w_value), packs[-1])
        rates = [p[8:].reshape(heads, width).astype(BF16) for p in packs]
        packs = [p[:8] for p in packs]
        all_rates = jnp.concatenate(rates + [jnp.zeros((lanes - ny * heads, width), BF16)], axis=0)
        w_small = jnp.concatenate([w_shared, all_rates.T], axis=1)
        fill = jnp.zeros((lanes - ny * heads,), F32)
        head_rows = jnp.concatenate(
            [
                jnp.concatenate([p[7, :heads] for p in packs] + [fill])[None],
                jnp.concatenate([-jnp.exp(p[7, heads : 2 * heads]) for p in packs] + [fill])[None],
                jnp.zeros((6, lanes), F32),
            ],
            axis=0,
        )
        shared_taps = jnp.concatenate(
            [conv_shared.T, shared_bias[None], jnp.zeros((3, maps), F32)], axis=0
        )
        scal = jnp.concatenate([lengths[0], (y * rows).reshape(1)]).astype(jnp.int32)

        residual = tokens.astype(F32)
        inverse_in = lax.rsqrt(jnp.mean(residual * residual, axis=1, keepdims=True) + EPS)
        normed = order.done(chip_rows(core, tokens, tokens_other, halo, norm_gain))
        step_rows = min(STEP_ROWS, rows)
        subs = step_rows // Q
        turns = rows // step_rows

        def up(columns):
            return pl.BlockSpec((step_rows, columns), lambda i, s: (i, 0))

        def up_lanes(depth):
            return pl.BlockSpec((depth, step_rows), lambda i, s: (0, i))

        def up_groups(*shape):
            return pl.BlockSpec((subs, *shape), lambda i, s: (i, 0, 0))

        def downward(i):
            return jnp.maximum(turns - 1 - i, 0)

        def down(columns):
            return pl.BlockSpec((step_rows, columns), lambda i, s: (downward(i), 0))

        def down_extended(columns):
            return pl.BlockSpec(
                (step_rows, columns), lambda i, s: (jnp.where(i == turns, turns, downward(i)), 0)
            )

        def down_lanes(depth):
            return pl.BlockSpec((depth, step_rows), lambda i, s: (0, downward(i)))

        def down_groups(*shape):
            return pl.BlockSpec((subs, *shape), lambda i, s: (downward(i), 0, 0))

        def down_before(columns):
            return pl.BlockSpec(
                (16, columns), lambda i, s: (jnp.maximum(downward(i) * (step_rows // 16) - 1, 0), 0)
            )

        def behind_rows(columns):
            return pl.BlockSpec((16, columns), lambda i, s: (rows // 16, 0))

        up_total = pl.BlockSpec((subs * 8, lanes), lambda i, s: (i, 0))
        down_total = pl.BlockSpec((subs * 8, lanes), lambda i, s: (downward(i), 0))
        row_depth = LOG + 8
        extended = rows + Q

        raw_values = [order.done(dot(order.hold(normed), w_value).astype(BF16))]
        small = order.done(dot(order.hold(normed), w_small))
        value_parts = order.holds(value_parts)
        values = from_parts(w_value, value_parts)
        gate_parts = fetched(own_part(w_gate), value_parts[-1])
        raw_shared = small[:, :maps].astype(BF16)
        bc, bct, cols, across, total = call(
            partial(prepare_kernel, subs),
            turns,
            [up(maps), up(lanes), behind_rows(maps), whole((8, maps)), whole((8, lanes))],
            [up(maps), up_lanes(maps), up(lanes), up_groups(row_depth, Q), up_total],
            [
                shape_of((rows, maps), BF16),
                shape_of((maps, rows), BF16),
                shape_of((rows, lanes), F32),
                shape_of((groups, row_depth, Q), F32),
                shape_of((groups * 8, lanes), F32),
            ],
            [pltpu.VMEM((Q + 8, maps), F32), pltpu.VMEM((8, lanes), F32)],
            "prepare",
            rows * 2000,
            (scal, raw_shared, small[:, maps:], raw_shared, shared_taps, head_rows),
        )
        order.done(total)

        flops_scan = rows * channels * 2 * 600
        acts, slopes, states, finals, throughs = [], [], [], [], []
        for j in blocks:
            if j == 1:
                gate_parts = order.holds(gate_parts)
                gates = from_parts(w_gate, gate_parts)
                out_parts = fetched(own_part(w_out), gate_parts[-1])
                values = [w_value] + [order.hold(v) for v in values[1:]]
            if j > 0:
                raw_values.append(order.done(dot(order.hold(normed), values[j]).astype(BF16)))
            if j == 1:
                raw_gates = [order.done(dot(order.hold(normed), w_gate).astype(BF16))]
            raw = raw_values[j]
            act, slope, state, final, through = call(
                partial(states_kernel, subs, j * heads),
                turns,
                [
                    up(channels),
                    behind_rows(channels),
                    whole((8, channels)),
                    up(lanes),
                    up_lanes(maps),
                    up_total,
                ],
                [
                    up(channels),
                    up(channels),
                    up_groups(STATE, channels),
                    whole((STATE, channels)),
                    whole((8, channels)),
                ],
                [
                    shape_of((rows, channels), BF16),
                    shape_of((rows, channels), BF16),
                    shape_of((groups, STATE, channels), BF16),
                    shape_of((STATE, channels), F32),
                    shape_of((8, channels), F32),
                ],
                [pltpu.VMEM((Q + 8, channels), F32), pltpu.VMEM((STATE, channels), F32)],
                "states",
                flops_scan // 2,
                (scal, order.hold(raw), raw, packs[j], cols, bct, total),
            )
            order.done(final)
            if j == 0:
                back_rows = order.done(chip_rows(core, cotangent, order.hold(back_other)))
            acts.append(act)
            slopes.append(slope)
            states.append(state)
            finals.append(final)
            throughs.append(through)

        before = [(j + 1) % ny for j in blocks]
        behind = [(j - 1) % ny for j in blocks]
        starts = split_blocks(next_y(jnp.concatenate([finals[k] for k in before]), 1), ny)
        for _ in range(ny - 2):
            sent = [finals[k] + throughs[k][0:1] * starts[k] for k in before]
            starts = split_blocks(next_y(jnp.concatenate(sent), 1), ny)

        out_parts = order.holds(out_parts)
        outs = from_parts(w_out, out_parts)
        backs = [order.done(dot(order.hold(back_rows), w_out, NT).astype(BF16))]
        scans, stats = [], []
        for j in blocks:
            if j == 1:
                gates = [w_gate] + [order.hold(w) for w in gates[1:]]
                outs = [w_out] + [order.hold(w) for w in outs[1:]]
            if j > 0:
                raw_gates.append(order.done(dot(order.hold(normed), gates[j]).astype(BF16)))
                backs.append(order.done(dot(order.hold(back_rows), outs[j], NT).astype(BF16)))
            raw_gate, back = raw_gates[j], backs[j]
            scanned, stat = call(
                partial(scan_kernel, subs, j * heads),
                turns,
                [
                    up(channels),
                    up(maps),
                    up(lanes),
                    up_groups(row_depth, Q),
                    up_total,
                    up(channels),
                    up(channels),
                    up_groups(STATE, channels),
                    whole((STATE, channels)),
                    whole((8, channels)),
                ],
                [up(channels), up_lanes(8)],
                [shape_of((rows, channels), F32), shape_of((8, rows), F32)],
                [],
                "scan",
                flops_scan,
                (scal, order.hold(acts[j]), bc, cols, across, total, raw_gate, back, states[j], starts[j],
                 packs[j]),
            )
            scans.append(order.done(scanned))
            stats.append(stat)

        stat = sum(stats[1:], stats[0])
        stat = stat + from_core(stat)

        mixeds, low_gates, back_heads, reaching, gate_sums = ([None] * ny for _ in range(5))
        for j in blocks:
            mixed, low_gate, back_head, reach, sums = call(
                partial(gate_back_kernel, subs, j * heads, inner),
                turns,
                [
                    up(channels),
                    up(channels),
                    up(channels),
                    up(channels),
                    up_lanes(8),
                    up_lanes(maps),
                    up(lanes),
                    up_total,
                    whole((8, channels)),
                ],
                [up(channels)] * 3 + [whole((STATE, channels)), whole((8, channels))],
                [shape_of((rows, channels), BF16)] * 3
                + [shape_of((STATE, channels), F32), shape_of((8, channels), F32)],
                [],
                "gate_back",
                flops_scan // 2,
                (scal, scans[j], order.hold(acts[j]), raw_gates[j], backs[j], stat, bct, cols, total, packs[j]),
            )
            mixeds[j], low_gates[j], back_heads[j] = mixed, low_gate, back_head
            reaching[j], gate_sums[j] = order.done(reach), sums

        leavings = [next_y(reaching[k], -1) for k in behind]
        for _ in range(ny - 2):
            leavings = [next_y(reaching[k] + throughs[k][0:1] * leavings[k], -1) for k in behind]

        def scattered(member):
            return member.reshape(nz, nx, width // copies, member.shape[1])

        out_blocks, gate_blocks = [None] * ny, [None] * ny
        for j in range(1, ny):
            out_blocks[j] = order.done(dot(order.hold(back_rows), mixeds[j], TN).astype(BF16))
            out_blocks[j] = after(out_blocks[j], leavings[-1])
        out_got = [from_y(out_blocks[j], ny - j) for j in range(1, ny)]
        for j in reversed(blocks):
            gate_blocks[j] = order.done(dot(order.hold(normed[:rows]), low_gates[j], TN).astype(BF16))
        gate_ways = [ways_x(scattered(b), x) for b in gate_blocks]
        out_blocks[0] = order.done(dot(order.hold(back_rows), mixeds[0], TN).astype(BF16))
        ahead = (1 - core) * own_rows

        channel = np.arange(channels)
        low_values, back_bcs, low_rates, conv_sums, head_sums_ = [None] * ny, [], [], [None] * ny, []
        value_blocks = [None] * ny
        for j in reversed(blocks):
            picks = jnp.asarray(
                (np.arange(lanes)[None, :] == (j * heads + channel // HEAD)[:, None]), BF16
            )
            low, back_bc, low_rate, sums, head_out, first_rows, last_rows = call(
                partial(scan_back_kernel, subs, j * heads),
                turns + 1,
                [
                    down(channels),
                    down(channels),
                    down(channels),
                    down(channels),
                    down(channels),
                    down_before(channels),
                    behind_rows(channels),
                    whole((8, channels)),
                    whole((channels, lanes)),
                    down(maps),
                    down_lanes(maps),
                    down(lanes),
                    down_groups(row_depth, Q),
                    down_total,
                    whole((8, lanes)),
                    down_groups(STATE, channels),
                    whole((STATE, channels)),
                    whole((STATE, channels)),
                ],
                [
                    down_extended(channels),
                    down(maps),
                    down_extended(lanes),
                    whole((8, channels)),
                    whole((8, lanes)),
                    whole((8, channels)),
                    whole((8, channels)),
                ],
                [
                    shape_of((extended, channels), BF16),
                    shape_of((rows, maps), F32),
                    shape_of((extended, lanes), BF16),
                    shape_of((8, channels), F32),
                    shape_of((8, lanes), F32),
                    shape_of((8, channels), F32),
                    shape_of((8, channels), F32),
                ],
                [
                    pltpu.VMEM((Q + 8, channels), F32),
                    pltpu.VMEM((Q + 8, channels), F32),
                    pltpu.VMEM((STATE, channels), F32),
                    pltpu.VMEM((Q, channels), F32),
                ],
                "scan_back",
                flops_scan * 3,
                (scal, order.hold(acts[j]), slopes[j], back_heads[j], scans[j], raw_values[j], raw_values[j],
                 raw_values[j], packs[j], picks, bc, bct, cols, across, total, head_rows, states[j],
                 starts[j], leavings[j]),
            )
            low_values[j] = (order.done(low), first_rows, last_rows)
            if j == ny - 1:
                gate_rows = [summed([w[0]] + order.holds(w[1:])) for w in gate_ways]
                gate_got = [from_y(gate_rows[k].astype(BF16), ny - k) for k in range(1, ny)]
                order.done(gate_rows[0])
            if j > 0:
                value_blocks[j] = order.done(dot(order.hold(normed), low, TN).astype(BF16))
            if j == 1:
                value_got = [from_y(value_blocks[k], ny - k) for k in range(1, ny)]
                out_sum = summed([out_blocks[0]] + order.holds(out_got))
                out_ways = ways_x(scattered(out_sum), x)
                order.done(out_sum)
                out_sent = order.done(
                    many_dots(
                        ahead, [order.hold(m) for m in mixeds], outs, [NN] * ny, own_rows, BF16, "out_other"
                    )
                )
                out_other = from_core(out_sent)
            back_bcs.append(back_bc)
            low_rates.append(low_rate)
            conv_sums[j] = sums
            head_sums_.append(head_out)

        later = [member[1] for member in low_values]
        later = next_y(jnp.concatenate([later[k] for k in behind], axis=1), -1)
        back_bc = sum(back_bcs[1:], back_bcs[0])
        back_bc_other = from_core(back_bc)
        out_sum = summed([out_ways[0]] + order.holds(out_ways[1:]))
        out_ways = ways_z(out_sum, z, 1)
        order.done(out_sum)
        out_kept = order.done(
            many_dots(
                own_start, [order.hold(m) for m in mixeds], outs, [NN] * ny, own_rows, F32, "out_own"
            )
        )

        back_bc = order.hold(back_bc)
        low_shared, shared_sums, first_rows, last_rows = call(
            partial(shared_back_kernel, subs),
            turns + 1,
            [
                down(maps),
                down(maps),
                down(maps),
                down_before(maps),
                behind_rows(maps),
                whole((8, maps)),
                down(lanes),
            ],
            [down_extended(maps), whole((8, maps)), whole((8, maps)), whole((8, maps))],
            [
                shape_of((extended, maps), BF16),
                shape_of((8, maps), F32),
                shape_of((8, maps), F32),
                shape_of((8, maps), F32),
            ],
            [pltpu.VMEM((Q + 8, maps), F32), pltpu.VMEM((Q + 8, maps), F32)],
            "shared_back",
            rows * 2000,
            (scal, back_bc, back_bc_other, raw_shared, raw_shared, raw_shared, shared_taps, cols),
        )
        order.done(low_shared)
        later_shared = next_y(first_rows, -1)
        low_rate = sum(low_rates[1:], low_rates[0])
        half = maps // 2
        cut = lax.dynamic_slice(low_shared, (0, core * half), (extended, half))
        small_block = jnp.concatenate([cut, low_rate], axis=1)
        value_got = order.holds(value_got)
        value_sum = order.done(summed([dot(order.hold(normed), low_values[0][0], TN)] + value_got))
        late_ways = ways_x(scattered(value_sum), x)
        gate_sum = summed([gate_rows[0]] + order.holds(gate_got))
        gate_ways = ways_z(gate_sum, z, 1)
        out_ways = out_ways[:1] + order.holds(out_ways[1:])
        bit = 2
        while bit < nz:
            out_ways = ways_z(summed(out_ways), z, bit)
            bit *= 2
        order.done(gate_sum)
        small_block = order.done(dot(order.hold(normed), small_block, TN).astype(BF16))
        small_got = [from_y(small_block, ny - j) for j in range(1, ny)]

        later = order.holds([later])[0]
        low_values = [
            joined(scal, m[0], later[:, j * channels : (j + 1) * channels], m[2], packs[j], rows)
            for j, m in enumerate(low_values)
        ]
        low_shared = joined(scal, low_shared, later_shared, last_rows, shared_taps, rows)

        lefts = [low_rate] + low_gates + low_values
        rights = [all_rates] + gates + values
        sent = order.done(
            many_dots(
                ahead, [order.hold(m) for m in lefts], rights, [NN] + [NT] * (2 * ny), own_rows, BF16,
                "back_other",
            )
        )
        back_normed_other = from_core(sent)
        small_sum = small_block[:, :half].astype(F32)
        rate_sum = small_block[:, half : half + heads].astype(F32)
        late = summed(late_ways[:1] + order.holds(late_ways[1:]))
        late_ways = ways_z(late, z, 1)
        for j, got in enumerate(order.holds(small_got)):
            got = got.astype(F32)
            at = half + (ny - 1 - j) * heads
            small_sum = small_sum + got[:, :half]
            rate_sum = rate_sum + got[:, at : at + heads]
        fill = jnp.zeros((width, lanes - heads), F32)
        least = scattered(jnp.concatenate([small_sum, rate_sum, fill], axis=1))
        least_ways = ways_x(least, x)
        gate_ways = gate_ways[:1] + order.holds(gate_ways[1:])
        bit = 2
        while bit < nz:
            gate_ways = ways_z(summed(gate_ways), z, bit)
            bit *= 2
        order.done(late)
        lefts = [order.hold(low_shared)] + lefts
        rights = [w_shared] + rights
        kept = order.done(
            many_dots(
                own_start, [order.hold(m) for m in lefts], rights, [NT, NN] + [NT] * (2 * ny), own_rows, F32,
                "back_own",
            )
        )
        late_ways = late_ways[:1] + order.holds(late_ways[1:])
        least = summed(least_ways[:1] + order.holds(least_ways[1:]))
        least_ways = ways_z(least, z, 1)
        bit = 2
        while bit < nz:
            late_ways = ways_z(summed(late_ways), z, bit)
            bit *= 2
        order.done(least)
        block_out = (residual + out_kept + out_other.astype(F32)).astype(BF16)
        back_normed = order.hold(kept) + back_normed_other.astype(F32)
        grad_norm = jnp.sum(back_normed * residual * inverse_in, axis=0)
        scaled = back_normed * norm_gain
        tokens_grad = (
            cotangent.astype(F32)
            + scaled * inverse_in
            - residual
            * (inverse_in * inverse_in * inverse_in)
            * jnp.sum(scaled * residual, axis=1, keepdims=True)
            / width
        )

        order.done(tokens_grad)

        bit = 2
        while bit < nz:
            least_ways = ways_z(summed(least_ways[:1] + order.holds(least_ways[1:])), z, bit)
            bit *= 2
        grad_out = summed(out_ways).reshape(width // copies, channels).T
        grad_gate = summed(gate_ways).reshape(width // copies, channels)
        grad_value = summed(late_ways).reshape(width // copies, channels)
        least = summed(least_ways).reshape(width // copies, half + lanes)
        grad_rate = least[:, half : half + heads]
        part = gather_rows(least[:, :half].astype(BF16), x, z)
        other = from_core(part)
        grad_shared = jnp.where(
            core == 0, jnp.concatenate([part, other], axis=1), jnp.concatenate([other, part], axis=1)
        ).astype(F32)

        head_out = sum(head_sums_[1:], head_sums_[0])
        smalls = []
        for j in blocks:
            skip = gate_sums[j][1].reshape(heads, HEAD).sum(axis=1)
            own_heads = head_out[:2, j * heads : (j + 1) * heads].reshape(2 * heads)
            line = jnp.concatenate([skip, own_heads, jnp.zeros((channels - 3 * heads,), F32)])
            smalls.append(
                jnp.concatenate(
                    [conv_sums[j][:5], gate_sums[j][:1], line[None], jnp.zeros((1, channels), F32)]
                )
            )
        shared_sums = jnp.where(core == 0, shared_sums, 0.0)
        alls = jnp.concatenate([shared_sums, grad_norm.reshape(-1, maps)], axis=0)
        alls = sum_row_group(alls)
        own = smalls[0]
        for j in range(1, ny):
            own = own + order.hold(from_y(smalls[j], ny - j))
        both = jnp.concatenate([own.reshape(-1, lanes), alls.reshape(-1, lanes)], axis=0)
        both = sum_rows(both)
        own = both[: own.size // lanes].reshape(own.shape)
        alls = both[own.size // lanes :].reshape(alls.shape)
        return (
            block_out,
            tokens_grad,
            alls[8:].reshape(width),
            grad_gate,
            grad_value,
            grad_shared,
            grad_rate,
            own[:4].T,
            own[4],
            alls[:4].T,
            alls[4],
            own[6, heads : 2 * heads],
            own[6, 2 * heads : 3 * heads],
            own[6, :heads],
            own[5],
            grad_out,
        )

    in_specs = (
        P(("dp", "tensor"), None),
        P("dp", None),
        P(),
        P(None, "tensor"),
        P(None, "tensor"),
        P(),
        P(None, "tensor"),
        P("tensor", None),
        P("tensor"),
        P(),
        P(),
        P("tensor"),
        P("tensor"),
        P("tensor"),
        P("tensor"),
        P("tensor", None),
        P(("dp", "tensor"), None),
    )
    out_specs = (
        P(("dp", "tensor"), None),
        P(("dp", "tensor"), None),
        P(),
        P("dp", "tensor"),
        P("dp", "tensor"),
        P(),
        P("dp", "tensor"),
        P("tensor", None),
        P("tensor"),
        P(),
        P(),
        P("tensor"),
        P("tensor"),
        P("tensor"),
        P("tensor"),
        P("tensor", "dp"),
    )
    return jax.shard_map(shards, mesh=mesh, in_specs=in_specs, out_specs=out_specs, check_vma=False)
```

time: 955 us -> 657 us (0.69)
  waiting for transfers between devices: 325 us -> 69.9 us
  starting transfers between devices: 80.7 us -> 54.6 us
  Pallas kernels: 301 us -> 277 us
  local copies, waits for them, and re-layouts: 48.1 us -> 61.8 us
  between operations: 22.3 us -> 9.26 us
    psum x1 -> x0, waiting for transfers between devices: 116 us -> none  [shards(): grad_shared = lax.psum(grad_shared, ('dp', 'tensor'))]
    ppermute x13 -> x9, waiting for transfers between devices: 115 us -> 27.2 us  [from_y(): return lax.ppermute(member, 'tensor', pairs)]
    ppermute x8 -> x6, waiting for transfers between devices: 42.5 us -> 3.6 us  [next_y(): return lax.ppermute(member, 'tensor', pairs)]
    pallas_call x14 -> x16, Pallas kernels: 301 us -> 277 us  [call(): pl.pallas_call(body, grid_spec=pltpu.PrefetchScalarGridSpec(num_scalar_pr...]
    ppermute x11 -> x12, waiting for transfers between devices: 29.9 us -> 17.1 us  [the longest x8 11.5 us: ways_z(): return [kept, lax.ppermute(sent.astype(BF16), 'dp', pairs)]]
    ppermute x13 -> x9, starting transfers between devices: 24.3 us -> 12.7 us  [from_y(): return lax.ppermute(member, 'tensor', pairs)]
    ppermute x9 -> x3, waiting for transfers between devices: 14.4 us -> 3.45 us  [sum_rows(): lax.ppermute(member, 'dp', [(d ^ bit, d) for d in range(copies)])]
    ppermute x9, waiting for transfers between devices: 8.16 us -> 18 us  [from_x(): return lax.ppermute(member, 'dp', pairs)]
  transfers between devices with their start and end apart: 57 -> 47, of which waited for: 22 -> 16; matrix products, arithmetic and copies ran while one was open for 20% -> 34% of each run, Pallas kernels for 27% -> 38%
where the time goes in v2:
time: 657 us; the launch traced here: 645 us
  Pallas kernels  277 us (42%)
  matrix products  104 us (16%)
  waiting for transfers between devices  69.9 us (11%)
  other arithmetic  68.4 us (10%)
  local copies, waits for them, and re-layouts  61.8 us (9%)
  starting transfers between devices  54.6 us (8%)
  between operations  9.26 us (1%)
    pallas_call x16, Pallas kernels, call(): pl.pallas_call(body, grid_spec=pltpu.PrefetchScalarGridSpec(num_scalar_pr...  277 us
    dot_general x14, matrix products, dot(): lax.dot_general(a, b, dims, precision=precision, preferred_element_type=F32)  104 us
    ppermute x9, waiting for transfers between devices, from_y(): return lax.ppermute(member, 'tensor', pairs)  27.2 us
    ppermute x9, waiting for transfers between devices, from_x(): return lax.ppermute(member, 'dp', pairs)  18 us
    add x10, other arithmetic, summed(): total = total + part.astype(F32)  16 us
  transfers between devices with their start and end apart: 47, of which 16 were waited for; matrix products, arithmetic and copies ran while one was open for 34% of the time, Pallas kernels for 38%

profile of v2, /device:TPU:0, one launch (start us, length us, event | category | flops | bytes accessed | tf_op | source)
XLA Modules:
  0.0 644.7 jit_solution(10269973359537449124)
XLA Ops:
  28.0 7.3 %chip_rows.2 = bf16[2176,1536]{1,0:T(8,128)(2,1)} custom-call(s32[1]{0:T(128)} %bitcast.3.scal, bf16[1024,1536]{1,0:T(8,128)(2,1)} %own.2, bf16[1024,1536]{1,0:T(8,128)(2,1)} %collective-permute-done.other, bf16[16,1536]{1,0:T(8,128)(2,1)} %broadcast_select_fusion.halo, f32[1,1536]{1,0:T(1,128)} %reshape.212.gain), custom_call_target="tpu_custom_call" | custom-call | flops 1000000 | bytes 100000 | tf_op jit(solution)/shard_map/chip_rows/pallas_call | solution.py:607
  35.4 9.9 %convolution_convert_fusion.3.raw.halo.before = bf16[2176,768]{1,0:T(8,128)(2,1)} fusion(bf16[2176,1536]{1,0:T(8,128)(2,1)} %chip_rows.2, bf16[1536,768]{1,0:T(8,128)(2,1)S(1)} %copy-done.1), kind=kOutput, calls=%fused_computation.18 | convolution fusion | flops 5135499264 | bytes 12386304 | tf_op jit(solution)/shard_map/dot_general | solution.py:29
  48.9 6.6 %collective-permute-done.5 = bf16[768,768]{1,0:T(8,128)(2,1)S(1)} collective-permute-done((bf16[768,768]{1,0:T(8,128)(2,1)}, bf16[768,768]{1,0:T(8,128)(2,1)S(1)}, u32[]{:S(2)}, u32[]{:S(2)}) %collective-permute-start.5) | collective-permute-done | bytes 1179680 | tf_op jit(solution)/shard_map/ppermute | solution.py:680
  65.5 14.4 %prepare.1 = (bf16[2048,256]{1,0:T(8,128)(2,1)}, bf16[256,2048]{1,0:T(8,128)(2,1)}, f32[2048,128]{1,0:T(8,128)}, f32[16,40,128]{2,1,0:T(8,128)}, f32[128,128]{1,0:T(8,128)}) custom-call(s32[5]{0:T(128)} %pad_add_fusion.scal, bf16[2176,256]{1,0:T(8,128)(2,1)} %slice.546.shared.halo.raw.before, f32[2176,128]{1,0:T(8,128)} %slice.219.rates, ...), custom_call_target="tpu_custom_call" | custom-call | flops 1000000 | bytes 100000 | tf_op jit(solution)/shard_map/prepare/pallas_call | solution.py:607
  79.9 18.1 %states.2 = (bf16[2048,768]{1,0:T(8,128)(2,1)}, bf16[2048,768]{1,0:T(8,128)(2,1)}, bf16[16,128,768]{2,1,0:T(8,128)(2,1)}, f32[128,768]{1,0:T(8,128)}, f32[8,768]{1,0:T(8,128)}) custom-call(s32[5]{0:T(128)} %pad_add_fusion.scal, bf16[2176,768]{1,0:T(8,128)(2,1)} %convolution_convert_fusion.3.raw.halo.before, ...), custom_call_target="tpu_custom_call" | custom-call | flops 1000000 | bytes 100000 | tf_op jit(solution)/shard_map/states/pallas_call | solution.py:607
  98.3 7.7 %chip_rows.3 = bf16[2048,1536]{1,0:T(8,128)(2,1)} custom-call(s32[1]{0:T(128)} %bitcast.3.scal, bf16[1024,1536]{1,0:T(8,128)(2,1)} %own.3, bf16[1024,1536]{1,0:T(8,128)(2,1)} %collective-permute-done.4.other), custom_call_target="tpu_custom_call" | custom-call | flops 1000000 | bytes 100000 | tf_op jit(solution)/shard_map/chip_rows/pallas_call | solution.py:607
  108.0 9.7 %convolution_convert_fusion.2.raw.halo.before = bf16[2176,768]{1,0:T(8,128)(2,1)} fusion(bf16[2176,1536]{1,0:T(8,128)(2,1)} %chip_rows.2, bf16[1536,768]{1,0:T(8,128)(2,1)S(1)} %constant_dynamic-update-slice_fusion.5.refs_9_.refs_11_), kind=kOutput, calls=%fused_computation.17 | convolution fusion | flops 5135499264 | bytes 12386304 | tf_op jit(solution)/shard_map/dot_general | solution.py:29
  117.7 9.7 %convolution_convert_fusion.1.gate_in = bf16[2176,768]{1,0:T(8,128)(2,1)} fusion(bf16[2176,1536]{1,0:T(8,128)(2,1)} %chip_rows.2, bf16[1536,768]{1,0:T(8,128)(2,1)S(1)} %copy-done.2), kind=kOutput, calls=%fused_computation.16 | convolution fusion | flops 5135499264 | bytes 12386304 | tf_op jit(solution)/shard_map/dot_general | solution.py:29
  127.4 18.1 %states.3 = (bf16[2048,768]{1,0:T(8,128)(2,1)}, bf16[2048,768]{1,0:T(8,128)(2,1)}, bf16[16,128,768]{2,1,0:T(8,128)(2,1)}, f32[128,768]{1,0:T(8,128)}, f32[8,768]{1,0:T(8,128)}) custom-call(s32[5]{0:T(128)} %pad_add_fusion.scal, bf16[2176,768]{1,0:T(8,128)(2,1)} %convolution_convert_fusion.2.raw.halo.before, ...), custom_call_target="tpu_custom_call" | custom-call | flops 1000000 | bytes 100000 | tf_op jit(solution)/shard_map/states/pallas_call | solution.py:607
  149.2 9.8 %convolution_convert_fusion.10.back_in = bf16[2048,768]{1,0:T(8,128)(2,1)} fusion(bf16[2048,1536]{1,0:T(8,128)(2,1)} %chip_rows.3, bf16[768,1536]{1,0:T(8,128)(2,1)S(1)} %copy-done.4), kind=kOutput, calls=%fused_computation.27 | convolution fusion | flops 4833411072 | bytes 11796480 | tf_op jit(solution)/shard_map/dot_general | solution.py:29
  164.9 19.4 %scan.2 = (f32[2048,768]{1,0:T(8,128)}, f32[8,2048]{1,0:T(8,128)}) custom-call(s32[5]{0:T(128)} %pad_add_fusion.scal, bf16[2048,768]{1,0:T(8,128)(2,1)} %get-tuple-element.183.act_in, bf16[2048,256]{1,0:T(8,128)(2,1)} %get-tuple-element.135.bc_in, f32[2048,128]{1,0:T(8,128)} %get-tuple-element.128.cols_in, f32[16,40,128]{2,1,0:T(8,128)} %get-tuple-element.136.rows_in, ...), custom_call_target="tpu_custom_call" | custom-call | flops 1000000 | bytes 100000 | tf_op jit(solution)/shard_map/scan/pallas_call | solution.py:607
  188.4 8.6 %convolution_convert_fusion.gate_in = bf16[2176,768]{1,0:T(8,128)(2,1)} fusion(bf16[2176,1536]{1,0:T(8,128)(2,1)S(1)} %bitcast.169, bf16[1536,768]{1,0:T(8,128)(2,1)} %constant_dynamic-update-slice_fusion.3.refs_7_.refs_9_), kind=kOutput, calls=%fused_computation.15 | convolution fusion | flops 5135499264 | bytes 12386304 | tf_op jit(solution)/shard_map/dot_general | solution.py:29
  198.3 11.0 %collective-permute-done.11 = bf16[384,1536]{1,0:T(8,128)(2,1)S(1)} collective-permute-done((bf16[384,1536]{1,0:T(8,128)(2,1)}, bf16[384,1536]{1,0:T(8,128)(2,1)S(1)}, u32[]{:S(2)}, u32[]{:S(2)}) %collective-permute-start.11) | collective-permute-done | bytes 1179680 | tf_op jit(solution)/shard_map/ppermute | solution.py:696
  209.5 6.5 %convolution_convert_fusion.9.back_in = bf16[2048,768]{1,0:T(8,128)(2,1)} fusion(bf16[2048,1536]{1,0:T(8,128)(2,1)S(1)} %bitcast.185, bf16[768,1536]{1,0:T(8,128)(2,1)S(1)} %constant_dynamic-update-slice_fusion.1.refs_3_), kind=kOutput, calls=%fused_computation.26 | convolution fusion | flops 4833411072 | bytes 11796480 | tf_op jit(solution)/shard_map/dot_general | solution.py:29
  216.0 19.2 %scan.3 = (f32[2048,768]{1,0:T(8,128)}, f32[8,2048]{1,0:T(8,128)}) custom-call(s32[5]{0:T(128)} %pad_add_fusion.scal, bf16[2048,768]{1,0:T(8,128)(2,1)} %get-tuple-element.174.act_in, bf16[2048,256]{1,0:T(8,128)(2,1)} %get-tuple-element.135.bc_in, f32[2048,128]{1,0:T(8,128)} %get-tuple-element.128.cols_in, f32[16,40,128]{2,1,0:T(8,128)} %get-tuple-element.136.rows_in, ...), custom_call_target="tpu_custom_call" | custom-call | flops 1000000 | bytes 100000 | tf_op jit(solution)/shard_map/scan/pallas_call | solution.py:607
  245.1 5.9 slice.443
  251.6 16.1 %gate_back.2 = (bf16[2048,768]{1,0:T(8,128)(2,1)}, bf16[2048,768]{1,0:T(8,128)(2,1)}, bf16[2048,768]{1,0:T(8,128)(2,1)}, f32[128,768]{1,0:T(8,128)}, f32[8,768]{1,0:T(8,128)}) custom-call(s32[5]{0:T(128)} %pad_add_fusion.scal, f32[2048,768]{1,0:T(8,128)} %get-tuple-element.148.scanned_in, bf16[2048,768]{1,0:T(8,128)(2,1)} %get-tuple-element.183.act_in, ...), custom_call_target="tpu_custom_call" | custom-call | flops 1000000 | bytes 100000 | tf_op jit(solution)/shard_map/gate_back/pallas_call | solution.py:607
  269.4 16.6 %gate_back.3 = (bf16[2048,768]{1,0:T(8,128)(2,1)}, bf16[2048,768]{1,0:T(8,128)(2,1)}, bf16[2048,768]{1,0:T(8,128)(2,1)}, f32[128,768]{1,0:T(8,128)}, f32[8,768]{1,0:T(8,128)}) custom-call(s32[5]{0:T(128)} %pad_add_fusion.scal, f32[2048,768]{1,0:T(8,128)} %get-tuple-element.158.scanned_in, bf16[2048,768]{1,0:T(8,128)(2,1)} %get-tuple-element.174.act_in, ...), custom_call_target="tpu_custom_call" | custom-call | flops 1000000 | bytes 100000 | tf_op jit(solution)/shard_map/gate_back/pallas_call | solution.py:607
  286.0 8.5 %convolution_convert_fusion.8 = bf16[1536,768]{1,0:T(8,128)(2,1)} fusion(bf16[2048,1536]{1,0:T(8,128)(2,1)S(1)} %bitcast.187, bf16[2048,768]{1,0:T(8,128)(2,1)} %get-tuple-element.189.refs_1_), kind=kOutput, calls=%fused_computation.25 | convolution fusion | flops 4833017856 | bytes 11796480 | tf_op jit(solution)/shard_map/dot_general | solution.py:29
  308.2 7.0 %convolution_convert_fusion.5 = bf16[1536,768]{1,0:T(8,128)(2,1)} fusion(bf16[2048,1536]{1,0:T(8,128)(2,1)S(1)} %bitcast.189, bf16[2048,768]{1,0:T(8,128)(2,1)S(1)} %copy-done.14), kind=kOutput, calls=%fused_computation.22 | convolution fusion | flops 4833017856 | bytes 11796480 | tf_op jit(solution)/shard_map/dot_general | solution.py:29
  319.5 38.0 %scan_back.2 = (bf16[2176,768]{1,0:T(8,128)(2,1)}, f32[2048,256]{1,0:T(8,128)}, bf16[2176,128]{1,0:T(8,128)(2,1)}, f32[8,768]{1,0:T(8,128)}, f32[8,128]{1,0:T(8,...) custom-call(s32[5]{0:T(128)} %pad_add_fusion.scal, bf16[2048,768]{1,0:T(8,128)(2,1)} %get-tuple-element.174.act_in, ...), custom_call_target="tpu_custom_call" | custom-call | flops 1000000 | bytes 100000 | tf_op jit(solution)/shard_map/scan_back/pallas_call | solution.py:607
  360.7 7.1 %convolution_convert_fusion.4 = bf16[1536,768]{1,0:T(8,128)(2,1)} fusion(bf16[2176,1536]{1,0:T(8,128)(2,1)S(1)} %bitcast.171, bf16[2176,768]{1,0:T(8,128)(2,1)S(1)} %copy-done.13), kind=kOutput, calls=%fused_computation.21 | convolution fusion | flops 5135007744 | bytes 12386304 | tf_op jit(solution)/shard_map/dot_general | solution.py:29
  387.7 9.5 %out_other.1 = bf16[1024,1536]{1,0:T(8,128)(2,1)} custom-call(s32[1]{0:T(128)} %bitcast.21.scal, bf16[2048,768]{1,0:T(8,128)(2,1)} %get-tuple-element.188.refs_0_, bf16[2048,768]{1,0:T(8,128)(2,1)} %get-tuple-element.189.refs_1_, bf16[768,1536]{1,0:T(8,128)(2,1)} %refs_2_.3, bf16[768,1536]{1,0:T(8,128)(2,1)} %copy-done.11), custom_call_target="tpu_custom_call" | custom-call | flops 1000000 | bytes 100000 | tf_op jit(solution)/shard_map/out_other/pallas_call | solution.py:607
  397.9 38.0 %scan_back.3 = (bf16[2176,768]{1,0:T(8,128)(2,1)}, f32[2048,256]{1,0:T(8,128)}, bf16[2176,128]{1,0:T(8,128)(2,1)}, f32[8,768]{1,0:T(8,128)}, f32[8,128]{1,0:T(8,...) custom-call(s32[5]{0:T(128)} %pad_add_fusion.scal, bf16[2048,768]{1,0:T(8,128)(2,1)} %get-tuple-element.183.act_in, ...), custom_call_target="tpu_custom_call" | custom-call | flops 1000000 | bytes 100000 | tf_op jit(solution)/shard_map/scan_back/pallas_call | solution.py:607
  450.0 14.2 %collective-permute-done.29 = f32[8,768]{1,0:T(8,128)S(1)} collective-permute-done((f32[8,768]{1,0:T(8,128)S(1)}, f32[8,768]{1,0:T(8,128)S(1)}, u32[]{:S(2)}, u32[]{:S(2)}) %collective-permute-start.29) | collective-permute-done | bytes 24608 | tf_op jit(solution)/shard_map/ppermute | solution.py:680
  470.2 9.8 %out_own.1 = f32[1024,1536]{1,0:T(8,128)} custom-call(s32[1]{0:T(128)} %bitcast.scal, bf16[2048,768]{1,0:T(8,128)(2,1)} %get-tuple-element.188.refs_0_, bf16[2048,768]{1,0:T(8,128)(2,1)} %get-tuple-element.189.refs_1_, bf16[768,1536]{1,0:T(8,128)(2,1)} %refs_2_.3, bf16[768,1536]{1,0:T(8,128)(2,1)} %copy-done.11), custom_call_target="tpu_custom_call" | custom-call | flops 1000000 | bytes 100000 | tf_op jit(solution)/shard_map/out_own/pallas_call | solution.py:607
  487.0 9.8 %shared_back.1 = (bf16[2176,256]{1,0:T(8,128)(2,1)}, f32[8,256]{1,0:T(8,128)}, f32[8,256]{1,0:T(8,128)}, f32[8,256]{1,0:T(8,128)}) custom-call(s32[5]{0:T(128)} %pad_add_fusion.scal, f32[2048,256]{1,0:T(8,128)} %add.303.back_bc, f32[2048,256]{1,0:T(8,128)} %collective-permute-done.19.back_more, bf16[2176,256]{1,0:T(8,128)(2,1)} %slice.546.shared.halo.raw.before, ...), custom_call_target="tpu_custom_call" | custom-call | flops 1000000 | bytes 100000 | tf_op jit(solution)/shard_map/shared_back/pallas_call | solution.py:607
  498.3 9.5 %convert_add_fusion.2 = f32[1536,768]{1,0:T(8,128)S(1)} fusion(bf16[1536,768]{1,0:T(8,128)(2,1)} %collective-permute-done.21, bf16[2176,1536]{1,0:T(8,128)(2,1)} %chip_rows.2, bf16[2176,768]{1,0:T(8,128)(2,1)} %get-tuple-element.186), kind=kOutput, calls=%fused_computation.19 | convolution fusion | flops 5136187392 | bytes 17104896 | tf_op jit(solution)/shard_map/dot_general | solution.py:29
  522.5 17.1 %back_other.1 = bf16[1024,1536]{1,0:T(8,128)(2,1)} custom-call(s32[1]{0:T(128)} %bitcast.21.scal, bf16[2176,128]{1,0:T(8,128)(2,1)} %add.644.refs_0_.refs_1_, bf16[2048,768]{1,0:T(8,128)(2,1)} %get-tuple-element.216.refs_1_.refs_2_, bf16[2048,768]{1,0:T(8,128)(2,1)} %get-tuple-element.217.refs_2_.refs_3_, ...), custom_call_target="tpu_custom_call" | custom-call | flops 1000000 | bytes 100000 | tf_op jit(solution)/shard_map/back_other/pallas_call | solution.py:607
  564.4 18.2 %back_own.1 = f32[1024,1536]{1,0:T(8,128)} custom-call(s32[1]{0:T(128)} %bitcast.scal, bf16[2176,256]{1,0:T(8,128)(2,1)} %constant_dynamic-update-slice_fusion.refs_0_, bf16[2176,128]{1,0:T(8,128)(2,1)} %add.644.refs_0_.refs_1_, bf16[2048,768]{1,0:T(8,128)(2,1)} %get-tuple-element.216.refs_1_.refs_2_, bf16[2048,768]{1,0:T(8,128)(2,1)} %get-tuple-element.217.refs_2_.refs_3_, ...), custom_call_target="tpu_custom_call" | custom-call | flops 1000000 | bytes 100000 | tf_op jit(solution)/shard_map/back_own/pallas_call | solution.py:607
  584.9 5.9 fusion.8
  591.5 12.6 %fusion.5 = (f32[1024,1536]{1,0:T(8,128)}, bf16[1024,1536]{1,0:T(8,128)(2,1)}) fusion(bf16[1024,1536]{1,0:T(8,128)(2,1)S(1)} %copy-done, bf16[1024,1536]{1,0:T(8,128)(2,1)} %own.3, f32[1024]{0:T(1024)} %get-tuple-element.247, f32[1024]{0:T(1024)} %get-tuple-element.286, f32[1024]{0:T(1024)} %copy-done.47, f32[1536]{0:T(1024)} %param.21, ...), kind=kLoop, calls=%fused_computation.10 | loop fusion | flops 23592960 | bytes 34621440 | tf_op jit(solution)/shard_map/sub | solution.py:1241
  (427 shorter events, 216.0 us)
Async XLA Ops:
  0.7 27.4 %collective-permute-start = (bf16[1024,1536]{1,0:T(8,128)(2,1)}, bf16[1024,1536]{1,0:T(8,128)(2,1)}, u32[]{:S(2)}, u32[]{:S(2)}) collective-permute-start(bf16[1024,1536]{1,0:T(8,128)(2,1)} %own.2), channel_id=1, source_target_pairs={{1,0},{0,1},{3,2},{2,3},{5,4},{4,5},{7,6},{6,7},{9,8},{8,9},{11,10... | collective-permute-start | bytes 9437192 | tf_op jit(solution)/shard_map/ppermute | solution.py:692
  27.8 27.7 %collective-permute-start.5 = (bf16[768,768]{1,0:T(8,128)(2,1)}, bf16[768,768]{1,0:T(8,128)(2,1)S(1)}, u32[]{:S(2)}, u32[]{:S(2)}) collective-permute-start(bf16[768,768]{1,0:T(8,128)(2,1)} %constant_dynamic-slice_fusion.2), channel_id=1, source_target_pairs={{2,0},{3,1},{0,2},{1,3},{6,4},{7,5},{4,6},{5,7},{10,8},{11,9},{8,1... | collective-permute-start | bytes 3538952 | tf_op jit(solution)/shard_map/ppermute | solution.py:680
  28.0 70.2 %collective-permute-start.4 = (bf16[1024,1536]{1,0:T(8,128)(2,1)}, bf16[1024,1536]{1,0:T(8,128)(2,1)}, u32[]{:S(2)}, u32[]{:S(2)}) collective-permute-start(bf16[1024,1536]{1,0:T(8,128)(2,1)} %own.3), channel_id=1, source_target_pairs={{1,0},{0,1},{3,2},{2,3},{5,4},{4,5},{7,6},{6,7},{9,8},{8,9},{11,10... | collective-permute-start | bytes 9437192 | tf_op jit(solution)/shard_map/ppermute | solution.py:692
  55.5 42.6 %collective-permute-start.7 = (bf16[768,768]{1,0:T(8,128)(2,1)S(1)}, bf16[768,768]{1,0:T(8,128)(2,1)S(1)}, u32[]{:S(2)}, u32[]{:S(2)}) collective-permute-start(bf16[768,768]{1,0:T(8,128)(2,1)S(1)} %collective-permute-done.5), channel_id=1, source_target_pairs={{4,0},{0,4},{12,8},{8,12},{20,16},{16,20},{28,24},{24,28},{5,1},{1... | collective-permute-start | bytes 3538952 | tf_op jit(solution)/shard_map/ppermute | solution.py:696
  57.1 48.9 %collective-permute-start.6 = (bf16[768,768]{1,0:T(8,128)(2,1)S(1)}, bf16[768,768]{1,0:T(8,128)(2,1)}, u32[]{:S(2)}, u32[]{:S(2)}) collective-permute-start(bf16[768,768]{1,0:T(8,128)(2,1)S(1)} %constant_dynamic-slice_fusion.3), channel_id=1, source_target_pairs={{2,0},{3,1},{0,2},{1,3},{6,4},{7,5},{4,6},{5,7},{10,8},{11,9},{8,1... | collective-permute-start | bytes 3538952 | tf_op jit(solution)/shard_map/ppermute | solution.py:680
  106.0 79.8 %collective-permute-start.9 = (bf16[768,768]{1,0:T(8,128)(2,1)}, bf16[768,768]{1,0:T(8,128)(2,1)}, u32[]{:S(2)}, u32[]{:S(2)}) collective-permute-start(bf16[768,768]{1,0:T(8,128)(2,1)} %collective-permute-done.6), channel_id=1, source_target_pairs={{4,0},{0,4},{12,8},{8,12},{20,16},{16,20},{28,24},{24,28},{5,1},{1... | collective-permute-start | bytes 3538952 | tf_op jit(solution)/shard_map/ppermute | solution.py:696
  106.5 77.7 %collective-permute-start.10 = (bf16[384,1536]{1,0:T(8,128)(2,1)S(1)}, bf16[384,1536]{1,0:T(8,128)(2,1)}, u32[]{:S(2)}, u32[]{:S(2)}) collective-permute-start(bf16[384,1536]{1,0:T(8,128)(2,1)S(1)} %copy-done.35), channel_id=1, source_target_pairs={{2,0},{3,1},{0,2},{1,3},{6,4},{7,5},{4,6},{5,7},{10,8},{11,9},{8,1... | collective-permute-start | bytes 3538952 | tf_op jit(solution)/shard_map/ppermute | solution.py:680
  146.6 17.4 %collective-permute-start.8 = (f32[256,768]{1,0:T(8,128)S(1)}, f32[256,768]{1,0:T(8,128)S(1)}, u32[]{:S(2)}, u32[]{:S(2)}) collective-permute-start(f32[256,768]{1,0:T(8,128)S(1)} %pad_maximum_fusion), channel_id=1, source_target_pairs={{0,2},{1,3},{4,6},{5,7},{8,10},{9,11},{12,14},{13,15},{16,18},{17,... | collective-permute-start | bytes 2359304 | tf_op jit(solution)/shard_map/ppermute | solution.py:689
  184.3 25.1 %collective-permute-start.11 = (bf16[384,1536]{1,0:T(8,128)(2,1)}, bf16[384,1536]{1,0:T(8,128)(2,1)S(1)}, u32[]{:S(2)}, u32[]{:S(2)}) collective-permute-start(bf16[384,1536]{1,0:T(8,128)(2,1)} %collective-permute-done.10), channel_id=1, source_target_pairs={{4,0},{0,4},{12,8},{8,12},{20,16},{16,20},{28,24},{24,28},{5,1},{1... | collective-permute-start | bytes 3538952 | tf_op jit(solution)/shard_map/ppermute | solution.py:696
  267.8 47.3 %collective-permute-start.13 = (f32[128,768]{1,0:T(8,128)}, f32[128,768]{1,0:T(8,128)S(1)}, u32[]{:S(2)}, u32[]{:S(2)}) collective-permute-start(f32[128,768]{1,0:T(8,128)} %get-tuple-element.163), channel_id=1, source_target_pairs={{2,0},{3,1},{6,4},{7,5},{10,8},{11,9},{14,12},{15,13},{18,16},{19,... | collective-permute-start | bytes 1179656 | tf_op jit(solution)/shard_map/ppermute | solution.py:689
  306.7 50.9 %collective-permute-start.15 = (bf16[4,192,768]{2,1,0:T(8,128)(2,1)}, bf16[4,192,768]{2,1,0:T(8,128)(2,1)S(1)}, u32[]{:S(2)}, u32[]{:S(2)}) collective-permute-start(bf16[4,192,768]{2,1,0:T(8,128)(2,1)} %dynamic-slice_bitcast_fusion.1), channel_id=1, source_target_pairs={{4,0},{0,4},{12,8},{8,12},{20,16},{16,20},{28,24},{24,28},{5,1},{1... | collective-permute-start | bytes 3538952 | tf_op jit(solution)/shard_map/ppermute | solution.py:696
  315.2 54.5 %collective-permute-start.14 = (bf16[1536,768]{1,0:T(8,128)(2,1)}, bf16[1536,768]{1,0:T(8,128)(2,1)}, u32[]{:S(2)}, u32[]{:S(2)}) collective-permute-start(bf16[1536,768]{1,0:T(8,128)(2,1)} %convolution_convert_fusion.8), channel_id=1, source_target_pairs={{2,0},{3,1},{0,2},{1,3},{6,4},{7,5},{4,6},{5,7},{10,8},{11,9},{8,1... | collective-permute-start | bytes 7077896 | tf_op jit(solution)/shard_map/ppermute | solution.py:680
  319.0 65.7 %collective-permute-start.23 = (bf16[4,192,768]{2,1,0:T(8,128)(2,1)}, bf16[4,192,768]{2,1,0:T(8,128)(2,1)}, u32[]{:S(2)}, u32[]{:S(2)}) collective-permute-start(bf16[4,192,768]{2,1,0:T(8,128)(2,1)} %dynamic-slice_bitcast_fusion), channel_id=1, source_target_pairs={{4,0},{0,4},{12,8},{8,12},{20,16},{16,20},{28,24},{24,28},{5,1},{1... | collective-permute-start | bytes 3538952 | tf_op jit(solution)/shard_map/ppermute | solution.py:696
  373.3 66.5 %collective-permute-start.16 = (bf16[4,192,768]{2,1,0:T(8,128)(2,1)}, bf16[4,192,768]{2,1,0:T(8,128)(2,1)}, u32[]{:S(2)}, u32[]{:S(2)}) collective-permute-start(bf16[4,192,768]{2,1,0:T(8,128)(2,1)} %fusion.10), channel_id=1, source_target_pairs={{4,0},{0,4},{12,8},{8,12},{20,16},{16,20},{28,24},{24,28},{5,1},{1... | collective-permute-start | bytes 3538952 | tf_op jit(solution)/shard_map/ppermute | solution.py:696
  375.2 22.0 %collective-permute-start.17 = (f32[128,768]{1,0:T(8,128)}, f32[128,768]{1,0:T(8,128)S(1)}, u32[]{:S(2)}, u32[]{:S(2)}) collective-permute-start(f32[128,768]{1,0:T(8,128)} %get-tuple-element.165), channel_id=1, source_target_pairs={{2,0},{3,1},{6,4},{7,5},{10,8},{11,9},{14,12},{15,13},{18,16},{19,... | collective-permute-start | bytes 1179656 | tf_op jit(solution)/shard_map/ppermute | solution.py:689
  382.1 114.6 %collective-permute-start.21 = (bf16[1536,768]{1,0:T(8,128)(2,1)}, bf16[1536,768]{1,0:T(8,128)(2,1)}, u32[]{:S(2)}, u32[]{:S(2)}) collective-permute-start(bf16[1536,768]{1,0:T(8,128)(2,1)} %convolution_convert_fusion.4), channel_id=1, source_target_pairs={{2,0},{3,1},{0,2},{1,3},{6,4},{7,5},{4,6},{5,7},{10,8},{11,9},{8,1... | collective-permute-start | bytes 7077896 | tf_op jit(solution)/shard_map/ppermute | solution.py:680
  387.7 121.7 %collective-permute-start.24 = (bf16[4,192,768]{2,1,0:T(8,128)(2,1)}, bf16[4,192,768]{2,1,0:T(8,128)(2,1)}, u32[]{:S(2)}, u32[]{:S(2)}) collective-permute-start(bf16[4,192,768]{2,1,0:T(8,128)(2,1)} %fusion.9), channel_id=1, source_target_pairs={{2,0},{3,1},{0,2},{1,3},{6,4},{7,5},{4,6},{5,7},{10,8},{11,9},{8,1... | collective-permute-start | bytes 3538952 | tf_op jit(solution)/shard_map/ppermute | solution.py:680
  439.8 47.2 %collective-permute-start.19 = (f32[2048,256]{1,0:T(8,128)}, f32[2048,256]{1,0:T(8,128)}, u32[]{:S(2)}, u32[]{:S(2)}) collective-permute-start(f32[2048,256]{1,0:T(8,128)} %add.303.back_bc), channel_id=1, source_target_pairs={{1,0},{0,1},{3,2},{2,3},{5,4},{4,5},{7,6},{6,7},{9,8},{8,9},{11,10... | collective-permute-start | bytes 6291464 | tf_op jit(solution)/shard_map/ppermute | solution.py:692
  443.7 20.5 %collective-permute-start.45 = (bf16[2,192,768]{2,1,0:T(8,128)(2,1)}, bf16[2,192,768]{2,1,0:T(8,128)(2,1)}, u32[]{:S(2)}, u32[]{:S(2)}) collective-permute-start(bf16[2,192,768]{2,1,0:T(8,128)(2,1)} %fusion.22), channel_id=1, source_target_pairs={{8,0},{12,4},{0,8},{4,12},{24,16},{28,20},{16,24},{20,28},{9,1},{1... | collective-permute-start | bytes 1769480 | tf_op jit(solution)/shard_map/ppermute | solution.py:730
  445.7 18.5 %collective-permute-start.29 = (f32[8,768]{1,0:T(8,128)S(1)}, f32[8,768]{1,0:T(8,128)S(1)}, u32[]{:S(2)}, u32[]{:S(2)}) collective-permute-start(f32[8,768]{1,0:T(8,128)S(1)} %maximum_maximum_fusion.2), channel_id=1, source_target_pairs={{2,0},{3,1},{0,2},{1,3},{6,4},{7,5},{4,6},{5,7},{10,8},{11,9},{8,1... | collective-permute-start | bytes 73736 | tf_op jit(solution)/shard_map/ppermute | solution.py:680
  464.2 127.3 %collective-permute-start.18 = (bf16[1024,1536]{1,0:T(8,128)(2,1)}, bf16[1024,1536]{1,0:T(8,128)(2,1)}, u32[]{:S(2)}, u32[]{:S(2)}) collective-permute-start(bf16[1024,1536]{1,0:T(8,128)(2,1)} %out_other.1), channel_id=1, source_target_pairs={{1,0},{0,1},{3,2},{2,3},{5,4},{4,5},{7,6},{6,7},{9,8},{8,9},{11,10... | collective-permute-start | bytes 9437192 | tf_op jit(solution)/shard_map/ppermute | solution.py:692
  466.8 16.8 %collective-permute-start.46 = (bf16[1,192,768]{2,1,0:T(8,128)(2,1)S(1)}, bf16[1,192,768]{2,1,0:T(8,128)(2,1)}, u32[]{:S(2)}, u32[]{:S(2)}) collective-permute-start(bf16[1,192,768]{2,1,0:T(8,128)(2,1)S(1)} %dynamic-slice_convert_fusion.4), channel_id=1, source_target_pairs={{16,0},{20,4},{24,8},{28,12},{0,16},{4,20},{8,24},{12,28},{17,1},{... | collective-permute-start | bytes 884744 | tf_op jit(solution)/shard_map/ppermute | solution.py:730
  483.6 33.3 %collective-permute-start.25 = (f32[8,1536]{1,0:T(8,128)S(1)}, f32[8,1536]{1,0:T(8,128)S(1)}, u32[]{:S(2)}, u32[]{:S(2)}) collective-permute-start(f32[8,1536]{1,0:T(8,128)S(1)} %pad_maximum_fusion.3), channel_id=1, source_target_pairs={{2,0},{3,1},{6,4},{7,5},{10,8},{11,9},{14,12},{15,13},{18,16},{19,... | collective-permute-start | bytes 147464 | tf_op jit(solution)/shard_map/ppermute | solution.py:689
  496.7 42.9 %collective-permute-start.20 = (f32[8,256]{1,0:T(8,128)}, f32[8,256]{1,0:T(8,128)S(1)}, u32[]{:S(2)}, u32[]{:S(2)}) collective-permute-start(f32[8,256]{1,0:T(8,128)} %get-tuple-element.195), channel_id=1, source_target_pairs={{2,0},{3,1},{6,4},{7,5},{10,8},{11,9},{14,12},{15,13},{18,16},{19,... | collective-permute-start | bytes 24584 | tf_op jit(solution)/shard_map/ppermute | solution.py:689
  514.1 31.1 %collective-permute-start.26 = (bf16[1536,256]{0,1:T(8,128)(2,1)}, bf16[1536,256]{0,1:T(8,128)(2,1)S(1)}, u32[]{:S(2)}, u32[]{:S(2)}) collective-permute-start(bf16[1536,256]{0,1:T(8,128)(2,1)} %convolution_convert_fusion.11), channel_id=1, source_target_pairs={{2,0},{3,1},{0,2},{1,3},{6,4},{7,5},{4,6},{5,7},{10,8},{11,9},{8,1... | collective-permute-start | bytes 2359304 | tf_op jit(solution)/shard_map/ppermute | solution.py:680
  517.0 23.4 %collective-permute-start.35 = (bf16[2,192,768]{2,1,0:T(8,128)(2,1)S(1)}, bf16[2,192,768]{2,1,0:T(8,128)(2,1)}, u32[]{:S(2)}, u32[]{:S(2)}) collective-permute-start(bf16[2,192,768]{2,1,0:T(8,128)(2,1)S(1)} %fusion.20), channel_id=1, source_target_pairs={{8,0},{12,4},{0,8},{4,12},{24,16},{28,20},{16,24},{20,28},{9,1},{1... | collective-permute-start | bytes 1769480 | tf_op jit(solution)/shard_map/ppermute | solution.py:730
  518.8 34.9 %collective-permute-start.22 = (bf16[4,192,768]{2,1,0:T(8,128)(2,1)}, bf16[4,192,768]{2,1,0:T(8,128)(2,1)}, u32[]{:S(2)}, u32[]{:S(2)}) collective-permute-start(bf16[4,192,768]{2,1,0:T(8,128)(2,1)} %fusion.11), channel_id=1, source_target_pairs={{4,0},{0,4},{12,8},{8,12},{20,16},{16,20},{28,24},{24,28},{5,1},{1... | collective-permute-start | bytes 3538952 | tf_op jit(solution)/shard_map/ppermute | solution.py:696
  539.6 45.2 %collective-permute-start.28 = (bf16[1024,1536]{1,0:T(8,128)(2,1)}, bf16[1024,1536]{1,0:T(8,128)(2,1)}, u32[]{:S(2)}, u32[]{:S(2)}) collective-permute-start(bf16[1024,1536]{1,0:T(8,128)(2,1)} %back_other.1), channel_id=1, source_target_pairs={{1,0},{0,1},{3,2},{2,3},{5,4},{4,5},{7,6},{6,7},{9,8},{8,9},{11,10... | collective-permute-start | bytes 9437192 | tf_op jit(solution)/shard_map/ppermute | solution.py:692
  541.7 17.6 %collective-permute-start.36 = (bf16[1,192,768]{2,1,0:T(8,128)(2,1)S(1)}, bf16[1,192,768]{2,1,0:T(8,128)(2,1)}, u32[]{:S(2)}, u32[]{:S(2)}) collective-permute-start(bf16[1,192,768]{2,1,0:T(8,128)(2,1)S(1)} %dynamic-slice_convert_fusion.6), channel_id=1, source_target_pairs={{16,0},{20,4},{24,8},{28,12},{0,16},{4,20},{8,24},{12,28},{17,1},{... | collective-permute-start | bytes 884744 | tf_op jit(solution)/shard_map/ppermute | solution.py:730
  556.9 25.7 %collective-permute-start.37 = (bf16[2,192,768]{2,1,0:T(8,128)(2,1)}, bf16[2,192,768]{2,1,0:T(8,128)(2,1)}, u32[]{:S(2)}, u32[]{:S(2)}) collective-permute-start(bf16[2,192,768]{2,1,0:T(8,128)(2,1)} %fusion.21), channel_id=1, source_target_pairs={{8,0},{12,4},{0,8},{4,12},{24,16},{28,20},{16,24},{20,28},{9,1},{1... | collective-permute-start | bytes 1769480 | tf_op jit(solution)/shard_map/ppermute | solution.py:730
  564.3 39.8 %collective-permute-start.39 = (bf16[2,192,256]{2,1,0:T(8,128)(2,1)S(1)}, bf16[2,192,256]{2,1,0:T(8,128)(2,1)S(1)}, u32[]{:S(2)}, u32[]{:S(2)}) collective-permute-start(bf16[2,192,256]{2,1,0:T(8,128)(2,1)S(1)} %fusion.24), channel_id=1, source_target_pairs={{8,0},{12,4},{0,8},{4,12},{24,16},{28,20},{16,24},{20,28},{9,1},{1... | collective-permute-start | bytes 589832 | tf_op jit(solution)/shard_map/ppermute | solution.py:730
  610.6 18.2 %collective-permute-start.38 = (bf16[1,192,768]{2,1,0:T(8,128)(2,1)S(1)}, bf16[1,192,768]{2,1,0:T(8,128)(2,1)S(1)}, u32[]{:S(2)}, u32[]{:S(2)}) collective-permute-start(bf16[1,192,768]{2,1,0:T(8,128)(2,1)S(1)} %dynamic-slice_convert_fusion.5), channel_id=1, source_target_pairs={{16,0},{20,4},{24,8},{28,12},{0,16},{4,20},{8,24},{12,28},{17,1},{... | collective-permute-start | bytes 884744 | tf_op jit(solution)/shard_map/ppermute | solution.py:730
  (102 other events, 1324.1 us)

commit v3 on v2

--- a/solution.py
+++ b/solution.py
@@ -19,6 +19,12 @@
 HIGH = lax.Precision.HIGHEST
 VMEM_LIMIT = 56 * 1024 * 1024
 STEP_ROWS = 512
+PACE = 1.15e9 * 1.0
+TIMES = dict(
+    chip_rows=7, prepare=10, states=13, scan=15, gate_back=16, scan_back=33, out_other=9, out_own=11,
+    back_other=17, back_own=22, shared_back=10,
+)
+SCAN_LANES = False
 
 NN = (((1,), (0,)), ((), ()))
 NT = (((1,), (1,)), ((), ()))
@@ -29,9 +35,10 @@
     return lax.dot_general(a, b, dims, precision=precision, preferred_element_type=F32)
 
 
-STEP, LOG, MARK, RISE = 0, 32, 64, 96
+STEP, MARK, RISE = 0, 64, 96
 CARRIES, ENDING, VALID, SEGMENT = MARK, MARK + 1, MARK + 2, MARK + 3
 EARLIER, LATER = MARK + 3, MARK + 6
+LOG = 32
 
 
 def loop(count, body):
@@ -76,7 +83,7 @@
     first = lax.broadcasted_iota(jnp.int32, (Q, Q), 0)
     second = lax.broadcasted_iota(jnp.int32, (Q, Q), 1)
     ordered = (first <= second) if flipped else (first >= second)
-    allowed = ordered & (cols[:, SEGMENT : SEGMENT + 1] == rows[LOG : LOG + 1, :])
+    allowed = ordered & (cols[:, SEGMENT : SEGMENT + 1] == rows[0:1, :])
     return jnp.where(allowed, 0.0, NEVER)
 
 
@@ -109,12 +116,17 @@
     return dot(high, picks) + dot(rest, picks)
 
 
-def in_order(member, ordered):
+def in_parts(member):
+    lane = lax.broadcasted_iota(jnp.int32, member.shape, 1)
+    member = jnp.where(lane < 32, member, 0.0)
     first = member.astype(BF16).astype(F32)
     rest = member - first
     second = rest.astype(BF16).astype(F32)
-    parts = first + pltpu.roll(second, 32, 1) + pltpu.roll(rest - second, 64, 1)
-    total = dot(ordered.astype(BF16), parts.astype(BF16))
+    return first + pltpu.roll(second, 32, 1) + pltpu.roll(rest - second, 64, 1)
+
+
+def in_order(member, ordered):
+    total = dot(ordered.astype(BF16), in_parts(member).astype(BF16))
     return total + pltpu.roll(total, 96, 1) + pltpu.roll(total, 64, 1)
 
 
@@ -122,29 +134,48 @@
     return 0.5 * jnp.tanh(0.5 * v) + 0.5
 
 
-def conv_before_act(ext, taps, cols):
-    total = ext[8 : 8 + Q, :] * taps[3:4, :] + taps[4:5, :]
+def shifts(marks, later):
+    row = lax.broadcasted_iota(jnp.int32, (Q, Q), 0)
+    column = lax.broadcasted_iota(jnp.int32, (Q, Q), 1)
+    parts = []
     for j in range(1, 4):
-        same = cols[:, EARLIER + j : EARLIER + j + 1]
-        total = total + (ext[8 - j : 8 - j + Q, :] * same) * taps[3 - j : 4 - j, :]
-    return total
-
-
-def follow(group, ext, halo, current):
-    @pl.when(group == 0)
-    def _():
-        ext[0:8, :] = halo[8:16, :].astype(F32)
-
-    @pl.when(group > 0)
-    def _():
-        ext[0:8, :] = ext[Q : Q + 8, :]
-
-    ext[8 : 8 + Q, :] = current.astype(F32)
+        if later:
+            parts.append(jnp.where(column == row + j, marks[j : j + 1, :], 0.0))
+        else:
+            parts.append(jnp.where(column == row - j, marks[3 + j : 4 + j, :], 0.0))
+    return jnp.concatenate(parts, axis=0).astype(BF16)
+
+
+def edge_shifts(scal, edge, later):
+    row = lax.broadcasted_iota(jnp.int32, (16, 16), 0)
+    column = lax.broadcasted_iota(jnp.int32, (16, 16), 1)
+    at = edge + row - (16 if later else 0)
+    other = edge + column - (0 if later else 16)
+    same = segment_of(scal, at) == segment_of(scal, other)
+    parts = [
+        jnp.where(same & (other == (at + j if later else at - j)), 1.0, 0.0) for j in range(1, 4)
+    ]
+    return jnp.concatenate(parts, axis=0).astype(BF16)
+
+
+def conv_before_act(scal, group, raw, halo, tail, taps, marks):
+    current = raw[...]
+    before = jnp.where(group == 0, halo[...], tail[...])
+    moved = dot(shifts(marks, False), current)
+    edge = dot(edge_shifts(scal, scal[4] + group * Q, False), before)
+    total = current.astype(F32) * taps[3:4, :] + taps[4:5, :]
+    first = jnp.zeros((16, current.shape[1]), F32)
+    for j in range(1, 4):
+        tap = taps[3 - j : 4 - j, :]
+        total = total + moved[(j - 1) * Q : j * Q] * tap
+        first = first + edge[(j - 1) * 16 : j * 16] * tap
+    tail[...] = current[Q - 16 : Q]
+    return jnp.concatenate([total[:16] + first, total[16:]], axis=0)
 
 
 def prepare_kernel(
-    subs, scal, shared, rates, halo, taps, head_rows, bc_out, bct_out, cols_out, rows_out, total_out,
-    ext, running,
+    subs, scal, shared, rates, halo, taps, head_rows, bc_out, bct_out, cols_out, logs_out, steps_out,
+    marks_out, across_out, total_out, tail, running,
 ):
     @pl.when(pl.program_id(0) == 0)
     def _():
@@ -153,40 +184,51 @@
     def body(k):
         group = pl.program_id(0) * subs + k
         bc, cols = group_of(bc_out, k), group_of(cols_out, k)
-        bct, rows = lane_group_of(bct_out, k), rows_out.at[k]
+        bct, marks, across = lane_group_of(bct_out, k), marks_out.at[k], across_out.at[k]
         width = bc.shape[1]
         raw = group_of(rates, k)[...] + head_rows[0:1, :]
         step = jnp.maximum(raw, 0.0) + jnp.log1p(jnp.exp(-jnp.abs(raw)))
         scaled = step * (head_rows[1:2, :] * LOG2E)
         at = lax.broadcasted_iota(jnp.int32, (Q, Q), 0)
         lane = lax.broadcasted_iota(jnp.int32, (Q, Q), 1)
-        summed = in_order(jnp.where(lane < 32, scaled, 0.0), (at >= lane).astype(F32))
+        summed = in_order(scaled, (at >= lane).astype(F32))
+        parts = in_parts(summed)
+        ones = (lane >= 96) & (lane < 99)
+        group_of(logs_out, k)[...] = jnp.where(ones, 1.0, parts).astype(BF16)
+        group_of(steps_out, k)[...] = in_parts(step).astype(BF16)
+        turned = parts.T
+        row = lax.broadcasted_iota(jnp.int32, (16, Q), 0)
+        for h in range(across.shape[1] // Q):
+            found = jnp.zeros((16, Q), F32)
+            for m in range(3):
+                found = jnp.where(row == m, -turned[32 * m + h : 32 * m + h + 1, :], found)
+            across[:, h * Q : (h + 1) * Q] = found.astype(BF16)
+
         first = scal[4] + group * Q
         position = first + at[:, 0:1]
         segment = segment_of(scal, position)
-        marks = {
+        marked = {
             CARRIES: segment == segment_of(scal, first - 1),
             ENDING: segment == segment_of(scal, first + Q - 1),
             VALID: position < scal[0] + scal[1] + scal[2] + scal[3],
         }
-        for j in range(1, 4):
-            marks[EARLIER + j] = segment == segment_of(scal, position - j)
-            marks[LATER + j] = segment == segment_of(scal, position + j)
         member = jnp.where(lane == SEGMENT, segment.astype(F32), 0.0)
-        for mark, found in marks.items():
+        for mark, found in marked.items():
             member = jnp.where(lane == mark, found.astype(F32), member)
         member = jnp.where(lane < LOG, step, member)
         member = jnp.where((lane >= LOG) & (lane < MARK), pltpu.roll(summed, LOG, 1), member)
-        member = jnp.where(lane >= RISE, pltpu.roll(sigmoid(raw), RISE, 1), member)
-        cols[...] = member
-        across = member.T
-        rows[0:LOG, :] = across[LOG:MARK]
-        rows[LOG : LOG + 8, :] = across[SEGMENT : SEGMENT + 8]
+        cols[...] = jnp.where(lane >= RISE, pltpu.roll(sigmoid(raw), RISE, 1), member)
+        mark = lax.broadcasted_iota(jnp.int32, (8, Q), 0)
+        position = first + lax.broadcasted_iota(jnp.int32, (8, Q), 1)
+        segment = segment_of(scal, position)
+        other = position + jnp.where(mark < 4, -mark, jnp.where(mark < 7, mark - 3, 0))
+        same = (segment_of(scal, other) == segment).astype(F32)
+        marks[0:8, :] = jnp.where(mark == 0, segment.astype(F32), same)
+        marks[8:40, :] = summed.T[:32]
         total_out[pl.ds(pl.multiple_of(k * 8, 8), 8), :] = running[...]
         running[...] = running[...] + summed[Q - 1 : Q, :]
 
-        follow(group, ext, halo, group_of(shared, k)[...])
-        pre = conv_before_act(ext, taps, cols)
+        pre = conv_before_act(scal, group, group_of(shared, k), halo, tail, taps, marks)
         act = pre * sigmoid(pre)
         bc[...] = act.astype(BF16)
         bct[...] = jnp.concatenate(
@@ -197,8 +239,8 @@
 
 
 def states_kernel(
-    subs, head, scal, raw, halo, taps, cols_in, bct_in, total, act_out, slope_out, states, final,
-    through, ext, state,
+    subs, head, scal, raw, halo, taps, spread, cols_in, logs_in, steps_in, marks_in, bct_in, total,
+    act_out, slope_out, states, final, through, tail, state,
 ):
     channels = raw.shape[1]
 
@@ -209,17 +251,16 @@
     def body(k):
         group = pl.program_id(0) * subs + k
         cols, bct = group_of(cols_in, k), lane_group_of(bct_in, k)
-        follow(group, ext, halo, group_of(raw, k)[...])
-        pre = conv_before_act(ext, taps, cols)
+        pre = conv_before_act(scal, group, group_of(raw, k), halo, tail, taps, marks_in.at[k])
         gate = sigmoid(pre)
         act = (pre * gate).astype(BF16)
         group_of(act_out, k)[...] = act
         group_of(slope_out, k)[...] = (gate * (1.0 + pre * (1.0 - gate))).astype(BF16)
-        summed = spread_heads(cols[...], LOG + head, channels)
+        summed = dot(group_of(logs_in, k)[...], spread[...])
         last = summed[Q - 1 : Q, :]
         tails = jnp.exp2(last - summed) * cols[:, ENDING : ENDING + 1]
-        scaled = (act.astype(F32) * spread_heads(cols[...], STEP + head, channels)).astype(BF16)
-        fresh = dot(bct[:STATE, :], (scaled.astype(F32) * tails).astype(BF16))
+        scaled = act.astype(F32) * dot(group_of(steps_in, k)[...], spread[...])
+        fresh = dot(bct[:STATE, :], (scaled * tails).astype(BF16))
         states[k] = state[...].astype(BF16)
         state[...] = state[...] * (jnp.exp2(last) * kept(scal, group)) + fresh
 
@@ -228,9 +269,9 @@
     @pl.when(pl.program_id(0) == pl.num_programs(0) - 1)
     def _():
         final[...] = state[...]
-        at = (subs - 1) * 8
-        ended = total[at : at + 8, :] + pltpu.roll(cols_in[subs * Q - 8 : subs * Q, :], 128 - LOG, 1)[7:8]
-        through[...] = jnp.exp2(spread_heads(ended, head, channels)) * reaches(
+        ended = total[(subs - 1) * 8 : subs * 8, :]
+        last = dot(logs_in[subs * Q - 16 : subs * Q, :], spread[...])[15:16]
+        through[...] = jnp.exp2(spread_heads(ended, head, channels) + last) * reaches(
             scal, pl.num_programs(0) * subs
         )
 
@@ -240,20 +281,40 @@
     return jnp.exp2(spread_heads(here, head, channels))[0:1] * reaches(scal, group)
 
 
+def gaps_of(pair, head, cols, logs, marks, between, across_lanes):
+    if not across_lanes:
+        both = dot(logs[...], between[:, 2 * pair * Q : 2 * (pair + 1) * Q])
+        return [both[:, :Q], both[:, Q:]]
+    lane = LOG + head + 2 * pair
+    return [
+        jnp.broadcast_to(cols[:, lane + m : lane + m + 1], (Q, Q))
+        - marks[8 + head + 2 * pair + m : 9 + head + 2 * pair + m, :]
+        for m in range(2)
+    ]
+
+
 def scan_kernel(
-    subs, head, scal, act_in, bc_in, cols_in, rows_in, total, gate_in, back_in, states, start, taps,
-    scanned_out, stats_out,
+    subs, head, scal, act_in, bc_in, cols_in, logs_in, steps_in, marks_in, across, spread, spread_rows,
+    total, gate_in, back_in, states, start, taps, scanned_out, stats_out, between,
 ):
     channels = act_in.shape[1]
+
+    @pl.when(pl.program_id(0) == 0)
+    def _():
+        between[...] = spread_rows[...]
 
     def body(k):
         group = pl.program_id(0) * subs + k
         act, bc, cols = group_of(act_in, k), group_of(bc_in, k), group_of(cols_in, k)
-        gate, back, rows = group_of(gate_in, k), group_of(back_in, k), rows_in.at[k]
+        gate, back, logs = group_of(gate_in, k), group_of(back_in, k), group_of(logs_in, k)
+        between[96:112, :] = across[k]
+        marks = marks_in.at[k]
+        summed_all = dot(logs[...], spread[...])
+        steps = dot(group_of(steps_in, k)[...], spread[...])
         scanned = group_of(scanned_out, k)
         b_map, c_map = bc[:, :STATE], bc[:, STATE:]
         scores = dot(c_map, b_map, NT)
-        allowed = triangle(cols, rows, False)
+        allowed = triangle(cols, marks, False)
         carries = cols[:, CARRIES : CARRIES + 1]
         share = total_share(scal, group, head, total, k, channels)
         state = (states[k].astype(F32) + share * start[...]).astype(BF16)
@@ -262,16 +323,14 @@
         inner = jnp.zeros((Q, 2 * HEAD), F32)
         for p in range(channels // (2 * HEAD)):
             part = slice(2 * HEAD * p, 2 * HEAD * (p + 1))
+            gaps = gaps_of(p, head, cols, logs, marks, between, SCAN_LANES)
             weights = []
-            columns = []
-            for h in (head + 2 * p, head + 2 * p + 1):
-                column = jnp.broadcast_to(cols[:, LOG + h : LOG + h + 1], (Q, Q))
-                columns.append(column)
-                decay = jnp.exp2(column + (allowed - rows[h : h + 1, :]))
+            for m in range(2):
+                decay = jnp.exp2(gaps[m] + allowed)
                 weights.append((decay * scores).astype(BF16))
-            summed = jnp.where(in_first(Q), columns[0], columns[1])
+            summed = summed_all[:, part]
             member = act[:, part].astype(F32)
-            scaled = (member * pair_of(cols[...], STEP + head + 2 * p)).astype(BF16)
+            scaled = (member * steps[:, part]).astype(BF16)
             result = dot(jnp.concatenate(weights, axis=1), stacked_heads(scaled))
             result = result + outside[:, part] * (jnp.exp2(summed) * carries)
             scanned[:, part] = result
@@ -290,8 +349,8 @@
 
 
 def gate_back_kernel(
-    subs, head, inner_channels, scal, scanned_in, act_in, gate_in, back_in, stats_in, bct_in, cols_in,
-    total, taps, mixed_out, low_gate_out, back_heads_out, reach, sums,
+    subs, turns, head, inner_channels, scal, scanned_in, act_in, gate_in, back_in, stats_in, bct_in, cols_in,
+    logs_in, spread, total, taps, mixed_out, low_gate_out, back_heads_out, reach, sums,
 ):
     channels = act_in.shape[1]
 
@@ -315,6 +374,7 @@
         valid, carries = cols[:, VALID : VALID + 1], cols[:, CARRIES : CARRIES + 1]
         slope = inverse * inverse * inverse * inner * valid / inner_channels
         inverse_valid = inverse * valid
+        summed = dot(group_of(logs_in, k)[...], spread[...])
         gradients = []
         for p in range(channels // (2 * HEAD)):
             part = slice(2 * HEAD * p, 2 * HEAD * (p + 1))
@@ -334,31 +394,25 @@
             wide = low.astype(F32)
             sums[0:1, part] = sums[0:1, part] + jnp.sum(scaled_back * gated, axis=0, keepdims=True)
             sums[1:2, part] = sums[1:2, part] + jnp.sum(wide * member, axis=0, keepdims=True)
-            entered = jnp.exp2(pair_of(cols[...], LOG + head + 2 * p)) * carries
+            entered = jnp.exp2(summed[:, part]) * carries
             gradients.append((wide * entered).astype(BF16))
         share = total_share(scal, group, head, total, k, channels)
         reach[...] = reach[...] + share * dot(bct[STATE:, :], jnp.concatenate(gradients, axis=1))
 
-    loop(subs, body)
-
-
-def first_sent_back(scal, later, taps):
-    row = lax.broadcasted_iota(jnp.int32, (16, 1), 0)
-    out = jnp.zeros((16, later.shape[1]), F32)
-    for back in range(1, 4):
-        at = scal[4] - back
-        extra = jnp.zeros((1, later.shape[1]), F32)
-        for j in range(back, 4):
-            same = same_segment(scal, at, at + j)
-            extra = extra + same * taps[3 - j : 4 - j, :] * later[j - back : j - back + 1, :]
-        out = jnp.where(row == 16 - back, extra, out)
-    return out
+    @pl.when(pl.program_id(0) < turns)
+    def _():
+        loop(subs, body)
+
+    @pl.when(pl.program_id(0) == turns)
+    def _():
+        low_gate_out[...] = jnp.zeros_like(low_gate_out)
 
 
 def scan_back_kernel(
-    subs, head, scal, act_in, slope_in, heads_in, scanned_in, raw, before, halo, taps, picks, bc_in,
-    bct_in, cols_in, rows_in, total, head_rows, states, start, leaving, low_out, back_bc_out,
-    low_rate_out, sums, head_out, first_rows, last_rows, ext, back_ext, back_state, difference,
+    subs, head, scal, act_in, slope_in, heads_in, scanned_in, raw, halo, taps, picks, bc_in, bct_in,
+    cols_in, logs_in, steps_in, marks_in, across, spread, spread_rows, total, head_rows, states, start,
+    leaving, low_out, back_bc_out, low_rate_out, sums, head_out, first_rows, last_rows, behind, back_pre,
+    back_state, difference, between,
 ):
     turn = pl.program_id(0)
     turns = pl.num_programs(0) - 1
@@ -367,7 +421,8 @@
     @pl.when(turn == 0)
     def _():
         back_state[...] = leaving[...]
-        back_ext[Q : Q + 8, :] = jnp.zeros_like(back_ext[Q : Q + 8, :])
+        behind[...] = jnp.zeros_like(behind)
+        between[...] = spread_rows[...]
         sums[...] = jnp.zeros_like(sums)
         head_out[...] = jnp.zeros_like(head_out)
 
@@ -376,10 +431,14 @@
         group = (turns - 1 - turn) * subs + k
         act, slope, back_heads = group_of(act_in, k), group_of(slope_in, k), group_of(heads_in, k)
         scanned, bc, cols = group_of(scanned_in, k), group_of(bc_in, k), group_of(cols_in, k)
-        bct, rows, back_bc = lane_group_of(bct_in, k), rows_in.at[k], group_of(back_bc_out, k)
+        bct, back_bc, logs = lane_group_of(bct_in, k), group_of(back_bc_out, k), group_of(logs_in, k)
+        between[96:112, :] = across[k]
+        marks = marks_in.at[k]
+        summed_all = dot(logs[...], spread[...])
+        steps = dot(group_of(steps_in, k)[...], spread[...])
         b_map, c_map = bc[:, :STATE], bc[:, STATE:]
         scores = dot(b_map, c_map, NT)
-        allowed = triangle(cols, rows, True)
+        allowed = triangle(cols, marks, True)
         carries, ending = cols[:, CARRIES : CARRIES + 1], cols[:, ENDING : ENDING + 1]
         share = total_share(scal, group, head, total, k, channels)
         state = states[k].astype(F32) + share * start[...]
@@ -393,20 +452,20 @@
             low = back_heads[:, part]
             wide = low.astype(F32)
             member = act[:, part].astype(F32)
-            step = pair_of(cols[...], STEP + head + 2 * p)
+            step = steps[:, part]
             scaled = (member * step).astype(BF16)
+            stacked = stacked_heads(low)
             back_weights = dot(stacked_heads(scaled), low, NT)
-            weights, columns = [], []
-            for m, h in enumerate((head + 2 * p, head + 2 * p + 1)):
-                column = jnp.broadcast_to(cols[:, LOG + h : LOG + h + 1], (Q, Q))
-                columns.append(column)
-                decay = jnp.exp2((rows[h : h + 1, :] + allowed) - column)
+            gaps = gaps_of(p, head, cols, logs, marks, between, True)
+            weights = []
+            for m in range(2):
+                decay = jnp.exp2(allowed - gaps[m])
                 weights.append((decay * scores).astype(BF16))
                 back_scores = back_scores + decay * back_weights[m * Q : (m + 1) * Q]
-            summed = jnp.where(in_first(Q), columns[0], columns[1])
+            summed = summed_all[:, part]
             last = summed[Q - 1 : Q, :]
             tails = jnp.exp2(last - summed) * ending
-            back_scaled = dot(jnp.concatenate(weights, axis=1), stacked_heads(low))
+            back_scaled = dot(jnp.concatenate(weights, axis=1), stacked)
             scaled_wide = scaled.astype(F32)
             from_end = tails * from_state[:, part]
             difference[:, part] = wide * scanned[:, part] - scaled_wide * back_scaled
@@ -416,7 +475,7 @@
             out_of_state.append((wide * (jnp.exp2(summed) * carries)).astype(BF16))
             products.append((back_scaled * member).astype(BF16))
             back_act = back_scaled * step + taps[6:7, part] * wide
-            back_ext[0:Q, part] = back_act * slope[:, part].astype(F32)
+            back_pre[:, part] = back_act * slope[:, part].astype(F32)
         into_state = jnp.concatenate(into_state, axis=1)
         out_of_state = jnp.concatenate(out_of_state, axis=1)
         back_b = dot(back_scores.astype(BF16), c_map) + dot(into_state, leaving_low, NT)
@@ -424,8 +483,7 @@
         back_bc[:, :STATE] = back_b
         back_bc[:, STATE:] = back_c
 
-        whole_group = spread_heads(cols[Q - 1 : Q, :], LOG + head, channels)
-        kept_state = back_state[...] * (jnp.exp2(whole_group) * kept(scal, group))
+        kept_state = back_state[...] * (jnp.exp2(summed_all[Q - 1 : Q, :]) * kept(scal, group))
         back_state[...] = kept_state + dot(bct[STATE:, :], out_of_state)
         crossing = jnp.sum(kept_state * state, axis=0, keepdims=True)
         difference[Q - 1 : Q, :] = difference[Q - 1 : Q, :] + crossing
@@ -444,8 +502,8 @@
         head_out[0:1, :] = head_out[0:1, :] + jnp.sum(back_rate, axis=0, keepdims=True)
         head_out[1:2, :] = head_out[1:2, :] + jnp.sum(decays * cols[...], axis=0, keepdims=True)
 
-        conv_back(turn, k, ext, back_ext, raw, before, halo, taps, cols, group_of(low_out, k), sums,
-                  first_rows, last_rows, group)
+        conv_back(scal, turn, k, group, back_pre[...], behind, group_of(raw, k), taps, marks,
+                  group_of(low_out, k), sums, first_rows, last_rows, subs)
 
     @pl.when(turn < turns)
     def _():
@@ -454,65 +512,77 @@
     @pl.when(turn == turns)
     def _():
         low_rate_out[...] = jnp.zeros_like(low_rate_out)
-        low_out[...] = jnp.zeros_like(low_out)
-        low_out[0:16, :] = first_sent_back(scal, first_rows, taps).astype(BF16)
+        rows_behind(scal, behind, halo, taps, low_out, sums)
 
 
 def conv_back(
-    turn, k, ext, back_ext, raw, before, halo, taps, cols, low, sums, first_rows, last_rows, group
+    scal, turn, k, group, now, behind, raw, taps, marks, low, sums, first_rows, last_rows, subs
 ):
-    start = pl.multiple_of(jnp.maximum(k * Q - 16, 0), 16)
-    earlier = jnp.where(group == 0, halo[...], before[...])
-    earlier = jnp.where(k == 0, earlier, raw[pl.ds(start, 16), :])
-    ext[0:8, :] = earlier[8:16].astype(F32)
-    ext[8 : 8 + Q, :] = group_of(raw, k)[...].astype(F32)
-    now = back_ext[0:Q, :]
-    sums[3:4, :] = sums[3:4, :] + jnp.sum(now * ext[8 : 8 + Q, :], axis=0, keepdims=True)
+    now_low = now.astype(BF16)
+    moved = dot(shifts(marks, True), now_low)
+    edge = dot(edge_shifts(scal, scal[4] + (group + 1) * Q, True), behind[...])
+    value = raw[...].astype(F32)
+    sums[3:4, :] = sums[3:4, :] + jnp.sum(now * value, axis=0, keepdims=True)
     sums[4:5, :] = sums[4:5, :] + jnp.sum(now, axis=0, keepdims=True)
     total = now * taps[3:4, :]
+    last = jnp.zeros((16, now.shape[1]), F32)
     for j in range(1, 4):
         tap = slice(3 - j, 4 - j)
-        earlier = ext[8 - j : 8 - j + Q, :] * cols[:, EARLIER + j : EARLIER + j + 1]
-        sums[tap, :] = sums[tap, :] + jnp.sum(now * earlier, axis=0, keepdims=True)
-        later = back_ext[j : j + Q, :] * cols[:, LATER + j : LATER + j + 1]
-        total = total + later * taps[tap, :]
-    low[...] = total.astype(BF16)
-
-    @pl.when((turn == 0) & (k == raw.shape[0] // Q - 1))
-    def _():
-        last_rows[...] = total[Q - 8 : Q, :]
-
-    back_ext[Q : Q + 8, :] = back_ext[0:8, :]
-    first_rows[...] = back_ext[0:8, :]
+        part, rest = moved[(j - 1) * Q : j * Q], edge[(j - 1) * 16 : j * 16]
+        total = total + part * taps[tap, :]
+        last = last + rest * taps[tap, :]
+        sums[tap, :] = (
+            sums[tap, :]
+            + jnp.sum(part * value, axis=0, keepdims=True)
+            + jnp.sum(rest * value[Q - 16 : Q], axis=0, keepdims=True)
+        )
+    last = total[Q - 16 :] + last
+    low[...] = jnp.concatenate([total[: Q - 16], last], axis=0).astype(BF16)
+
+    @pl.when((turn == 0) & (k == subs - 1))
+    def _():
+        last_rows[...] = last[8:]
+
+    behind[...] = now_low[0:16]
+    first_rows[...] = now[0:8]
+
+
+def rows_behind(scal, behind, halo, taps, low_out, sums):
+    edge = dot(edge_shifts(scal, scal[4], True), behind[...])
+    value = halo[...].astype(F32)
+    total = jnp.zeros((16, value.shape[1]), F32)
+    for j in range(1, 4):
+        tap, rest = slice(3 - j, 4 - j), edge[(j - 1) * 16 : j * 16]
+        total = total + rest * taps[tap, :]
+        sums[tap, :] = sums[tap, :] + jnp.sum(rest * value, axis=0, keepdims=True)
+    low_out[...] = jnp.zeros_like(low_out)
+    low_out[0:16, :] = total.astype(BF16)
 
 
 def shared_back_kernel(
-    subs, scal, back_bc, back_more, raw, before, halo, taps, cols_in, low_out, sums, first_rows,
-    last_rows, ext, back_ext,
+    subs, scal, back_bc, back_more, raw, before, halo, taps, marks_in, low_out, sums, first_rows,
+    last_rows, behind, tail,
 ):
     turn = pl.program_id(0)
     turns = pl.num_programs(0) - 1
 
     @pl.when(turn == 0)
     def _():
-        back_ext[Q : Q + 8, :] = jnp.zeros_like(back_ext[Q : Q + 8, :])
+        behind[...] = jnp.zeros_like(behind)
         sums[...] = jnp.zeros_like(sums)
 
     def body(count):
         k = subs - 1 - count
         group = (turns - 1 - turn) * subs + k
-        cols = group_of(cols_in, k)
         start = pl.multiple_of(jnp.maximum(k * Q - 16, 0), 16)
-        earlier = jnp.where(group == 0, halo[...], before[...])
-        earlier = jnp.where(k == 0, earlier, raw[pl.ds(start, 16), :])
-        ext[0:8, :] = earlier[8:16].astype(F32)
-        ext[8 : 8 + Q, :] = group_of(raw, k)[...].astype(F32)
-        pre = conv_before_act(ext, taps, cols)
+        tail[...] = jnp.where(k == 0, before[...], raw[pl.ds(start, 16), :])
+        marks = marks_in.at[k]
+        pre = conv_before_act(scal, group, group_of(raw, k), halo, tail, taps, marks)
         gate = sigmoid(pre)
         back = group_of(back_bc, k)[...] + group_of(back_more, k)[...]
-        back_ext[0:Q, :] = back * (gate * (1.0 + pre * (1.0 - gate)))
-        conv_back(turn, k, ext, back_ext, raw, before, halo, taps, cols, group_of(low_out, k), sums,
-                  first_rows, last_rows, group)
+        now = back * (gate * (1.0 + pre * (1.0 - gate)))
+        conv_back(scal, turn, k, group, now, behind, group_of(raw, k), taps, marks,
+                  group_of(low_out, k), sums, first_rows, last_rows, subs)
 
     @pl.when(turn < turns)
     def _():
@@ -520,8 +590,7 @@
 
     @pl.when(turn == turns)
     def _():
-        low_out[...] = jnp.zeros_like(low_out)
-        low_out[0:16, :] = first_sent_back(scal, first_rows, taps).astype(BF16)
+        rows_behind(scal, behind, halo, taps, low_out, sums)
 
 
 def joined(scal, low, later, last_rows, taps, rows):
@@ -545,25 +614,21 @@
     out[...] = jnp.where(mine, own[...], other[...])
 
 
-def normed_rows_kernel(tiles, scal, own, other, halo, gain, out):
-    def normed(member):
-        wide = member.astype(F32)
+def normed_rows_kernel(tiles, scal, own, other, gain, out):
+    step = pl.program_id(0)
+
+    @pl.when(step < 2 * tiles)
+    def _():
+        wide = jnp.where(step // tiles == scal[0], own[...], other[...]).astype(F32)
         inverse = lax.rsqrt(jnp.mean(wide * wide, axis=1, keepdims=True) + EPS)
-        return (wide * inverse * gain[...]).astype(BF16)
-
-    step = pl.program_id(0)
-
-    @pl.when(step < 2 * tiles)
-    def _():
-        out[...] = normed(jnp.where(step // tiles == scal[0], own[...], other[...]))
+        out[...] = (wide * inverse * gain[...]).astype(BF16)
 
     @pl.when(step == 2 * tiles)
     def _():
         out[...] = jnp.zeros_like(out)
-        out[0:16, :] = normed(halo[...])
-
-
-def chip_rows(core, own, other, halo=None, gain=None):
+
+
+def chip_rows(core, own, other, gain=None):
     rows, width = own.shape
     tile = min(512, rows)
     tiles = rows // tile
@@ -576,8 +641,8 @@
     body, extra = partial(chip_rows_kernel, tiles), 0
     if gain is not None:
         body, extra = partial(normed_rows_kernel, tiles), 1
-        specs += [whole(halo.shape), whole((1, width))]
-        args += [halo, gain.reshape(1, width)]
+        specs.append(whole((1, width)))
+        args.append(gain.reshape(1, width))
     return call(
         body,
         2 * tiles + extra,
@@ -586,38 +651,64 @@
         [shape_of((2 * rows + extra * Q, width), BF16)],
         [],
         "chip_rows",
-        rows * width * 8,
         tuple(args),
     )[0]
 
 
-def many_dots_kernel(dims, scal, *refs):
+def many_dots_kernel(dims, finish, scal, *refs):
     count = len(dims)
-    out = refs[2 * count]
     total = dot(refs[0][...], refs[count][...], dims[0])
     for k in range(1, count):
         total = total + dot(refs[k][...], refs[count + k][...], dims[k])
+    finish(total, *refs[2 * count :])
+
+
+def write_sum(total, out):
     out[...] = total.astype(out.dtype)
 
 
-def call(body, grid, in_specs, out_specs, out_shape, scratch, name, flops, args):
-    moved = sum(a.size * a.dtype.itemsize for a in args) + sum(
-        int(np.prod(o.shape)) * np.dtype(o.dtype).itemsize for o in out_shape
-    )
+def write_output(total, tokens, other, out):
+    out[...] = (tokens[...].astype(F32) + total + other[...].astype(F32)).astype(out.dtype)
+
+
+def write_input_gradient(total, tokens, other, cotangent, gain, out, gain_sum):
+    @pl.when(pl.program_id(0) == 0)
+    def _():
+        gain_sum[...] = jnp.zeros_like(gain_sum)
+
+    residual = tokens[...].astype(F32)
+    inverse = lax.rsqrt(jnp.mean(residual * residual, axis=1, keepdims=True) + EPS)
+    back = total + other[...].astype(F32)
+    gain_sum[0:1, :] = gain_sum[0:1, :] + jnp.sum(back * residual * inverse, axis=0, keepdims=True)
+    scaled = back * gain[...]
+    slope = inverse * inverse * inverse * jnp.mean(scaled * residual, axis=1, keepdims=True)
+    out[...] = cotangent[...].astype(F32) + scaled * inverse - residual * slope
+
+
+def call(body, grid, in_specs, out_specs, out_shape, scratch, name, args, waits=()):
+    given, made = len(in_specs), len(out_specs)
+
+    def kernel(scal, *refs):
+        outs = refs[given + len(waits) :]
+        outs[made][...] = jnp.ones_like(outs[made])
+        body(scal, *refs[:given], *outs[:made], *outs[made + 1 :])
+
     return pl.pallas_call(
-        body,
+        kernel,
         grid_spec=pltpu.PrefetchScalarGridSpec(
             num_scalar_prefetch=1,
             grid=(grid,),
-            in_specs=in_specs,
-            out_specs=out_specs,
+            in_specs=list(in_specs) + [pl.BlockSpec(memory_space=pl.ANY)] * len(waits),
+            out_specs=list(out_specs) + [whole((8, 128))],
             scratch_shapes=scratch,
         ),
-        out_shape=out_shape,
+        out_shape=list(out_shape) + [shape_of((8, 128), F32)],
         compiler_params=pltpu.CompilerParams(vmem_limit_bytes=VMEM_LIMIT),
-        cost_estimate=pl.CostEstimate(flops=10**6, bytes_accessed=10**5, transcendentals=0),
+        cost_estimate=pl.CostEstimate(
+            flops=int(PACE * TIMES[name]), bytes_accessed=10**5, transcendentals=0
+        ),
         name=name,
-    )(*args)
+    )(*args, *waits)
 
 
 def whole(shape):
@@ -649,23 +740,26 @@
     return jax.ShapeDtypeStruct(shape, dtype)
 
 
-def many_dots(offset_rows, lefts, rights, dims, rows, dtype, name):
+def many_dots(
+    offset_rows, lefts, rights, dims, rows, name, finish=write_sum, extras=(), dtype=BF16, sums=(), waits=()
+):
     tile = min(256, rows)
     columns = rights[0].shape[0 if dims[0] == NT else 1]
     scal = (offset_rows // tile).reshape(1).astype(jnp.int32)
-    flops = 2 * rows * columns * sum(a.shape[1] for a in lefts)
+    by_row = pl.BlockSpec((tile, columns), lambda i, s: (i, 0))
     return call(
-        partial(many_dots_kernel, tuple(dims)),
+        partial(many_dots_kernel, tuple(dims), finish),
         rows // tile,
         [pl.BlockSpec((tile, a.shape[1]), lambda i, s: (s[0] + i, 0)) for a in lefts]
-        + [whole(b.shape) for b in rights],
-        [pl.BlockSpec((tile, columns), lambda i, s: (i, 0))],
-        [shape_of((rows, columns), dtype)],
+        + [whole(b.shape) for b in rights]
+        + [by_row if e.shape[0] == rows else whole(e.shape) for e in extras],
+        [by_row] + [whole(shape) for shape in sums],
+        [shape_of((rows, columns), dtype)] + [shape_of(shape, F32) for shape in sums],
         [],
         name,
-        flops,
-        (scal, *lefts, *rights),
-    )[0]
+        (scal, *lefts, *rights, *extras),
+        waits,
+    )
 
 
 def solution(mesh):
@@ -706,13 +800,6 @@
             bit *= 2
         return member
 
-    def sum_row_group(member):
-        bit = 1
-        while bit < tensor:
-            member = member + lax.ppermute(member, "tensor", [(t ^ bit, t) for t in range(tensor)])
-            bit *= 2
-        return member
-
     def ways_x(member, x):
         kept = lax.dynamic_index_in_dim(member, x, 1, keepdims=False)
         got = []
@@ -729,10 +816,11 @@
         pairs = [((p ^ bit) * nx + x, p * nx + x) for p in range(nz) for x in range(nx)]
         return [kept, lax.ppermute(sent.astype(BF16), "dp", pairs)]
 
-    def summed(parts):
+    def summed(parts, one=None):
         total = parts[0].astype(F32)
         for part in parts[1:]:
-            total = total + part.astype(F32)
+            part = part.astype(F32)
+            total = total + (part if one is None else part * one[0, 0])
         return total
 
     def gather_rows(member, x, z):
@@ -826,15 +914,22 @@
         )
         scal = jnp.concatenate([lengths[0], (y * rows).reshape(1)]).astype(jnp.int32)
 
-        residual = tokens.astype(F32)
-        inverse_in = lax.rsqrt(jnp.mean(residual * residual, axis=1, keepdims=True) + EPS)
-        normed = order.done(chip_rows(core, tokens, tokens_other, halo, norm_gain))
+        normed = chip_rows(core, tokens, tokens_other, norm_gain)
+        halo = halo.astype(F32)
+        halo = halo * lax.rsqrt(jnp.mean(halo * halo, axis=1, keepdims=True) + EPS) * norm_gain
+        normed = order.done(lax.dynamic_update_slice(normed, halo.astype(BF16), (rows, 0)))
         step_rows = min(STEP_ROWS, rows)
         subs = step_rows // Q
         turns = rows // step_rows
 
         def up(columns):
             return pl.BlockSpec((step_rows, columns), lambda i, s: (i, 0))
+
+        def stay(columns):
+            return pl.BlockSpec((step_rows, columns), lambda i, s: (jnp.minimum(i, turns - 1), 0))
+
+        def stay_lanes(depth):
+            return pl.BlockSpec((depth, step_rows), lambda i, s: (0, jnp.minimum(i, turns - 1)))
 
         def up_lanes(depth):
             return pl.BlockSpec((depth, step_rows), lambda i, s: (0, i))
@@ -867,9 +962,9 @@
         def behind_rows(columns):
             return pl.BlockSpec((16, columns), lambda i, s: (rows // 16, 0))
 
+        stay_total = pl.BlockSpec((subs * 8, lanes), lambda i, s: (jnp.minimum(i, turns - 1), 0))
         up_total = pl.BlockSpec((subs * 8, lanes), lambda i, s: (i, 0))
         down_total = pl.BlockSpec((subs * 8, lanes), lambda i, s: (downward(i), 0))
-        row_depth = LOG + 8
         extended = rows + Q
 
         raw_values = [order.done(dot(order.hold(normed), w_value).astype(BF16))]
@@ -878,26 +973,47 @@
         values = from_parts(w_value, value_parts)
         gate_parts = fetched(own_part(w_gate), value_parts[-1])
         raw_shared = small[:, :maps].astype(BF16)
-        bc, bct, cols, across, total = call(
+        heads_here = ny * heads
+        channel = np.arange(channels)
+        column = np.arange(heads * Q)
+        part_row = np.arange(lanes)[:, None]
+        picks, spreads, spread_rows = [], [], []
+        for j in blocks:
+            mine = (j * heads + channel // HEAD)[None, :]
+            picks.append(jnp.asarray((part_row == mine).T, BF16))
+            spreads.append(jnp.asarray((part_row % 32 == mine) & (part_row < 96), BF16))
+            mine = (j * heads + column // Q)[None, :]
+            spread_rows.append(jnp.asarray((part_row % 32 == mine) & (part_row < 96), BF16))
+        bc, bct, cols, logs, steps, marks, across, total, _ = call(
             partial(prepare_kernel, subs),
             turns,
             [up(maps), up(lanes), behind_rows(maps), whole((8, maps)), whole((8, lanes))],
-            [up(maps), up_lanes(maps), up(lanes), up_groups(row_depth, Q), up_total],
+            [
+                up(maps),
+                up_lanes(maps),
+                up(lanes),
+                up(lanes),
+                up(lanes),
+                up_groups(40, Q),
+                up_groups(16, heads_here * Q),
+                up_total,
+            ],
             [
                 shape_of((rows, maps), BF16),
                 shape_of((maps, rows), BF16),
                 shape_of((rows, lanes), F32),
-                shape_of((groups, row_depth, Q), F32),
+                shape_of((rows, lanes), BF16),
+                shape_of((rows, lanes), BF16),
+                shape_of((groups, 40, Q), F32),
+                shape_of((groups, 16, heads_here * Q), BF16),
                 shape_of((groups * 8, lanes), F32),
             ],
-            [pltpu.VMEM((Q + 8, maps), F32), pltpu.VMEM((8, lanes), F32)],
+            [pltpu.VMEM((16, maps), BF16), pltpu.VMEM((8, lanes), F32)],
             "prepare",
-            rows * 2000,
             (scal, raw_shared, small[:, maps:], raw_shared, shared_taps, head_rows),
         )
         order.done(total)
 
-        flops_scan = rows * channels * 2 * 600
         acts, slopes, states, finals, throughs = [], [], [], [], []
         for j in blocks:
             if j == 1:
@@ -910,14 +1026,18 @@
             if j == 1:
                 raw_gates = [order.done(dot(order.hold(normed), w_gate).astype(BF16))]
             raw = raw_values[j]
-            act, slope, state, final, through = call(
+            act, slope, state, final, through, _ = call(
                 partial(states_kernel, subs, j * heads),
                 turns,
                 [
                     up(channels),
                     behind_rows(channels),
                     whole((8, channels)),
+                    whole((lanes, channels)),
                     up(lanes),
+                    up(lanes),
+                    up(lanes),
+                    up_groups(40, Q),
                     up_lanes(maps),
                     up_total,
                 ],
@@ -935,10 +1055,10 @@
                     shape_of((STATE, channels), F32),
                     shape_of((8, channels), F32),
                 ],
-                [pltpu.VMEM((Q + 8, channels), F32), pltpu.VMEM((STATE, channels), F32)],
+                [pltpu.VMEM((16, channels), BF16), pltpu.VMEM((STATE, channels), F32)],
                 "states",
-                flops_scan // 2,
-                (scal, order.hold(raw), raw, packs[j], cols, bct, total),
+                (scal, order.hold(raw), raw, packs[j], spreads[j], cols, logs, steps, marks, bct, total),
+                gate_parts if j == 1 else (),
             )
             order.done(final)
             if j == 0:
@@ -968,14 +1088,19 @@
                 raw_gates.append(order.done(dot(order.hold(normed), gates[j]).astype(BF16)))
                 backs.append(order.done(dot(order.hold(back_rows), outs[j], NT).astype(BF16)))
             raw_gate, back = raw_gates[j], backs[j]
-            scanned, stat = call(
+            scanned, stat, _ = call(
                 partial(scan_kernel, subs, j * heads),
                 turns,
                 [
                     up(channels),
                     up(maps),
                     up(lanes),
-                    up_groups(row_depth, Q),
+                    up(lanes),
+                    up(lanes),
+                    up_groups(40, Q),
+                    pl.BlockSpec((subs, 16, heads * Q), lambda i, s, j=j: (i, 0, j)),
+                    whole((lanes, channels)),
+                    whole((lanes, heads * Q)),
                     up_total,
                     up(channels),
                     up(channels),
@@ -985,11 +1110,11 @@
                 ],
                 [up(channels), up_lanes(8)],
                 [shape_of((rows, channels), F32), shape_of((8, rows), F32)],
-                [],
+                [pltpu.VMEM((lanes, heads * Q), BF16)],
                 "scan",
-                flops_scan,
-                (scal, order.hold(acts[j]), bc, cols, across, total, raw_gate, back, states[j], starts[j],
-                 packs[j]),
+                (scal, order.hold(acts[j]), bc, cols, logs, steps, marks, across, spreads[j], spread_rows[j],
+                 total, raw_gate, back, states[j], starts[j], packs[j]),
+                out_parts if j == 0 else (),
             )
             scans.append(order.done(scanned))
             stats.append(stat)
@@ -999,27 +1124,29 @@
 
         mixeds, low_gates, back_heads, reaching, gate_sums = ([None] * ny for _ in range(5))
         for j in blocks:
-            mixed, low_gate, back_head, reach, sums = call(
-                partial(gate_back_kernel, subs, j * heads, inner),
-                turns,
+            mixed, low_gate, back_head, reach, sums, _ = call(
+                partial(gate_back_kernel, subs, turns, j * heads, inner),
+                turns + 1,
                 [
-                    up(channels),
-                    up(channels),
-                    up(channels),
-                    up(channels),
-                    up_lanes(8),
-                    up_lanes(maps),
-                    up(lanes),
-                    up_total,
+                    stay(channels),
+                    stay(channels),
+                    stay(channels),
+                    stay(channels),
+                    stay_lanes(8),
+                    stay_lanes(maps),
+                    stay(lanes),
+                    stay(lanes),
+                    whole((lanes, channels)),
+                    stay_total,
                     whole((8, channels)),
                 ],
-                [up(channels)] * 3 + [whole((STATE, channels)), whole((8, channels))],
-                [shape_of((rows, channels), BF16)] * 3
+                [stay(channels), up(channels), stay(channels)] + [whole((STATE, channels)), whole((8, channels))],
+                [shape_of((m, channels), BF16) for m in (rows, extended, rows)]
                 + [shape_of((STATE, channels), F32), shape_of((8, channels), F32)],
                 [],
                 "gate_back",
-                flops_scan // 2,
-                (scal, scans[j], order.hold(acts[j]), raw_gates[j], backs[j], stat, bct, cols, total, packs[j]),
+                (scal, scans[j], order.hold(acts[j]), raw_gates[j], backs[j], stat, bct, cols, logs,
+                 spreads[j], total, packs[j]),
             )
             mixeds[j], low_gates[j], back_heads[j] = mixed, low_gate, back_head
             reaching[j], gate_sums[j] = order.done(reach), sums
@@ -1037,19 +1164,15 @@
             out_blocks[j] = after(out_blocks[j], leavings[-1])
         out_got = [from_y(out_blocks[j], ny - j) for j in range(1, ny)]
         for j in reversed(blocks):
-            gate_blocks[j] = order.done(dot(order.hold(normed[:rows]), low_gates[j], TN).astype(BF16))
+            gate_blocks[j] = order.done(dot(order.hold(normed), low_gates[j], TN).astype(BF16))
         gate_ways = [ways_x(scattered(b), x) for b in gate_blocks]
         out_blocks[0] = order.done(dot(order.hold(back_rows), mixeds[0], TN).astype(BF16))
         ahead = (1 - core) * own_rows
 
-        channel = np.arange(channels)
         low_values, back_bcs, low_rates, conv_sums, head_sums_ = [None] * ny, [], [], [None] * ny, []
         value_blocks = [None] * ny
         for j in reversed(blocks):
-            picks = jnp.asarray(
-                (np.arange(lanes)[None, :] == (j * heads + channel // HEAD)[:, None]), BF16
-            )
-            low, back_bc, low_rate, sums, head_out, first_rows, last_rows = call(
+            low, back_bc, low_rate, sums, head_out, first_rows, last_rows, scan_one = call(
                 partial(scan_back_kernel, subs, j * heads),
                 turns + 1,
                 [
@@ -1058,14 +1181,18 @@
                     down(channels),
                     down(channels),
                     down(channels),
-                    down_before(channels),
                     behind_rows(channels),
                     whole((8, channels)),
                     whole((channels, lanes)),
                     down(maps),
                     down_lanes(maps),
                     down(lanes),
-                    down_groups(row_depth, Q),
+                    down(lanes),
+                    down(lanes),
+                    down_groups(40, Q),
+                    pl.BlockSpec((subs, 16, heads * Q), lambda i, s, j=j: (downward(i), 0, j)),
+                    whole((lanes, channels)),
+                    whole((lanes, heads * Q)),
                     down_total,
                     whole((8, lanes)),
                     down_groups(STATE, channels),
@@ -1091,16 +1218,16 @@
                     shape_of((8, channels), F32),
                 ],
                 [
-                    pltpu.VMEM((Q + 8, channels), F32),
-                    pltpu.VMEM((Q + 8, channels), F32),
+                    pltpu.VMEM((16, channels), BF16),
+                    pltpu.VMEM((Q, channels), F32),
                     pltpu.VMEM((STATE, channels), F32),
                     pltpu.VMEM((Q, channels), F32),
+                    pltpu.VMEM((lanes, heads * Q), BF16),
                 ],
                 "scan_back",
-                flops_scan * 3,
-                (scal, order.hold(acts[j]), slopes[j], back_heads[j], scans[j], raw_values[j], raw_values[j],
-                 raw_values[j], packs[j], picks, bc, bct, cols, across, total, head_rows, states[j],
-                 starts[j], leavings[j]),
+                (scal, order.hold(acts[j]), slopes[j], back_heads[j], scans[j], raw_values[j],
+                 raw_values[j], packs[j], picks[j], bc, bct, cols, logs, steps, marks, across, spreads[j],
+                 spread_rows[j], total, head_rows, states[j], starts[j], leavings[j]),
             )
             low_values[j] = (order.done(low), first_rows, last_rows)
             if j == ny - 1:
@@ -1116,8 +1243,8 @@
                 order.done(out_sum)
                 out_sent = order.done(
                     many_dots(
-                        ahead, [order.hold(m) for m in mixeds], outs, [NN] * ny, own_rows, BF16, "out_other"
-                    )
+                        ahead, [order.hold(m) for m in mixeds], outs, [NN] * ny, own_rows, "out_other"
+                    )[0]
                 )
                 out_other = from_core(out_sent)
             back_bcs.append(back_bc)
@@ -1129,17 +1256,14 @@
         later = next_y(jnp.concatenate([later[k] for k in behind], axis=1), -1)
         back_bc = sum(back_bcs[1:], back_bcs[0])
         back_bc_other = from_core(back_bc)
-        out_sum = summed([out_ways[0]] + order.holds(out_ways[1:]))
+        out_sum = summed(out_ways, scan_one)
         out_ways = ways_z(out_sum, z, 1)
-        order.done(out_sum)
-        out_kept = order.done(
-            many_dots(
-                own_start, [order.hold(m) for m in mixeds], outs, [NN] * ny, own_rows, F32, "out_own"
-            )
+        block_out, own_one = many_dots(
+            own_start, mixeds, outs, [NN] * ny, own_rows, "out_own", write_output, (tokens, out_other),
+            waits=(back_bc, out_sum),
         )
 
-        back_bc = order.hold(back_bc)
-        low_shared, shared_sums, first_rows, last_rows = call(
+        low_shared, shared_sums, first_rows, last_rows, shared_one = call(
             partial(shared_back_kernel, subs),
             turns + 1,
             [
@@ -1149,7 +1273,7 @@
                 down_before(maps),
                 behind_rows(maps),
                 whole((8, maps)),
-                down(lanes),
+                down_groups(40, Q),
             ],
             [down_extended(maps), whole((8, maps)), whole((8, maps)), whole((8, maps))],
             [
@@ -1158,32 +1282,26 @@
                 shape_of((8, maps), F32),
                 shape_of((8, maps), F32),
             ],
-            [pltpu.VMEM((Q + 8, maps), F32), pltpu.VMEM((Q + 8, maps), F32)],
+            [pltpu.VMEM((16, maps), BF16), pltpu.VMEM((16, maps), BF16)],
             "shared_back",
-            rows * 2000,
-            (scal, back_bc, back_bc_other, raw_shared, raw_shared, raw_shared, shared_taps, cols),
+            (scal, back_bc, back_bc_other, raw_shared, raw_shared, raw_shared, shared_taps, marks),
+            (own_one,),
         )
-        order.done(low_shared)
         later_shared = next_y(first_rows, -1)
         low_rate = sum(low_rates[1:], low_rates[0])
         half = maps // 2
-        cut = lax.dynamic_slice(low_shared, (0, core * half), (extended, half))
-        small_block = jnp.concatenate([cut, low_rate], axis=1)
-        value_got = order.holds(value_got)
-        value_sum = order.done(summed([dot(order.hold(normed), low_values[0][0], TN)] + value_got))
+        part = lax.dynamic_slice(low_shared, (0, core * half), (extended, half))
+        small_block = dot(normed, jnp.concatenate([part, low_rate], axis=1), TN).astype(BF16)
+        small_got = [from_y(small_block, ny - j) for j in range(1, ny)]
+        value_sum = summed([dot(normed, low_values[0][0], TN)] + value_got, shared_one)
         late_ways = ways_x(scattered(value_sum), x)
-        gate_sum = summed([gate_rows[0]] + order.holds(gate_got))
+        gate_sum = summed([gate_rows[0]] + gate_got, shared_one)
         gate_ways = ways_z(gate_sum, z, 1)
-        out_ways = out_ways[:1] + order.holds(out_ways[1:])
         bit = 2
         while bit < nz:
-            out_ways = ways_z(summed(out_ways), z, bit)
+            out_ways = ways_z(summed(out_ways, shared_one), z, bit)
             bit *= 2
-        order.done(gate_sum)
-        small_block = order.done(dot(order.hold(normed), small_block, TN).astype(BF16))
-        small_got = [from_y(small_block, ny - j) for j in range(1, ny)]
-
-        later = order.holds([later])[0]
+
         low_values = [
             joined(scal, m[0], later[:, j * channels : (j + 1) * channels], m[2], packs[j], rows)
             for j, m in enumerate(low_values)
@@ -1192,68 +1310,45 @@
 
         lefts = [low_rate] + low_gates + low_values
         rights = [all_rates] + gates + values
-        sent = order.done(
-            many_dots(
-                ahead, [order.hold(m) for m in lefts], rights, [NN] + [NT] * (2 * ny), own_rows, BF16,
-                "back_other",
-            )
+        sent, other_one = many_dots(
+            ahead, lefts, rights, [NN] + [NT] * (2 * ny), own_rows, "back_other",
+            waits=(value_sum, small_block),
         )
         back_normed_other = from_core(sent)
         small_sum = small_block[:, :half].astype(F32)
         rate_sum = small_block[:, half : half + heads].astype(F32)
-        late = summed(late_ways[:1] + order.holds(late_ways[1:]))
+        late = summed(late_ways, other_one)
         late_ways = ways_z(late, z, 1)
-        for j, got in enumerate(order.holds(small_got)):
-            got = got.astype(F32)
+        for j, got in enumerate(small_got):
+            got = got.astype(F32) * other_one[0, 0]
             at = half + (ny - 1 - j) * heads
             small_sum = small_sum + got[:, :half]
             rate_sum = rate_sum + got[:, at : at + heads]
         fill = jnp.zeros((width, lanes - heads), F32)
         least = scattered(jnp.concatenate([small_sum, rate_sum, fill], axis=1))
         least_ways = ways_x(least, x)
-        gate_ways = gate_ways[:1] + order.holds(gate_ways[1:])
         bit = 2
         while bit < nz:
-            gate_ways = ways_z(summed(gate_ways), z, bit)
+            gate_ways = ways_z(summed(gate_ways, other_one), z, bit)
             bit *= 2
-        order.done(late)
-        lefts = [order.hold(low_shared)] + lefts
-        rights = [w_shared] + rights
-        kept = order.done(
-            many_dots(
-                own_start, [order.hold(m) for m in lefts], rights, [NT, NN] + [NT] * (2 * ny), own_rows, F32,
-                "back_own",
-            )
+        tokens_grad, gain_sum, kept_one = many_dots(
+            own_start, [low_shared] + lefts, [w_shared] + rights, [NT, NN] + [NT] * (2 * ny), own_rows,
+            "back_own", write_input_gradient, (tokens, back_normed_other, cotangent, norm_gain[None]), F32,
+            ((8, width),), waits=(late, least),
         )
-        late_ways = late_ways[:1] + order.holds(late_ways[1:])
-        least = summed(least_ways[:1] + order.holds(least_ways[1:]))
-        least_ways = ways_z(least, z, 1)
+        least_ways = ways_z(summed(least_ways, kept_one), z, 1)
         bit = 2
         while bit < nz:
-            late_ways = ways_z(summed(late_ways), z, bit)
+            late_ways = ways_z(summed(late_ways, kept_one), z, bit)
             bit *= 2
-        order.done(least)
-        block_out = (residual + out_kept + out_other.astype(F32)).astype(BF16)
-        back_normed = order.hold(kept) + back_normed_other.astype(F32)
-        grad_norm = jnp.sum(back_normed * residual * inverse_in, axis=0)
-        scaled = back_normed * norm_gain
-        tokens_grad = (
-            cotangent.astype(F32)
-            + scaled * inverse_in
-            - residual
-            * (inverse_in * inverse_in * inverse_in)
-            * jnp.sum(scaled * residual, axis=1, keepdims=True)
-            / width
-        )
-
-        order.done(tokens_grad)
+        grad_norm = gain_sum[0]
 
         bit = 2
         while bit < nz:
-            least_ways = ways_z(summed(least_ways[:1] + order.holds(least_ways[1:])), z, bit)
+            least_ways = ways_z(summed(least_ways), z, bit)
             bit *= 2
-        grad_out = summed(out_ways).reshape(width // copies, channels).T
-        grad_gate = summed(gate_ways).reshape(width // copies, channels)
+        grad_out = summed(out_ways, other_one).reshape(width // copies, channels).T
+        grad_gate = summed(gate_ways, kept_one).reshape(width // copies, channels)
         grad_value = summed(late_ways).reshape(width // copies, channels)
         least = summed(least_ways).reshape(width // copies, half + lanes)
         grad_rate = least[:, half : half + heads]
@@ -1276,14 +1371,20 @@
             )
         shared_sums = jnp.where(core == 0, shared_sums, 0.0)
         alls = jnp.concatenate([shared_sums, grad_norm.reshape(-1, maps)], axis=0)
-        alls = sum_row_group(alls)
-        own = smalls[0]
+        alls = alls.reshape(-1, lanes)
+        alls = alls + from_core(alls)
+        size = smalls[0].size // lanes
+        ways = [jnp.concatenate([smalls[0].reshape(-1, lanes), alls], axis=0)]
         for j in range(1, ny):
-            own = own + order.hold(from_y(smalls[j], ny - j))
-        both = jnp.concatenate([own.reshape(-1, lanes), alls.reshape(-1, lanes)], axis=0)
-        both = sum_rows(both)
-        own = both[: own.size // lanes].reshape(own.shape)
-        alls = both[own.size // lanes :].reshape(alls.shape)
+            sent = jnp.concatenate([smalls[j].reshape(-1, lanes), alls], axis=0)
+            ways.append(from_y(sent, ny - j))
+        own = summed([way[:size] for way in ways])
+        if ny > 1:
+            ways = jnp.stack([way[size:] for way in ways])
+            alls = summed([lax.dynamic_index_in_dim(ways, (y - k) % ny, 0, False) for k in range(ny)])
+        both = sum_rows(jnp.concatenate([own, alls], axis=0))
+        own = both[:size].reshape(smalls[0].shape)
+        alls = both[size:].reshape(-1, maps)
         return (
             block_out,
             tokens_grad,

time: 657 us -> 586 us (0.89)
  waiting for transfers between devices: 69.9 us -> 42.6 us
  Pallas kernels: 277 us -> 251 us
  other arithmetic: 68.4 us -> 53.8 us
  local copies, waits for them, and re-layouts: 61.8 us -> 53.5 us
    pallas_call x16, Pallas kernels: 277 us -> 251 us  [call(): pl.pallas_call(kernel, grid_spec=pltpu.PrefetchScalarGridSpec(num_scalar_...]
    ppermute x9, waiting for transfers between devices: 27.2 us -> 9.08 us  [from_y(): return lax.ppermute(member, 'tensor', pairs)]
    sub x1 -> x0, other arithmetic: 12.6 us -> none  [shards(): cotangent.astype(F32) + scaled * inverse_in]
    ppermute x9, waiting for transfers between devices: 18 us -> 7.53 us  [from_x(): return lax.ppermute(member, 'dp', pairs)]
    ppermute x8, waiting for transfers between devices: 11.5 us -> 1.43 us  [ways_z(): return [kept, lax.ppermute(sent.astype(BF16), 'dp', pairs)]]
    ppermute x3, waiting for transfers between devices: 3.45 us -> 12.4 us  [sum_rows(): lax.ppermute(member, 'dp', [(d ^ bit, d) for d in range(copies)])]
    dot_general x14, matrix products: 104 us -> 110 us  [dot(): lax.dot_general(a, b, dims, precision=precision, preferred_element_type=F32)]
  transfers between devices with their start and end apart: 47 -> 46, of which waited for: 16 -> 14; matrix products, arithmetic and copies ran while one was open for 34% -> 36% of each run, Pallas kernels for 38% -> 38%
where the time goes in v3:
time: 586 us; the launch traced here: 575 us
  Pallas kernels  251 us (43%)
  matrix products  110 us (19%)
  starting transfers between devices  54.7 us (9%)
  other arithmetic  53.8 us (9%)
  local copies, waits for them, and re-layouts  53.5 us (9%)
  waiting for transfers between devices  42.6 us (7%)
  between operations  8.97 us (2%)
    pallas_call x16, Pallas kernels, call(): pl.pallas_call(kernel, grid_spec=pltpu.PrefetchScalarGridSpec(num_scalar_...  251 us
    dot_general x14, matrix products, dot(): lax.dot_general(a, b, dims, precision=precision, preferred_element_type=F32)  110 us
    ppermute x9, starting transfers between devices, from_y(): return lax.ppermute(member, 'tensor', pairs)  15.6 us
    add x12, other arithmetic, summed(): total = total + (part if one is None else part * one[0, 0])  15.5 us
    ppermute x6, starting transfers between devices, next_y(): return lax.ppermute(member, 'tensor', pairs)  12.7 us
    ppermute x3, waiting for transfers between devices, sum_rows(): lax.ppermute(member, 'dp', [(d ^ bit, d) for d in range(copies)])  12.4 us
  transfers between devices with their start and end apart: 46, of which 14 were waited for; matrix products, arithmetic and copies ran while one was open for 36% of the time, Pallas kernels for 38%

profile of v3, /device:TPU:0, one launch (start us, length us, event | category | flops | bytes accessed | tf_op | source)
XLA Modules:
  0.0 574.6 jit_solution(17868314631635814723)
XLA Ops:
  29.7 7.5 %chip_rows.2 = (bf16[2176,1536]{1,0:T(8,128)(2,1)}, f32[8,128]{1,0:T(8,128)}) custom-call(s32[1]{0:T(128)} %bitcast.3.scal, bf16[1024,1536]{1,0:T(8,128)(2,1)} %refs_12_.1, bf16[1024,1536]{1,0:T(8,128)(2,1)} %collective-permute-done.refs_1_, f32[1,1536]{1,0:T(1,128)} %reshape.206.refs_2_.refs_15_), custom_call_target="tpu_custom_call" | custom-call | flops 8049999872 | bytes 100000 | tf_op jit(solution)/shard_map/chip_rows/pallas_call | solution.py:696
  37.8 10.0 %convolution_convert_fusion.3.refs_0_.refs_1_.refs_4_.refs_5_ = bf16[2176,768]{1,0:T(8,128)(2,1)} fusion(bf16[2176,1536]{1,0:T(8,128)(2,1)} %fusion.24, bf16[1536,768]{1,0:T(8,128)(2,1)S(1)} %copy-done.8), kind=kOutput, calls=%fused_computation.3 | convolution fusion | flops 5135499264 | bytes 12386304 | tf_op jit(solution)/shard_map/dot_general | solution.py:35
  57.6 10.4 %prepare.1 = (bf16[2048,256]{1,0:T(8,128)(2,1)}, bf16[256,2048]{1,0:T(8,128)(2,1)}, f32[2048,128]{1,0:T(8,128)}, bf16[2048,128]{1,0:T(8,128)(2,1)}, bf16[2048,12...) custom-call(s32[5]{0:T(128)} %pad_add_fusion.scal, ...), custom_call_target="tpu_custom_call" | custom-call | flops 11500000256 | bytes 100000 | tf_op jit(solution)/shard_map/prepare/pallas_call | solution.py:696
  68.0 13.4 %states.2 = (bf16[2048,768]{1,0:T(8,128)(2,1)}, bf16[2048,768]{1,0:T(8,128)(2,1)}, bf16[16,128,768]{2,1,0:T(8,128)(2,1)}, f32[128,768]{1,0:T(8,128)}, f32[8,768]{1,0:T(8,128)}, /*index=5*/f32[8,128]{1,0:T(8,128)}) custom-call(s32[5]{0:T(128)} %pad_add_fusion.scal, bf16[2176,768]{1,0:T(8,128)(2,1)} %convolution_convert_fusion.3.refs_0_.refs_1_.refs_4_.refs_5_, ...), custom_call_target="tpu_custom_call" | custom-call | flops 14949999616 | bytes 100000 | tf_op jit(solution)/shard_map/states/pallas_call | solution.py:696
  82.2 7.4 %chip_rows.3 = (bf16[2048,1536]{1,0:T(8,128)(2,1)}, f32[8,128]{1,0:T(8,128)}) custom-call(s32[1]{0:T(128)} %bitcast.3.scal, bf16[1024,1536]{1,0:T(8,128)(2,1)} %refs_14_.1, bf16[1024,1536]{1,0:T(8,128)(2,1)} %collective-permute-done.4.refs_1_), custom_call_target="tpu_custom_call" | custom-call | flops 8049999872 | bytes 100000 | tf_op jit(solution)/shard_map/chip_rows/pallas_call | solution.py:696
  92.9 9.9 %convolution_convert_fusion.2.refs_0_.refs_1_.refs_4_.refs_5_ = bf16[2176,768]{1,0:T(8,128)(2,1)} fusion(bf16[2176,1536]{1,0:T(8,128)(2,1)} %fusion.24, bf16[1536,768]{1,0:T(8,128)(2,1)S(1)} %constant_dynamic-update-slice_fusion.5.refs_9_.refs_11_), kind=kOutput, calls=%fused_computation.2 | convolution fusion | flops 5135499264 | bytes 12386304 | tf_op jit(solution)/shard_map/dot_general | solution.py:35
  102.8 6.7 %convolution_convert_fusion.1.refs_10_.refs_2_ = bf16[2176,768]{1,0:T(8,128)(2,1)} fusion(bf16[2176,1536]{1,0:T(8,128)(2,1)S(1)} %bitcast.228, bf16[1536,768]{1,0:T(8,128)(2,1)S(1)} %copy-done.9), kind=kOutput, calls=%fused_computation.1 | convolution fusion | flops 5135499264 | bytes 12386304 | tf_op jit(solution)/shard_map/dot_general | solution.py:35
  109.5 13.4 %states.3 = (bf16[2048,768]{1,0:T(8,128)(2,1)}, bf16[2048,768]{1,0:T(8,128)(2,1)}, bf16[16,128,768]{2,1,0:T(8,128)(2,1)}, f32[128,768]{1,0:T(8,128)}, f32[8,768]{1,0:T(8,128)}, /*index=5*/f32[8,128]{1,0:T(8,128)}) custom-call(s32[5]{0:T(128)} %pad_add_fusion.scal, bf16[2176,768]{1,0:T(8,128)(2,1)} %convolution_convert_fusion.2.refs_0_.refs_1_.refs_4_.refs_5_, ...), custom_call_target="tpu_custom_call" | custom-call | flops 14949999616 | bytes 100000 | tf_op jit(solution)/shard_map/states/pallas_call | solution.py:696
  127.0 9.7 %convolution_convert_fusion.10.refs_11_.refs_3_ = bf16[2048,768]{1,0:T(8,128)(2,1)} fusion(bf16[2048,1536]{1,0:T(8,128)(2,1)} %get-tuple-element.167, bf16[768,1536]{1,0:T(8,128)(2,1)S(1)} %copy-done.5), kind=kOutput, calls=%fused_computation.12 | convolution fusion | flops 4833411072 | bytes 11796480 | tf_op jit(solution)/shard_map/dot_general | solution.py:35
  143.5 14.5 %scan.2 = (f32[2048,768]{1,0:T(8,128)}, f32[8,2048]{1,0:T(8,128)}, f32[8,128]{1,0:T(8,128)}) custom-call(s32[5]{0:T(128)} %pad_add_fusion.scal, bf16[2048,768]{1,0:T(8,128)(2,1)} %get-tuple-element.180.refs_0_.refs_1_, bf16[2048,256]{1,0:T(8,128)(2,1)} %get-tuple-element.130.refs_1_.refs_8_, f32[2048,128]{1,0:T(8,128)} %get-tuple-element.119.refs_4_.refs_2_.refs_6_.refs_10_, ...), custom_call_target="tpu_custom_call" | custom-call | flops 17250000896 | bytes 100000 | tf_op jit(solution)/shard_map/scan/pallas_call | solution.py:696
  159.6 10.7 %convolution_convert_fusion.refs_10_.refs_2_ = bf16[2176,768]{1,0:T(8,128)(2,1)} fusion(bf16[2176,1536]{1,0:T(8,128)(2,1)} %fusion.24, bf16[1536,768]{1,0:T(8,128)(2,1)S(1)} %constant_dynamic-update-slice_fusion.3.refs_7_.refs_9_), kind=kOutput, calls=%fused_computation | convolution fusion | flops 5135499264 | bytes 12386304 | tf_op jit(solution)/shard_map/dot_general | solution.py:35
  171.8 6.5 %convolution_convert_fusion.9.refs_11_.refs_3_ = bf16[2048,768]{1,0:T(8,128)(2,1)} fusion(bf16[2048,1536]{1,0:T(8,128)(2,1)S(1)} %bitcast.234, bf16[768,1536]{1,0:T(8,128)(2,1)S(1)} %constant_dynamic-update-slice_fusion.1.refs_3_), kind=kOutput, calls=%fused_computation.11 | convolution fusion | flops 4833411072 | bytes 11796480 | tf_op jit(solution)/shard_map/dot_general | solution.py:35
  178.3 14.6 %scan.3 = (f32[2048,768]{1,0:T(8,128)}, f32[8,2048]{1,0:T(8,128)}, f32[8,128]{1,0:T(8,128)}) custom-call(s32[5]{0:T(128)} %pad_add_fusion.scal, bf16[2048,768]{1,0:T(8,128)(2,1)} %get-tuple-element.169.refs_0_.refs_1_, bf16[2048,256]{1,0:T(8,128)(2,1)} %get-tuple-element.130.refs_1_.refs_8_, f32[2048,128]{1,0:T(8,128)} %get-tuple-element.119.refs_4_.refs_2_.refs_6_.refs_10_, ...), custom_call_target="tpu_custom_call" | custom-call | flops 17250000896 | bytes 100000 | tf_op jit(solution)/shard_map/scan/pallas_call | solution.py:696
  203.4 15.9 %gate_back.2 = (bf16[2048,768]{1,0:T(8,128)(2,1)}, bf16[2176,768]{1,0:T(8,128)(2,1)}, bf16[2048,768]{1,0:T(8,128)(2,1)}, f32[128,768]{1,0:T(8,128)}, f32[8,768]{1,0:T(8,128)}, /*index=5*/f32[8,128]{1,0:T(8,128)}) custom-call(s32[5]{0:T(128)} %pad_add_fusion.scal, f32[2048,768]{1,0:T(8,128)} %get-tuple-element.145.refs_0_.refs_3_, ...), custom_call_target="tpu_custom_call" | custom-call | flops 18400000000 | bytes 100000 | tf_op jit(solution)/shard_map/gate_back/pallas_call | solution.py:696
  220.7 15.9 %gate_back.3 = (bf16[2048,768]{1,0:T(8,128)(2,1)}, bf16[2176,768]{1,0:T(8,128)(2,1)}, bf16[2048,768]{1,0:T(8,128)(2,1)}, f32[128,768]{1,0:T(8,128)}, f32[8,768]{1,0:T(8,128)}, /*index=5*/f32[8,128]{1,0:T(8,128)}) custom-call(s32[5]{0:T(128)} %pad_add_fusion.scal, f32[2048,768]{1,0:T(8,128)} %get-tuple-element.153.refs_0_.refs_3_, ...), custom_call_target="tpu_custom_call" | custom-call | flops 18400000000 | bytes 100000 | tf_op jit(solution)/shard_map/gate_back/pallas_call | solution.py:696
  239.1 9.4 %convolution_convert_fusion.8 = bf16[1536,768]{1,0:T(8,128)(2,1)} fusion(bf16[2048,1536]{1,0:T(8,128)(2,1)} %get-tuple-element.167, bf16[2048,768]{1,0:T(8,128)(2,1)} %get-tuple-element.177.refs_1_), kind=kOutput, calls=%fused_computation.10 | convolution fusion | flops 4833017856 | bytes 11796480 | tf_op jit(solution)/shard_map/dot_general | solution.py:35
  248.5 8.1 %convolution_convert_fusion.7 = bf16[1536,768]{1,0:T(8,128)(2,1)S(1)} fusion(bf16[2176,1536]{1,0:T(8,128)(2,1)} %fusion.24, bf16[2176,768]{1,0:T(8,128)(2,1)S(1)} %copy-done.60), kind=kOutput, calls=%fused_computation.9 | convolution fusion | flops 5135007744 | bytes 12386304 | tf_op jit(solution)/shard_map/dot_general | solution.py:35
  259.6 6.0 %convolution_convert_fusion.6 = bf16[1536,768]{1,0:T(8,128)(2,1)S(1)} fusion(bf16[2176,1536]{1,0:T(8,128)(2,1)S(1)} %bitcast.230, bf16[2176,768]{1,0:T(8,128)(2,1)S(1)} %copy-done.59), kind=kOutput, calls=%fused_computation.8 | convolution fusion | flops 5135007744 | bytes 12386304 | tf_op jit(solution)/shard_map/dot_general | solution.py:35
  265.7 6.4 %convolution_convert_fusion.5 = bf16[1536,768]{1,0:T(8,128)(2,1)} fusion(bf16[2048,1536]{1,0:T(8,128)(2,1)S(1)} %bitcast.236, bf16[2048,768]{1,0:T(8,128)(2,1)S(1)} %copy-done.58), kind=kOutput, calls=%fused_computation.7 | convolution fusion | flops 4833017856 | bytes 11796480 | tf_op jit(solution)/shard_map/dot_general | solution.py:35
  275.9 33.3 %scan_back.2 = (bf16[2176,768]{1,0:T(8,128)(2,1)}, f32[2048,256]{1,0:T(8,128)}, bf16[2176,128]{1,0:T(8,128)(2,1)}, f32[8,768]{1,0:T(8,128)}, f32[8,128]{1,0:T(8,...) custom-call(s32[5]{0:T(128)} %pad_add_fusion.scal, ...), custom_call_target="tpu_custom_call" | custom-call | flops 37950001152 | bytes 100000 | tf_op jit(solution)/shard_map/scan_back/pallas_call | solution.py:696
  313.7 9.0 %convolution_convert_fusion.4 = bf16[1536,768]{1,0:T(8,128)(2,1)} fusion(bf16[2176,1536]{1,0:T(8,128)(2,1)} %fusion.24, bf16[2176,768]{1,0:T(8,128)(2,1)S(1)} %copy-done.53), kind=kOutput, calls=%fused_computation.6 | convolution fusion | flops 5135007744 | bytes 12386304 | tf_op jit(solution)/shard_map/dot_general | solution.py:35
  330.7 11.0 %out_other.1 = (bf16[1024,1536]{1,0:T(8,128)(2,1)}, f32[8,128]{1,0:T(8,128)}) custom-call(s32[1]{0:T(128)} %bitcast.15.scal, bf16[2048,768]{1,0:T(8,128)(2,1)} %get-tuple-element.176.refs_0_, bf16[2048,768]{1,0:T(8,128)(2,1)} %get-tuple-element.177.refs_1_, bf16[768,1536]{1,0:T(8,128)(2,1)} %refs_2_.3, bf16[768,1536]{1,0:T(8,128)(2,1)} %copy-done.15), custom_call_target="tpu_custom_call" | custom-call | flops 10350000128 | bytes 100000 | tf_op jit(solution)/shard_map/out_other/pallas_call | solution.py:696
  343.7 33.1 %scan_back.3 = (bf16[2176,768]{1,0:T(8,128)(2,1)}, f32[2048,256]{1,0:T(8,128)}, bf16[2176,128]{1,0:T(8,128)(2,1)}, f32[8,768]{1,0:T(8,128)}, f32[8,128]{1,0:T(8,...) custom-call(s32[5]{0:T(128)} %pad_add_fusion.scal, ...), custom_call_target="tpu_custom_call" | custom-call | flops 37950001152 | bytes 100000 | tf_op jit(solution)/shard_map/scan_back/pallas_call | solution.py:696
  405.1 10.5 %out_own.1 = (bf16[1024,1536]{1,0:T(8,128)(2,1)}, f32[8,128]{1,0:T(8,128)}) custom-call(s32[1]{0:T(128)} %bitcast.scal, bf16[2048,768]{1,0:T(8,128)(2,1)} %get-tuple-element.176.refs_0_, bf16[2048,768]{1,0:T(8,128)(2,1)} %get-tuple-element.177.refs_1_, bf16[768,1536]{1,0:T(8,128)(2,1)} %refs_2_.3, bf16[768,1536]{1,0:T(8,128)(2,1)} %copy-done.15, ...), custom_call_target="tpu_custom_call" | custom-call | flops 12650000384 | bytes 100000 | tf_op jit(solution)/shard_map/out_own/pallas_call | solution.py:696
  415.5 9.8 %shared_back.1 = (bf16[2176,256]{1,0:T(8,128)(2,1)}, f32[8,256]{1,0:T(8,128)}, f32[8,256]{1,0:T(8,128)}, f32[8,256]{1,0:T(8,128)}, f32[8,128]{1,0:T(8,128)}) custom-call(s32[5]{0:T(128)} %pad_add_fusion.scal, f32[2048,256]{1,0:T(8,128)} %add.305.refs_6_.refs_0_, f32[2048,256]{1,0:T(8,128)} %collective-permute-done.19.refs_1_, ...), custom_call_target="tpu_custom_call" | custom-call | flops 11500000256 | bytes 100000 | tf_op jit(solution)/shard_map/shared_back/pallas_call | solution.py:696
  435.5 6.0 %convolution_convert_fusion.11.refs_11_ = bf16[1536,256]{1,0:T(8,128)(2,1)} fusion(bf16[2176,1536]{1,0:T(8,128)(2,1)} %fusion.24, bf16[2176,128]{1,0:T(8,128)(2,1)S(1)} %copy-done.22, bf16[2176,128]{1,0:T(8,128)(2,1)S(1)} %constant_dynamic-slice_fusion), kind=kOutput, calls=%fused_computation.13 | convolution fusion | flops 1713897472 | bytes 8585216 | tf_op jit(solution)/shard_map/dot_general | solution.py:35
  444.7 8.1 %multiply_add_fusion.refs_10_ = f32[1536,768]{1,0:T(8,128)S(1)} fusion(bf16[1536,768]{1,0:T(8,128)(2,1)} %collective-permute-done.22, bf16[2176,1536]{1,0:T(8,128)(2,1)S(1)} %bitcast.232, bf16[2176,768]{1,0:T(8,128)(2,1)S(1)} %copy-done.54, f32[]{:T(128)} %bitcast.27), kind=kOutput, calls=%fused_computation.4 | convolution fusion | flops 5137367040 | bytes 17104900 | tf_op jit(solution)/shard_map/dot_general | solution.py:35
  457.2 17.4 %back_other.1 = (bf16[1024,1536]{1,0:T(8,128)(2,1)}, f32[8,128]{1,0:T(8,128)}) custom-call(s32[1]{0:T(128)} %bitcast.15.scal, bf16[2176,128]{1,0:T(8,128)(2,1)} %add.641.refs_0_.refs_1_, bf16[2176,768]{1,0:T(8,128)(2,1)} %get-tuple-element.166.refs_1_.refs_2_, bf16[2176,768]{1,0:T(8,128)(2,1)} %get-tuple-element.164.refs_2_.refs_3_, ...), custom_call_target="tpu_custom_call" | custom-call | flops 19549999104 | bytes 100000 | tf_op jit(solution)/shard_map/back_other/pallas_call | solution.py:696
  494.1 22.7 %back_own.1 = (f32[1024,1536]{1,0:T(8,128)}, f32[8,1536]{1,0:T(8,128)}, f32[8,128]{1,0:T(8,128)}) custom-call(s32[1]{0:T(128)} %bitcast.scal, bf16[2176,256]{1,0:T(8,128)(2,1)} %constant_dynamic-update-slice_fusion.refs_0_, bf16[2176,128]{1,0:T(8,128)(2,1)} %add.641.refs_0_.refs_1_, bf16[2176,768]{1,0:T(8,128)(2,1)} %get-tuple-element.166.refs_1_.refs_2_, ...), custom_call_target="tpu_custom_call" | custom-call | flops 25300000768 | bytes 100000 | tf_op jit(solution)/shard_map/back_own/pallas_call | solution.py:696
  542.4 10.5 %collective-permute-done.30 = f32[76,128]{1,0:T(8,128)S(1)} collective-permute-done((f32[76,128]{1,0:T(8,128)S(1)}, f32[76,128]{1,0:T(8,128)S(1)}, u32[]{:S(2)}, u32[]{:S(2)}) %collective-permute-start.30) | collective-permute-done | bytes 38944 | tf_op jit(solution)/shard_map/ppermute | solution.py:799
  555.0 4.8 collective-permute-done.40
  565.7 4.6 collective-permute-done.42
  (397 shorter events, 188.4 us)
Async XLA Ops:
  0.6 29.0 %collective-permute-start = (bf16[1024,1536]{1,0:T(8,128)(2,1)}, bf16[1024,1536]{1,0:T(8,128)(2,1)}, u32[]{:S(2)}, u32[]{:S(2)}) collective-permute-start(bf16[1024,1536]{1,0:T(8,128)(2,1)} %refs_12_.1), channel_id=1, source_target_pairs={{1,0},{0,1},{3,2},{2,3},{5,4},{4,5},{7,6},{6,7},{9,8},{8,9},{11,10... | collective-permute-start | bytes 9437192 | tf_op jit(solution)/shard_map/ppermute | solution.py:786
  2.0 18.8 %collective-permute-start.1 = (bf16[16,1536]{1,0:T(8,128)(2,1)S(1)}, bf16[16,1536]{1,0:T(8,128)(2,1)S(1)}, u32[]{:S(2)}, u32[]{:S(2)}) collective-permute-start(bf16[16,1536]{1,0:T(8,128)(2,1)S(1)} %slice.168), channel_id=1, source_target_pairs={{0,2},{1,3},{4,6},{5,7},{8,10},{9,11},{12,14},{13,15},{16,18},{17,... | collective-permute-start | bytes 147464 | tf_op jit(solution)/shard_map/ppermute | solution.py:783
  27.9 27.6 %collective-permute-start.5 = (bf16[768,768]{1,0:T(8,128)(2,1)}, bf16[768,768]{1,0:T(8,128)(2,1)S(1)}, u32[]{:S(2)}, u32[]{:S(2)}) collective-permute-start(bf16[768,768]{1,0:T(8,128)(2,1)} %constant_dynamic-slice_fusion.2), channel_id=1, source_target_pairs={{2,0},{3,1},{0,2},{1,3},{6,4},{7,5},{4,6},{5,7},{10,8},{11,9},{8,1... | collective-permute-start | bytes 3538952 | tf_op jit(solution)/shard_map/ppermute | solution.py:774
  29.7 52.5 %collective-permute-start.4 = (bf16[1024,1536]{1,0:T(8,128)(2,1)}, bf16[1024,1536]{1,0:T(8,128)(2,1)}, u32[]{:S(2)}, u32[]{:S(2)}) collective-permute-start(bf16[1024,1536]{1,0:T(8,128)(2,1)} %refs_14_.1), channel_id=1, source_target_pairs={{1,0},{0,1},{3,2},{2,3},{5,4},{4,5},{7,6},{6,7},{9,8},{8,9},{11,10... | collective-permute-start | bytes 9437192 | tf_op jit(solution)/shard_map/ppermute | solution.py:786
  55.5 26.5 %collective-permute-start.7 = (bf16[768,768]{1,0:T(8,128)(2,1)S(1)}, bf16[768,768]{1,0:T(8,128)(2,1)S(1)}, u32[]{:S(2)}, u32[]{:S(2)}) collective-permute-start(bf16[768,768]{1,0:T(8,128)(2,1)S(1)} %collective-permute-done.5), channel_id=1, source_target_pairs={{4,0},{0,4},{12,8},{8,12},{20,16},{16,20},{28,24},{24,28},{5,1},{1... | collective-permute-start | bytes 3538952 | tf_op jit(solution)/shard_map/ppermute | solution.py:790
  57.0 32.5 %collective-permute-start.6 = (bf16[768,768]{1,0:T(8,128)(2,1)}, bf16[768,768]{1,0:T(8,128)(2,1)}, u32[]{:S(2)}, u32[]{:S(2)}) collective-permute-start(bf16[768,768]{1,0:T(8,128)(2,1)} %constant_dynamic-slice_fusion.3), channel_id=1, source_target_pairs={{2,0},{3,1},{0,2},{1,3},{6,4},{7,5},{4,6},{5,7},{10,8},{11,9},{8,1... | collective-permute-start | bytes 3538952 | tf_op jit(solution)/shard_map/ppermute | solution.py:774
  89.5 68.4 %collective-permute-start.10 = (bf16[768,768]{1,0:T(8,128)(2,1)}, bf16[768,768]{1,0:T(8,128)(2,1)}, u32[]{:S(2)}, u32[]{:S(2)}) collective-permute-start(bf16[768,768]{1,0:T(8,128)(2,1)} %collective-permute-done.6.refs_10_), channel_id=1, source_target_pairs={{4,0},{0,4},{12,8},{8,12},{20,16},{16,20},{28,24},{24,28},{5,1},{1... | collective-permute-start | bytes 3538952 | tf_op jit(solution)/shard_map/ppermute | solution.py:790
  91.1 52.3 %collective-permute-start.9 = (bf16[384,1536]{1,0:T(8,128)(2,1)S(1)}, bf16[384,1536]{1,0:T(8,128)(2,1)}, u32[]{:S(2)}, u32[]{:S(2)}) collective-permute-start(bf16[384,1536]{1,0:T(8,128)(2,1)S(1)} %copy-done.21), channel_id=1, source_target_pairs={{2,0},{3,1},{0,2},{1,3},{6,4},{7,5},{4,6},{5,7},{10,8},{11,9},{8,1... | collective-permute-start | bytes 3538952 | tf_op jit(solution)/shard_map/ppermute | solution.py:774
  124.0 18.4 %collective-permute-start.8 = (f32[256,768]{1,0:T(8,128)S(1)}, f32[256,768]{1,0:T(8,128)S(1)}, u32[]{:S(2)}, u32[]{:S(2)}) collective-permute-start(f32[256,768]{1,0:T(8,128)S(1)} %pad_maximum_fusion), channel_id=1, source_target_pairs={{0,2},{1,3},{4,6},{5,7},{8,10},{9,11},{12,14},{13,15},{16,18},{17,... | collective-permute-start | bytes 2359304 | tf_op jit(solution)/shard_map/ppermute | solution.py:783
  143.4 28.3 %collective-permute-start.11 = (bf16[384,1536]{1,0:T(8,128)(2,1)}, bf16[384,1536]{1,0:T(8,128)(2,1)S(1)}, u32[]{:S(2)}, u32[]{:S(2)}) collective-permute-start(bf16[384,1536]{1,0:T(8,128)(2,1)} %collective-permute-done.9.refs_15_), channel_id=1, source_target_pairs={{4,0},{0,4},{12,8},{8,12},{20,16},{16,20},{28,24},{24,28},{5,1},{1... | collective-permute-start | bytes 3538952 | tf_op jit(solution)/shard_map/ppermute | solution.py:790
  219.4 53.1 %collective-permute-start.13 = (f32[128,768]{1,0:T(8,128)}, f32[128,768]{1,0:T(8,128)S(1)}, u32[]{:S(2)}, u32[]{:S(2)}) collective-permute-start(f32[128,768]{1,0:T(8,128)} %get-tuple-element.158), channel_id=1, source_target_pairs={{2,0},{3,1},{6,4},{7,5},{10,8},{11,9},{14,12},{15,13},{18,16},{19,... | collective-permute-start | bytes 1179656 | tf_op jit(solution)/shard_map/ppermute | solution.py:783
  236.5 107.2 %collective-permute-start.17 = (f32[128,768]{1,0:T(8,128)}, f32[128,768]{1,0:T(8,128)}, u32[]{:S(2)}, u32[]{:S(2)}) collective-permute-start(f32[128,768]{1,0:T(8,128)} %get-tuple-element.161), channel_id=1, source_target_pairs={{2,0},{3,1},{6,4},{7,5},{10,8},{11,9},{14,12},{15,13},{18,16},{19,... | collective-permute-start | bytes 1179656 | tf_op jit(solution)/shard_map/ppermute | solution.py:783
  257.7 68.1 %collective-permute-start.31 = (bf16[4,192,768]{2,1,0:T(8,128)(2,1)}, bf16[4,192,768]{2,1,0:T(8,128)(2,1)}, u32[]{:S(2)}, u32[]{:S(2)}) collective-permute-start(bf16[4,192,768]{2,1,0:T(8,128)(2,1)} %dynamic-slice_bitcast_fusion), channel_id=1, source_target_pairs={{4,0},{0,4},{12,8},{8,12},{20,16},{16,20},{28,24},{24,28},{5,1},{1... | collective-permute-start | bytes 3538952 | tf_op jit(solution)/shard_map/ppermute | solution.py:790
  272.2 39.5 %collective-permute-start.15 = (bf16[4,192,768]{2,1,0:T(8,128)(2,1)S(1)}, bf16[4,192,768]{2,1,0:T(8,128)(2,1)S(1)}, u32[]{:S(2)}, u32[]{:S(2)}) collective-permute-start(bf16[4,192,768]{2,1,0:T(8,128)(2,1)S(1)} %dynamic-slice_bitcast_fusion.1), channel_id=1, source_target_pairs={{4,0},{0,4},{12,8},{8,12},{20,16},{16,20},{28,24},{24,28},{5,1},{1... | collective-permute-start | bytes 3538952 | tf_op jit(solution)/shard_map/ppermute | solution.py:790
  272.5 56.0 %collective-permute-start.14 = (bf16[1536,768]{1,0:T(8,128)(2,1)}, bf16[1536,768]{1,0:T(8,128)(2,1)}, u32[]{:S(2)}, u32[]{:S(2)}) collective-permute-start(bf16[1536,768]{1,0:T(8,128)(2,1)} %convolution_convert_fusion.8), channel_id=1, source_target_pairs={{2,0},{3,1},{0,2},{1,3},{6,4},{7,5},{4,6},{5,7},{10,8},{11,9},{8,1... | collective-permute-start | bytes 7077896 | tf_op jit(solution)/shard_map/ppermute | solution.py:774
  322.6 122.1 %collective-permute-start.22 = (bf16[1536,768]{1,0:T(8,128)(2,1)}, bf16[1536,768]{1,0:T(8,128)(2,1)}, u32[]{:S(2)}, u32[]{:S(2)}) collective-permute-start(bf16[1536,768]{1,0:T(8,128)(2,1)} %convolution_convert_fusion.4), channel_id=1, source_target_pairs={{2,0},{3,1},{0,2},{1,3},{6,4},{7,5},{4,6},{5,7},{10,8},{11,9},{8,1... | collective-permute-start | bytes 7077896 | tf_op jit(solution)/shard_map/ppermute | solution.py:774
  341.7 63.4 %collective-permute-start.16 = (bf16[1024,1536]{1,0:T(8,128)(2,1)}, bf16[1024,1536]{1,0:T(8,128)(2,1)}, u32[]{:S(2)}, u32[]{:S(2)}) collective-permute-start(bf16[1024,1536]{1,0:T(8,128)(2,1)} %get-tuple-element.178), channel_id=1, source_target_pairs={{1,0},{0,1},{3,2},{2,3},{5,4},{4,5},{7,6},{6,7},{9,8},{8,9},{11,10... | collective-permute-start | bytes 9437192 | tf_op jit(solution)/shard_map/ppermute | solution.py:786
  341.9 58.4 %collective-permute-start.18 = (bf16[4,192,768]{2,1,0:T(8,128)(2,1)S(1)}, bf16[4,192,768]{2,1,0:T(8,128)(2,1)}, u32[]{:S(2)}, u32[]{:S(2)}) collective-permute-start(bf16[4,192,768]{2,1,0:T(8,128)(2,1)S(1)} %fusion.1), channel_id=1, source_target_pairs={{4,0},{0,4},{12,8},{8,12},{20,16},{16,20},{28,24},{24,28},{5,1},{1... | collective-permute-start | bytes 3538952 | tf_op jit(solution)/shard_map/ppermute | solution.py:790
  387.9 27.6 %collective-permute-start.19 = (f32[2048,256]{1,0:T(8,128)}, f32[2048,256]{1,0:T(8,128)}, u32[]{:S(2)}, u32[]{:S(2)}) collective-permute-start(f32[2048,256]{1,0:T(8,128)} %add.305.refs_6_.refs_0_), channel_id=1, source_target_pairs={{1,0},{0,1},{3,2},{2,3},{5,4},{4,5},{7,6},{6,7},{9,8},{8,9},{11,10... | collective-permute-start | bytes 6291464 | tf_op jit(solution)/shard_map/ppermute | solution.py:786
  394.9 37.3 %collective-permute-start.32 = (bf16[4,192,768]{2,1,0:T(8,128)(2,1)}, bf16[4,192,768]{2,1,0:T(8,128)(2,1)S(1)}, u32[]{:S(2)}, u32[]{:S(2)}) collective-permute-start(bf16[4,192,768]{2,1,0:T(8,128)(2,1)} %fusion), channel_id=1, source_target_pairs={{2,0},{3,1},{0,2},{1,3},{6,4},{7,5},{4,6},{5,7},{10,8},{11,9},{8,1... | collective-permute-start | bytes 3538952 | tf_op jit(solution)/shard_map/ppermute | solution.py:774
  403.4 24.7 %collective-permute-start.44 = (bf16[2,192,768]{2,1,0:T(8,128)(2,1)S(1)}, bf16[2,192,768]{2,1,0:T(8,128)(2,1)S(1)}, u32[]{:S(2)}, u32[]{:S(2)}) collective-permute-start(bf16[2,192,768]{2,1,0:T(8,128)(2,1)S(1)} %fusion.13), channel_id=1, source_target_pairs={{8,0},{12,4},{0,8},{4,12},{24,16},{28,20},{16,24},{20,28},{9,1},{1... | collective-permute-start | bytes 1769480 | tf_op jit(solution)/shard_map/ppermute | solution.py:817
  426.6 49.2 %collective-permute-start.20 = (f32[8,256]{1,0:T(8,128)}, f32[8,256]{1,0:T(8,128)}, u32[]{:S(2)}, u32[]{:S(2)}) collective-permute-start(f32[8,256]{1,0:T(8,128)} %get-tuple-element.189), channel_id=1, source_target_pairs={{2,0},{3,1},{6,4},{7,5},{10,8},{11,9},{14,12},{15,13},{18,16},{19,... | collective-permute-start | bytes 24584 | tf_op jit(solution)/shard_map/ppermute | solution.py:783
  429.6 47.6 %collective-permute-start.45 = (bf16[1,192,768]{2,1,0:T(8,128)(2,1)}, bf16[1,192,768]{2,1,0:T(8,128)(2,1)}, u32[]{:S(2)}, u32[]{:S(2)}) collective-permute-start(bf16[1,192,768]{2,1,0:T(8,128)(2,1)} %dynamic-slice_convert_fusion.2), channel_id=1, source_target_pairs={{16,0},{20,4},{24,8},{28,12},{0,16},{4,20},{8,24},{12,28},{17,1},{... | collective-permute-start | bytes 884744 | tf_op jit(solution)/shard_map/ppermute | solution.py:817
  434.2 45.6 %collective-permute-start.33 = (bf16[2,192,768]{2,1,0:T(8,128)(2,1)}, bf16[2,192,768]{2,1,0:T(8,128)(2,1)}, u32[]{:S(2)}, u32[]{:S(2)}) collective-permute-start(bf16[2,192,768]{2,1,0:T(8,128)(2,1)} %fusion.11), channel_id=1, source_target_pairs={{8,0},{12,4},{0,8},{4,12},{24,16},{28,20},{16,24},{20,28},{9,1},{1... | collective-permute-start | bytes 1769480 | tf_op jit(solution)/shard_map/ppermute | solution.py:817
  441.5 41.5 %collective-permute-start.25 = (bf16[1536,256]{1,0:T(8,128)(2,1)}, bf16[1536,256]{1,0:T(8,128)(2,1)}, u32[]{:S(2)}, u32[]{:S(2)}) collective-permute-start(bf16[1536,256]{1,0:T(8,128)(2,1)} %convolution_convert_fusion.11.refs_11_), channel_id=1, source_target_pairs={{2,0},{3,1},{0,2},{1,3},{6,4},{7,5},{4,6},{5,7},{10,8},{11,9},{8,1... | collective-permute-start | bytes 2359304 | tf_op jit(solution)/shard_map/ppermute | solution.py:774
  454.3 35.8 %collective-permute-start.24 = (bf16[4,192,768]{2,1,0:T(8,128)(2,1)}, bf16[4,192,768]{2,1,0:T(8,128)(2,1)}, u32[]{:S(2)}, u32[]{:S(2)}) collective-permute-start(bf16[4,192,768]{2,1,0:T(8,128)(2,1)} %fusion.2), channel_id=1, source_target_pairs={{4,0},{0,4},{12,8},{8,12},{20,16},{16,20},{28,24},{24,28},{5,1},{1... | collective-permute-start | bytes 3538952 | tf_op jit(solution)/shard_map/ppermute | solution.py:790
  475.8 18.3 %collective-permute-start.23 = (bf16[1024,1536]{1,0:T(8,128)(2,1)}, bf16[1024,1536]{1,0:T(8,128)(2,1)}, u32[]{:S(2)}, u32[]{:S(2)}) collective-permute-start(bf16[1024,1536]{1,0:T(8,128)(2,1)} %get-tuple-element.198), channel_id=1, source_target_pairs={{1,0},{0,1},{3,2},{2,3},{5,4},{4,5},{7,6},{6,7},{9,8},{8,9},{11,10... | collective-permute-start | bytes 9437192 | tf_op jit(solution)/shard_map/ppermute | solution.py:786
  482.7 57.2 %collective-permute-start.34 = (bf16[1,192,768]{2,1,0:T(8,128)(2,1)}, bf16[1,192,768]{2,1,0:T(8,128)(2,1)}, u32[]{:S(2)}, u32[]{:S(2)}) collective-permute-start(bf16[1,192,768]{2,1,0:T(8,128)(2,1)} %dynamic-slice_convert_fusion.4), channel_id=1, source_target_pairs={{16,0},{20,4},{24,8},{28,12},{0,16},{4,20},{8,24},{12,28},{17,1},{... | collective-permute-start | bytes 884744 | tf_op jit(solution)/shard_map/ppermute | solution.py:817
  488.4 33.3 %collective-permute-start.37 = (bf16[4,192,256]{2,1,0:T(8,128)(2,1)}, bf16[4,192,256]{2,1,0:T(8,128)(2,1)}, u32[]{:S(2)}, u32[]{:S(2)}) collective-permute-start(bf16[4,192,256]{2,1,0:T(8,128)(2,1)} %fusion.14), channel_id=1, source_target_pairs={{4,0},{0,4},{12,8},{8,12},{20,16},{16,20},{28,24},{24,28},{5,1},{1... | collective-permute-start | bytes 1179656 | tf_op jit(solution)/shard_map/ppermute | solution.py:790
  493.3 35.6 %collective-permute-start.35 = (bf16[2,192,768]{2,1,0:T(8,128)(2,1)}, bf16[2,192,768]{2,1,0:T(8,128)(2,1)}, u32[]{:S(2)}, u32[]{:S(2)}) collective-permute-start(bf16[2,192,768]{2,1,0:T(8,128)(2,1)} %fusion.12), channel_id=1, source_target_pairs={{8,0},{12,4},{0,8},{4,12},{24,16},{28,20},{16,24},{20,28},{9,1},{1... | collective-permute-start | bytes 1769480 | tf_op jit(solution)/shard_map/ppermute | solution.py:817
  533.9 37.9 %collective-permute-start.36 = (bf16[1,192,768]{2,1,0:T(8,128)(2,1)S(1)}, bf16[1,192,768]{2,1,0:T(8,128)(2,1)S(1)}, u32[]{:S(2)}, u32[]{:S(2)}) collective-permute-start(bf16[1,192,768]{2,1,0:T(8,128)(2,1)S(1)} %dynamic-slice_convert_fusion.3), channel_id=1, source_target_pairs={{16,0},{20,4},{24,8},{28,12},{0,16},{4,20},{8,24},{12,28},{17,1},{... | collective-permute-start | bytes 884744 | tf_op jit(solution)/shard_map/ppermute | solution.py:817
  536.8 16.1 %collective-permute-start.30 = (f32[76,128]{1,0:T(8,128)S(1)}, f32[76,128]{1,0:T(8,128)S(1)}, u32[]{:S(2)}, u32[]{:S(2)}) collective-permute-start(f32[76,128]{1,0:T(8,128)S(1)} %add.665), channel_id=1, source_target_pairs={{16,0},{20,4},{24,8},{28,12},{0,16},{4,20},{8,24},{12,28},{17,1},{... | collective-permute-start | bytes 116744 | tf_op jit(solution)/shard_map/ppermute | solution.py:799
  (87 other events, 703.6 us)

commit v4 on v3

--- a/solution.py
+++ b/solution.py
@@ -1352,12 +1352,6 @@
         grad_value = summed(late_ways).reshape(width // copies, channels)
         least = summed(least_ways).reshape(width // copies, half + lanes)
         grad_rate = least[:, half : half + heads]
-        part = gather_rows(least[:, :half].astype(BF16), x, z)
-        other = from_core(part)
-        grad_shared = jnp.where(
-            core == 0, jnp.concatenate([part, other], axis=1), jnp.concatenate([other, part], axis=1)
-        ).astype(F32)
-
         head_out = sum(head_sums_[1:], head_sums_[0])
         smalls = []
         for j in blocks:
@@ -1372,7 +1366,6 @@
         shared_sums = jnp.where(core == 0, shared_sums, 0.0)
         alls = jnp.concatenate([shared_sums, grad_norm.reshape(-1, maps)], axis=0)
         alls = alls.reshape(-1, lanes)
-        alls = alls + from_core(alls)
         size = smalls[0].size // lanes
         ways = [jnp.concatenate([smalls[0].reshape(-1, lanes), alls], axis=0)]
         for j in range(1, ny):
@@ -1382,9 +1375,33 @@
         if ny > 1:
             ways = jnp.stack([way[size:] for way in ways])
             alls = summed([lax.dynamic_index_in_dim(ways, (y - k) % ny, 0, False) for k in range(ny)])
-        both = sum_rows(jnp.concatenate([own, alls], axis=0))
+        both = jnp.concatenate([own, alls], axis=0)
+
+        part = least[:, :half].reshape(-1, lanes)
+        each = part.shape[0]
+        part = part[None]
+
+        def step(pairs, axis):
+            sent = jnp.concatenate([part.reshape(-1, lanes), both], axis=0)
+            got = lax.ppermute(sent, axis, pairs)
+            return got[: part.size // lanes].reshape(part.shape), got[part.size // lanes :]
+
+        def joined_parts(high, other):
+            pair = [jnp.where(high, other, part), jnp.where(high, part, other)]
+            return jnp.stack(pair, axis=1).reshape(-1, each, lanes)
+
+        bit = copies // 2
+        while bit >= 1:
+            got, more = step([(d ^ bit, d) for d in range(copies)], "dp")
+            part, both = joined_parts((dp // bit) % 2 == 1, got), both + more
+            bit //= 2
+        got, more = step([(t ^ 1, t) for t in range(tensor)], "tensor")
+        part, got = part.reshape(width, half), got.reshape(width, half)
+        grad_shared = jnp.concatenate(
+            [jnp.where(core == 0, part, got), jnp.where(core == 0, got, part)], axis=1
+        )
         own = both[:size].reshape(smalls[0].shape)
-        alls = both[size:].reshape(-1, maps)
+        alls = (both[size:] + more[size:]).reshape(-1, maps)
         return (
             block_out,
             tokens_grad,

time: 586 us -> 613 us (1.046)
  waiting for transfers between devices: 42.6 us -> 81.1 us
  starting transfers between devices: 54.7 us -> 47.8 us
    ppermute x8, waiting for transfers between devices: 1.43 us -> 30 us  [ways_z(): return [kept, lax.ppermute(sent.astype(BF16), 'dp', pairs)]]
    ppermute x9 -> x8, waiting for transfers between devices: 7.53 us -> 27.2 us  [from_x(): return lax.ppermute(member, 'dp', pairs)]
    ppermute x5 -> x4, waiting for transfers between devices: 19.9 us -> 12.2 us  [step(): got = lax.ppermute(sent, axis, pairs)]
    unnamed x150 -> x146, local copies, waits for them, and re-layouts: 10.7 us -> 13.2 us
  transfers between devices with their start and end apart: 46 -> 42, of which waited for: 14 -> 15; matrix products, arithmetic and copies ran while one was open for 36% -> 32% of each run, Pallas kernels for 38% -> 37%
where the time goes in v4:
time: 613 us; the launch traced here: 602 us
  Pallas kernels  251 us (41%)
  matrix products  111 us (18%)
  waiting for transfers between devices  81.1 us (13%)
  local copies, waits for them, and re-layouts  52.8 us (9%)
  other arithmetic  50.1 us (8%)
  starting transfers between devices  47.8 us (8%)
  between operations  9.09 us (1%)
    pallas_call x16, Pallas kernels, call(): pl.pallas_call(kernel, grid_spec=pltpu.PrefetchScalarGridSpec(num_scalar_...  251 us
    dot_general x14, matrix products, dot(): lax.dot_general(a, b, dims, precision=precision, preferred_element_type=F32)  111 us
    ppermute x8, waiting for transfers between devices, ways_z(): return [kept, lax.ppermute(sent.astype(BF16), 'dp', pairs)]  30 us
    ppermute x8, waiting for transfers between devices, from_x(): return lax.ppermute(member, 'dp', pairs)  27.2 us
    ppermute x9, starting transfers between devices, from_y(): return lax.ppermute(member, 'tensor', pairs)  15.2 us
    add x12, other arithmetic, summed(): total = total + (part if one is None else part * one[0, 0])  14.8 us
    unnamed x146, local copies, waits for them, and re-layouts  13.2 us
    ppermute x6, starting transfers between devices, next_y(): return lax.ppermute(member, 'tensor', pairs)  12.7 us
  transfers between devices with their start and end apart: 42, of which 15 were waited for; matrix products, arithmetic and copies ran while one was open for 32% of the time, Pallas kernels for 37%

profile of v4, /device:TPU:0, one launch (start us, length us, event | category | flops | bytes accessed | tf_op | source)
XLA Modules:
  0.0 602.3 jit_solution(18109235280010571078)
XLA Ops:
  29.6 7.5 %chip_rows.2 = (bf16[2176,1536]{1,0:T(8,128)(2,1)}, f32[8,128]{1,0:T(8,128)}) custom-call(s32[1]{0:T(128)} %bitcast.3.scal, bf16[1024,1536]{1,0:T(8,128)(2,1)} %refs_12_.1, bf16[1024,1536]{1,0:T(8,128)(2,1)} %collective-permute-done.refs_1_, f32[1,1536]{1,0:T(1,128)} %reshape.280.refs_2_.refs_15_), custom_call_target="tpu_custom_call" | custom-call | flops 8049999872 | bytes 100000 | tf_op jit(solution)/shard_map/chip_rows/pallas_call | solution.py:696
  37.8 9.9 %convolution_convert_fusion.3.refs_0_.refs_1_.refs_4_.refs_5_ = bf16[2176,768]{1,0:T(8,128)(2,1)} fusion(bf16[2176,1536]{1,0:T(8,128)(2,1)} %fusion.18, bf16[1536,768]{1,0:T(8,128)(2,1)S(1)} %copy-done.9), kind=kOutput, calls=%fused_computation.3 | convolution fusion | flops 5135499264 | bytes 12386304 | tf_op jit(solution)/shard_map/dot_general | solution.py:35
  57.6 10.4 %prepare.1 = (bf16[2048,256]{1,0:T(8,128)(2,1)}, bf16[256,2048]{1,0:T(8,128)(2,1)}, f32[2048,128]{1,0:T(8,128)}, bf16[2048,128]{1,0:T(8,128)(2,1)}, bf16[2048,12...) custom-call(s32[5]{0:T(128)} %pad_add_fusion.scal, ...), custom_call_target="tpu_custom_call" | custom-call | flops 11500000256 | bytes 100000 | tf_op jit(solution)/shard_map/prepare/pallas_call | solution.py:696
  68.0 13.4 %states.2 = (bf16[2048,768]{1,0:T(8,128)(2,1)}, bf16[2048,768]{1,0:T(8,128)(2,1)}, bf16[16,128,768]{2,1,0:T(8,128)(2,1)}, f32[128,768]{1,0:T(8,128)}, f32[8,768]{1,0:T(8,128)}, /*index=5*/f32[8,128]{1,0:T(8,128)}) custom-call(s32[5]{0:T(128)} %pad_add_fusion.scal, bf16[2176,768]{1,0:T(8,128)(2,1)} %convolution_convert_fusion.3.refs_0_.refs_1_.refs_4_.refs_5_, ...), custom_call_target="tpu_custom_call" | custom-call | flops 14949999616 | bytes 100000 | tf_op jit(solution)/shard_map/states/pallas_call | solution.py:696
  82.1 7.4 %chip_rows.3 = (bf16[2048,1536]{1,0:T(8,128)(2,1)}, f32[8,128]{1,0:T(8,128)}) custom-call(s32[1]{0:T(128)} %bitcast.3.scal, bf16[1024,1536]{1,0:T(8,128)(2,1)} %refs_14_.1, bf16[1024,1536]{1,0:T(8,128)(2,1)} %collective-permute-done.4.refs_1_), custom_call_target="tpu_custom_call" | custom-call | flops 8049999872 | bytes 100000 | tf_op jit(solution)/shard_map/chip_rows/pallas_call | solution.py:696
  92.7 9.9 %convolution_convert_fusion.2.refs_0_.refs_1_.refs_4_.refs_5_ = bf16[2176,768]{1,0:T(8,128)(2,1)} fusion(bf16[2176,1536]{1,0:T(8,128)(2,1)} %fusion.18, bf16[1536,768]{1,0:T(8,128)(2,1)S(1)} %constant_dynamic-update-slice_fusion.5.refs_9_.refs_11_), kind=kOutput, calls=%fused_computation.2 | convolution fusion | flops 5135499264 | bytes 12386304 | tf_op jit(solution)/shard_map/dot_general | solution.py:35
  102.6 6.7 %convolution_convert_fusion.1.refs_10_.refs_2_ = bf16[2176,768]{1,0:T(8,128)(2,1)} fusion(bf16[2176,1536]{1,0:T(8,128)(2,1)S(1)} %bitcast.213, bf16[1536,768]{1,0:T(8,128)(2,1)S(1)} %copy-done.10), kind=kOutput, calls=%fused_computation.1 | convolution fusion | flops 5135499264 | bytes 12386304 | tf_op jit(solution)/shard_map/dot_general | solution.py:35
  109.3 13.4 %states.3 = (bf16[2048,768]{1,0:T(8,128)(2,1)}, bf16[2048,768]{1,0:T(8,128)(2,1)}, bf16[16,128,768]{2,1,0:T(8,128)(2,1)}, f32[128,768]{1,0:T(8,128)}, f32[8,768]{1,0:T(8,128)}, /*index=5*/f32[8,128]{1,0:T(8,128)}) custom-call(s32[5]{0:T(128)} %pad_add_fusion.scal, bf16[2176,768]{1,0:T(8,128)(2,1)} %convolution_convert_fusion.2.refs_0_.refs_1_.refs_4_.refs_5_, ...), custom_call_target="tpu_custom_call" | custom-call | flops 14949999616 | bytes 100000 | tf_op jit(solution)/shard_map/states/pallas_call | solution.py:696
  126.8 9.8 %convolution_convert_fusion.10.refs_11_.refs_3_ = bf16[2048,768]{1,0:T(8,128)(2,1)} fusion(bf16[2048,1536]{1,0:T(8,128)(2,1)} %get-tuple-element.167, bf16[768,1536]{1,0:T(8,128)(2,1)S(1)} %copy-done.6), kind=kOutput, calls=%fused_computation.12 | convolution fusion | flops 4833411072 | bytes 11796480 | tf_op jit(solution)/shard_map/dot_general | solution.py:35
  143.2 14.5 %scan.2 = (f32[2048,768]{1,0:T(8,128)}, f32[8,2048]{1,0:T(8,128)}, f32[8,128]{1,0:T(8,128)}) custom-call(s32[5]{0:T(128)} %pad_add_fusion.scal, bf16[2048,768]{1,0:T(8,128)(2,1)} %get-tuple-element.180.refs_0_.refs_1_, bf16[2048,256]{1,0:T(8,128)(2,1)} %get-tuple-element.130.refs_1_.refs_8_, f32[2048,128]{1,0:T(8,128)} %get-tuple-element.119.refs_4_.refs_2_.refs_6_.refs_10_, ...), custom_call_target="tpu_custom_call" | custom-call | flops 17250000896 | bytes 100000 | tf_op jit(solution)/shard_map/scan/pallas_call | solution.py:696
  159.3 10.7 %convolution_convert_fusion.refs_10_.refs_2_ = bf16[2176,768]{1,0:T(8,128)(2,1)} fusion(bf16[2176,1536]{1,0:T(8,128)(2,1)} %fusion.18, bf16[1536,768]{1,0:T(8,128)(2,1)S(1)} %constant_dynamic-update-slice_fusion.3.refs_7_.refs_9_), kind=kOutput, calls=%fused_computation | convolution fusion | flops 5135499264 | bytes 12386304 | tf_op jit(solution)/shard_map/dot_general | solution.py:35
  171.5 6.5 %convolution_convert_fusion.9.refs_11_.refs_3_ = bf16[2048,768]{1,0:T(8,128)(2,1)} fusion(bf16[2048,1536]{1,0:T(8,128)(2,1)S(1)} %bitcast.219, bf16[768,1536]{1,0:T(8,128)(2,1)S(1)} %constant_dynamic-update-slice_fusion.1.refs_3_), kind=kOutput, calls=%fused_computation.11 | convolution fusion | flops 4833411072 | bytes 11796480 | tf_op jit(solution)/shard_map/dot_general | solution.py:35
  178.0 14.7 %scan.3 = (f32[2048,768]{1,0:T(8,128)}, f32[8,2048]{1,0:T(8,128)}, f32[8,128]{1,0:T(8,128)}) custom-call(s32[5]{0:T(128)} %pad_add_fusion.scal, bf16[2048,768]{1,0:T(8,128)(2,1)} %get-tuple-element.169.refs_0_.refs_1_, bf16[2048,256]{1,0:T(8,128)(2,1)} %get-tuple-element.130.refs_1_.refs_8_, f32[2048,128]{1,0:T(8,128)} %get-tuple-element.119.refs_4_.refs_2_.refs_6_.refs_10_, ...), custom_call_target="tpu_custom_call" | custom-call | flops 17250000896 | bytes 100000 | tf_op jit(solution)/shard_map/scan/pallas_call | solution.py:696
  203.2 15.9 %gate_back.2 = (bf16[2048,768]{1,0:T(8,128)(2,1)}, bf16[2176,768]{1,0:T(8,128)(2,1)}, bf16[2048,768]{1,0:T(8,128)(2,1)}, f32[128,768]{1,0:T(8,128)}, f32[8,768]{1,0:T(8,128)}, /*index=5*/f32[8,128]{1,0:T(8,128)}) custom-call(s32[5]{0:T(128)} %pad_add_fusion.scal, f32[2048,768]{1,0:T(8,128)} %get-tuple-element.145.refs_0_.refs_3_, ...), custom_call_target="tpu_custom_call" | custom-call | flops 18400000000 | bytes 100000 | tf_op jit(solution)/shard_map/gate_back/pallas_call | solution.py:696
  220.5 15.8 %gate_back.3 = (bf16[2048,768]{1,0:T(8,128)(2,1)}, bf16[2176,768]{1,0:T(8,128)(2,1)}, bf16[2048,768]{1,0:T(8,128)(2,1)}, f32[128,768]{1,0:T(8,128)}, f32[8,768]{1,0:T(8,128)}, /*index=5*/f32[8,128]{1,0:T(8,128)}) custom-call(s32[5]{0:T(128)} %pad_add_fusion.scal, f32[2048,768]{1,0:T(8,128)} %get-tuple-element.153.refs_0_.refs_3_, ...), custom_call_target="tpu_custom_call" | custom-call | flops 18400000000 | bytes 100000 | tf_op jit(solution)/shard_map/gate_back/pallas_call | solution.py:696
  238.8 9.4 %convolution_convert_fusion.8 = bf16[1536,768]{1,0:T(8,128)(2,1)} fusion(bf16[2048,1536]{1,0:T(8,128)(2,1)} %get-tuple-element.167, bf16[2048,768]{1,0:T(8,128)(2,1)} %get-tuple-element.177.refs_1_), kind=kOutput, calls=%fused_computation.10 | convolution fusion | flops 4833017856 | bytes 11796480 | tf_op jit(solution)/shard_map/dot_general | solution.py:35
  248.3 8.1 %convolution_convert_fusion.7 = bf16[1536,768]{1,0:T(8,128)(2,1)S(1)} fusion(bf16[2176,1536]{1,0:T(8,128)(2,1)} %fusion.18, bf16[2176,768]{1,0:T(8,128)(2,1)S(1)} %copy-done.60), kind=kOutput, calls=%fused_computation.9 | convolution fusion | flops 5135007744 | bytes 12386304 | tf_op jit(solution)/shard_map/dot_general | solution.py:35
  265.4 6.4 %convolution_convert_fusion.5 = bf16[1536,768]{1,0:T(8,128)(2,1)} fusion(bf16[2048,1536]{1,0:T(8,128)(2,1)S(1)} %bitcast.221, bf16[2048,768]{1,0:T(8,128)(2,1)S(1)} %copy-done.58), kind=kOutput, calls=%fused_computation.7 | convolution fusion | flops 4833017856 | bytes 11796480 | tf_op jit(solution)/shard_map/dot_general | solution.py:35
  275.6 33.3 %scan_back.2 = (bf16[2176,768]{1,0:T(8,128)(2,1)}, f32[2048,256]{1,0:T(8,128)}, bf16[2176,128]{1,0:T(8,128)(2,1)}, f32[8,768]{1,0:T(8,128)}, f32[8,128]{1,0:T(8,...) custom-call(s32[5]{0:T(128)} %pad_add_fusion.scal, ...), custom_call_target="tpu_custom_call" | custom-call | flops 37950001152 | bytes 100000 | tf_op jit(solution)/shard_map/scan_back/pallas_call | solution.py:696
  313.4 9.0 %convolution_convert_fusion.4 = bf16[1536,768]{1,0:T(8,128)(2,1)} fusion(bf16[2176,1536]{1,0:T(8,128)(2,1)} %fusion.18, bf16[2176,768]{1,0:T(8,128)(2,1)S(1)} %copy-done.53), kind=kOutput, calls=%fused_computation.6 | convolution fusion | flops 5135007744 | bytes 12386304 | tf_op jit(solution)/shard_map/dot_general | solution.py:35
  330.4 11.0 %out_other.1 = (bf16[1024,1536]{1,0:T(8,128)(2,1)}, f32[8,128]{1,0:T(8,128)}) custom-call(s32[1]{0:T(128)} %bitcast.15.scal, bf16[2048,768]{1,0:T(8,128)(2,1)} %get-tuple-element.176.refs_0_, bf16[2048,768]{1,0:T(8,128)(2,1)} %get-tuple-element.177.refs_1_, bf16[768,1536]{1,0:T(8,128)(2,1)} %refs_2_.3, bf16[768,1536]{1,0:T(8,128)(2,1)} %copy-done.15), custom_call_target="tpu_custom_call" | custom-call | flops 10350000128 | bytes 100000 | tf_op jit(solution)/shard_map/out_other/pallas_call | solution.py:696
  343.5 33.1 %scan_back.3 = (bf16[2176,768]{1,0:T(8,128)(2,1)}, f32[2048,256]{1,0:T(8,128)}, bf16[2176,128]{1,0:T(8,128)(2,1)}, f32[8,768]{1,0:T(8,128)}, f32[8,128]{1,0:T(8,...) custom-call(s32[5]{0:T(128)} %pad_add_fusion.scal, ...), custom_call_target="tpu_custom_call" | custom-call | flops 37950001152 | bytes 100000 | tf_op jit(solution)/shard_map/scan_back/pallas_call | solution.py:696
  404.2 10.5 %out_own.1 = (bf16[1024,1536]{1,0:T(8,128)(2,1)}, f32[8,128]{1,0:T(8,128)}) custom-call(s32[1]{0:T(128)} %bitcast.scal, bf16[2048,768]{1,0:T(8,128)(2,1)} %get-tuple-element.176.refs_0_, bf16[2048,768]{1,0:T(8,128)(2,1)} %get-tuple-element.177.refs_1_, bf16[768,1536]{1,0:T(8,128)(2,1)} %refs_2_.3, bf16[768,1536]{1,0:T(8,128)(2,1)} %copy-done.15, ...), custom_call_target="tpu_custom_call" | custom-call | flops 12650000384 | bytes 100000 | tf_op jit(solution)/shard_map/out_own/pallas_call | solution.py:696
  414.7 9.8 %shared_back.1 = (bf16[2176,256]{1,0:T(8,128)(2,1)}, f32[8,256]{1,0:T(8,128)}, f32[8,256]{1,0:T(8,128)}, f32[8,256]{1,0:T(8,128)}, f32[8,128]{1,0:T(8,128)}) custom-call(s32[5]{0:T(128)} %pad_add_fusion.scal, f32[2048,256]{1,0:T(8,128)} %add.296.refs_6_.refs_0_, f32[2048,256]{1,0:T(8,128)} %collective-permute-done.19.refs_1_, ...), custom_call_target="tpu_custom_call" | custom-call | flops 11500000256 | bytes 100000 | tf_op jit(solution)/shard_map/shared_back/pallas_call | solution.py:696
  444.0 9.4 %multiply_add_fusion.refs_10_ = f32[1536,768]{1,0:T(8,128)} fusion(bf16[1536,768]{1,0:T(8,128)(2,1)} %collective-permute-done.22, bf16[2176,1536]{1,0:T(8,128)(2,1)S(1)} %bitcast.217, bf16[2176,768]{1,0:T(8,128)(2,1)S(1)} %copy-done.54, f32[]{:T(128)} %bitcast.27), kind=kOutput, calls=%fused_computation.4 | convolution fusion | flops 5137367040 | bytes 17104900 | tf_op jit(solution)/shard_map/dot_general | solution.py:35
  455.9 17.2 %back_other.1 = (bf16[1024,1536]{1,0:T(8,128)(2,1)}, f32[8,128]{1,0:T(8,128)}) custom-call(s32[1]{0:T(128)} %bitcast.15.scal, bf16[2176,128]{1,0:T(8,128)(2,1)} %add.633.refs_0_.refs_1_, bf16[2176,768]{1,0:T(8,128)(2,1)} %get-tuple-element.166.refs_1_.refs_2_, bf16[2176,768]{1,0:T(8,128)(2,1)} %get-tuple-element.164.refs_2_.refs_3_, ...), custom_call_target="tpu_custom_call" | custom-call | flops 19549999104 | bytes 100000 | tf_op jit(solution)/shard_map/back_other/pallas_call | solution.py:696
  479.7 24.3 %collective-permute-done.24 = bf16[4,192,768]{2,1,0:T(8,128)(2,1)S(1)} collective-permute-done((bf16[4,192,768]{2,1,0:T(8,128)(2,1)S(1)}, bf16[4,192,768]{2,1,0:T(8,128)(2,1)S(1)}, u32[]{:S(2)}, u32[]{:S(2)}) %collective-permute-start.24) | collective-permute-done | bytes 1179680 | tf_op jit(solution)/shard_map/ppermute | solution.py:790
  506.5 23.1 %back_own.1 = (f32[1024,1536]{1,0:T(8,128)}, f32[8,1536]{1,0:T(8,128)}, f32[8,128]{1,0:T(8,128)}) custom-call(s32[1]{0:T(128)} %bitcast.scal, bf16[2176,256]{1,0:T(8,128)(2,1)} %constant_dynamic-update-slice_fusion.refs_0_, bf16[2176,128]{1,0:T(8,128)(2,1)} %add.633.refs_0_.refs_1_, bf16[2176,768]{1,0:T(8,128)(2,1)} %get-tuple-element.166.refs_1_.refs_2_, ...), custom_call_target="tpu_custom_call" | custom-call | flops 25300000768 | bytes 100000 | tf_op jit(solution)/shard_map/back_own/pallas_call | solution.py:696
  544.0 6.2 %collective-permute-done.29 = bf16[1,192,256]{2,1,0:T(8,128)(2,1)S(1)} collective-permute-done((bf16[1,192,256]{2,1,0:T(8,128)(2,1)S(1)}, bf16[1,192,256]{2,1,0:T(8,128)(2,1)S(1)}, u32[]{:S(2)}, u32[]{:S(2)}) %collective-permute-start.29) | collective-permute-done | bytes 98336 | tf_op jit(solution)/shard_map/ppermute | solution.py:817
  561.4 7.9 %collective-permute-done.31 = f32[460,128]{1,0:T(8,128)S(1)} collective-permute-done((f32[460,128]{1,0:T(8,128)S(1)}, f32[460,128]{1,0:T(8,128)S(1)}, u32[]{:S(2)}, u32[]{:S(2)}) %collective-permute-start.31) | collective-permute-done | bytes 235552 | tf_op jit(solution)/shard_map/ppermute | solution.py:1386
  569.9 9.9 %collective-permute-done.38 = bf16[2,192,768]{2,1,0:T(8,128)(2,1)S(1)} collective-permute-done((bf16[2,192,768]{2,1,0:T(8,128)(2,1)S(1)}, bf16[2,192,768]{2,1,0:T(8,128)(2,1)S(1)}, u32[]{:S(2)}, u32[]{:S(2)}) %collective-permute-start.38) | collective-permute-done | bytes 589856 | tf_op jit(solution)/shard_map/ppermute | solution.py:817
  581.1 8.0 %collective-permute-done.37 = bf16[1,192,768]{2,1,0:T(8,128)(2,1)S(1)} collective-permute-done((bf16[1,192,768]{2,1,0:T(8,128)(2,1)S(1)}, bf16[1,192,768]{2,1,0:T(8,128)(2,1)S(1)}, u32[]{:S(2)}, u32[]{:S(2)}) %collective-permute-start.37) | collective-permute-done | bytes 294944 | tf_op jit(solution)/shard_map/ppermute | solution.py:817
  (393 shorter events, 190.3 us)
Async XLA Ops:
  0.6 29.0 %collective-permute-start = (bf16[1024,1536]{1,0:T(8,128)(2,1)}, bf16[1024,1536]{1,0:T(8,128)(2,1)}, u32[]{:S(2)}, u32[]{:S(2)}) collective-permute-start(bf16[1024,1536]{1,0:T(8,128)(2,1)} %refs_12_.1), channel_id=1, source_target_pairs={{1,0},{0,1},{3,2},{2,3},{5,4},{4,5},{7,6},{6,7},{9,8},{8,9},{11,10... | collective-permute-start | bytes 9437192 | tf_op jit(solution)/shard_map/ppermute | solution.py:786
  2.0 18.8 %collective-permute-start.1 = (bf16[16,1536]{1,0:T(8,128)(2,1)S(1)}, bf16[16,1536]{1,0:T(8,128)(2,1)S(1)}, u32[]{:S(2)}, u32[]{:S(2)}) collective-permute-start(bf16[16,1536]{1,0:T(8,128)(2,1)S(1)} %slice.183), channel_id=1, source_target_pairs={{0,2},{1,3},{4,6},{5,7},{8,10},{9,11},{12,14},{13,15},{16,18},{17,... | collective-permute-start | bytes 147464 | tf_op jit(solution)/shard_map/ppermute | solution.py:783
  27.9 27.6 %collective-permute-start.5 = (bf16[768,768]{1,0:T(8,128)(2,1)}, bf16[768,768]{1,0:T(8,128)(2,1)S(1)}, u32[]{:S(2)}, u32[]{:S(2)}) collective-permute-start(bf16[768,768]{1,0:T(8,128)(2,1)} %constant_dynamic-slice_fusion.2), channel_id=1, source_target_pairs={{2,0},{3,1},{0,2},{1,3},{6,4},{7,5},{4,6},{5,7},{10,8},{11,9},{8,1... | collective-permute-start | bytes 3538952 | tf_op jit(solution)/shard_map/ppermute | solution.py:774
  29.6 52.4 %collective-permute-start.4 = (bf16[1024,1536]{1,0:T(8,128)(2,1)}, bf16[1024,1536]{1,0:T(8,128)(2,1)}, u32[]{:S(2)}, u32[]{:S(2)}) collective-permute-start(bf16[1024,1536]{1,0:T(8,128)(2,1)} %refs_14_.1), channel_id=1, source_target_pairs={{1,0},{0,1},{3,2},{2,3},{5,4},{4,5},{7,6},{6,7},{9,8},{8,9},{11,10... | collective-permute-start | bytes 9437192 | tf_op jit(solution)/shard_map/ppermute | solution.py:786
  55.5 26.4 %collective-permute-start.7 = (bf16[768,768]{1,0:T(8,128)(2,1)S(1)}, bf16[768,768]{1,0:T(8,128)(2,1)S(1)}, u32[]{:S(2)}, u32[]{:S(2)}) collective-permute-start(bf16[768,768]{1,0:T(8,128)(2,1)S(1)} %collective-permute-done.5), channel_id=1, source_target_pairs={{4,0},{0,4},{12,8},{8,12},{20,16},{16,20},{28,24},{24,28},{5,1},{1... | collective-permute-start | bytes 3538952 | tf_op jit(solution)/shard_map/ppermute | solution.py:790
  57.0 32.5 %collective-permute-start.6 = (bf16[768,768]{1,0:T(8,128)(2,1)}, bf16[768,768]{1,0:T(8,128)(2,1)}, u32[]{:S(2)}, u32[]{:S(2)}) collective-permute-start(bf16[768,768]{1,0:T(8,128)(2,1)} %constant_dynamic-slice_fusion.3), channel_id=1, source_target_pairs={{2,0},{3,1},{0,2},{1,3},{6,4},{7,5},{4,6},{5,7},{10,8},{11,9},{8,1... | collective-permute-start | bytes 3538952 | tf_op jit(solution)/shard_map/ppermute | solution.py:774
  89.5 68.2 %collective-permute-start.10 = (bf16[768,768]{1,0:T(8,128)(2,1)}, bf16[768,768]{1,0:T(8,128)(2,1)}, u32[]{:S(2)}, u32[]{:S(2)}) collective-permute-start(bf16[768,768]{1,0:T(8,128)(2,1)} %collective-permute-done.6.refs_10_), channel_id=1, source_target_pairs={{4,0},{0,4},{12,8},{8,12},{20,16},{16,20},{28,24},{24,28},{5,1},{1... | collective-permute-start | bytes 3538952 | tf_op jit(solution)/shard_map/ppermute | solution.py:790
  91.0 52.0 %collective-permute-start.9 = (bf16[384,1536]{1,0:T(8,128)(2,1)S(1)}, bf16[384,1536]{1,0:T(8,128)(2,1)}, u32[]{:S(2)}, u32[]{:S(2)}) collective-permute-start(bf16[384,1536]{1,0:T(8,128)(2,1)S(1)} %copy-done.21), channel_id=1, source_target_pairs={{2,0},{3,1},{0,2},{1,3},{6,4},{7,5},{4,6},{5,7},{10,8},{11,9},{8,1... | collective-permute-start | bytes 3538952 | tf_op jit(solution)/shard_map/ppermute | solution.py:774
  123.8 18.2 %collective-permute-start.8 = (f32[256,768]{1,0:T(8,128)S(1)}, f32[256,768]{1,0:T(8,128)S(1)}, u32[]{:S(2)}, u32[]{:S(2)}) collective-permute-start(f32[256,768]{1,0:T(8,128)S(1)} %pad_maximum_fusion.2), channel_id=1, source_target_pairs={{0,2},{1,3},{4,6},{5,7},{8,10},{9,11},{12,14},{13,15},{16,18},{17,... | collective-permute-start | bytes 2359304 | tf_op jit(solution)/shard_map/ppermute | solution.py:783
  143.0 28.3 %collective-permute-start.11 = (bf16[384,1536]{1,0:T(8,128)(2,1)}, bf16[384,1536]{1,0:T(8,128)(2,1)S(1)}, u32[]{:S(2)}, u32[]{:S(2)}) collective-permute-start(bf16[384,1536]{1,0:T(8,128)(2,1)} %collective-permute-done.9.refs_15_), channel_id=1, source_target_pairs={{4,0},{0,4},{12,8},{8,12},{20,16},{16,20},{28,24},{24,28},{5,1},{1... | collective-permute-start | bytes 3538952 | tf_op jit(solution)/shard_map/ppermute | solution.py:790
  219.2 53.0 %collective-permute-start.13 = (f32[128,768]{1,0:T(8,128)}, f32[128,768]{1,0:T(8,128)S(1)}, u32[]{:S(2)}, u32[]{:S(2)}) collective-permute-start(f32[128,768]{1,0:T(8,128)} %get-tuple-element.158), channel_id=1, source_target_pairs={{2,0},{3,1},{6,4},{7,5},{10,8},{11,9},{14,12},{15,13},{18,16},{19,... | collective-permute-start | bytes 1179656 | tf_op jit(solution)/shard_map/ppermute | solution.py:783
  236.3 107.2 %collective-permute-start.17 = (f32[128,768]{1,0:T(8,128)}, f32[128,768]{1,0:T(8,128)}, u32[]{:S(2)}, u32[]{:S(2)}) collective-permute-start(f32[128,768]{1,0:T(8,128)} %get-tuple-element.161), channel_id=1, source_target_pairs={{2,0},{3,1},{6,4},{7,5},{10,8},{11,9},{14,12},{15,13},{18,16},{19,... | collective-permute-start | bytes 1179656 | tf_op jit(solution)/shard_map/ppermute | solution.py:783
  257.5 68.1 %collective-permute-start.34 = (bf16[4,192,768]{2,1,0:T(8,128)(2,1)}, bf16[4,192,768]{2,1,0:T(8,128)(2,1)}, u32[]{:S(2)}, u32[]{:S(2)}) collective-permute-start(bf16[4,192,768]{2,1,0:T(8,128)(2,1)} %dynamic-slice_bitcast_fusion), channel_id=1, source_target_pairs={{4,0},{0,4},{12,8},{8,12},{20,16},{16,20},{28,24},{24,28},{5,1},{1... | collective-permute-start | bytes 3538952 | tf_op jit(solution)/shard_map/ppermute | solution.py:790
  271.9 39.5 %collective-permute-start.15 = (bf16[4,192,768]{2,1,0:T(8,128)(2,1)S(1)}, bf16[4,192,768]{2,1,0:T(8,128)(2,1)S(1)}, u32[]{:S(2)}, u32[]{:S(2)}) collective-permute-start(bf16[4,192,768]{2,1,0:T(8,128)(2,1)S(1)} %dynamic-slice_bitcast_fusion.1), channel_id=1, source_target_pairs={{4,0},{0,4},{12,8},{8,12},{20,16},{16,20},{28,24},{24,28},{5,1},{1... | collective-permute-start | bytes 3538952 | tf_op jit(solution)/shard_map/ppermute | solution.py:790
  272.2 56.0 %collective-permute-start.14 = (bf16[1536,768]{1,0:T(8,128)(2,1)}, bf16[1536,768]{1,0:T(8,128)(2,1)}, u32[]{:S(2)}, u32[]{:S(2)}) collective-permute-start(bf16[1536,768]{1,0:T(8,128)(2,1)} %convolution_convert_fusion.8), channel_id=1, source_target_pairs={{2,0},{3,1},{0,2},{1,3},{6,4},{7,5},{4,6},{5,7},{10,8},{11,9},{8,1... | collective-permute-start | bytes 7077896 | tf_op jit(solution)/shard_map/ppermute | solution.py:774
  322.3 121.6 %collective-permute-start.22 = (bf16[1536,768]{1,0:T(8,128)(2,1)}, bf16[1536,768]{1,0:T(8,128)(2,1)}, u32[]{:S(2)}, u32[]{:S(2)}) collective-permute-start(bf16[1536,768]{1,0:T(8,128)(2,1)} %convolution_convert_fusion.4), channel_id=1, source_target_pairs={{2,0},{3,1},{0,2},{1,3},{6,4},{7,5},{4,6},{5,7},{10,8},{11,9},{8,1... | collective-permute-start | bytes 7077896 | tf_op jit(solution)/shard_map/ppermute | solution.py:774
  341.4 62.8 %collective-permute-start.16 = (bf16[1024,1536]{1,0:T(8,128)(2,1)}, bf16[1024,1536]{1,0:T(8,128)(2,1)}, u32[]{:S(2)}, u32[]{:S(2)}) collective-permute-start(bf16[1024,1536]{1,0:T(8,128)(2,1)} %get-tuple-element.178), channel_id=1, source_target_pairs={{1,0},{0,1},{3,2},{2,3},{5,4},{4,5},{7,6},{6,7},{9,8},{8,9},{11,10... | collective-permute-start | bytes 9437192 | tf_op jit(solution)/shard_map/ppermute | solution.py:786
  341.6 57.9 %collective-permute-start.18 = (bf16[4,192,768]{2,1,0:T(8,128)(2,1)S(1)}, bf16[4,192,768]{2,1,0:T(8,128)(2,1)}, u32[]{:S(2)}, u32[]{:S(2)}) collective-permute-start(bf16[4,192,768]{2,1,0:T(8,128)(2,1)S(1)} %fusion.1), channel_id=1, source_target_pairs={{4,0},{0,4},{12,8},{8,12},{20,16},{16,20},{28,24},{24,28},{5,1},{1... | collective-permute-start | bytes 3538952 | tf_op jit(solution)/shard_map/ppermute | solution.py:790
  387.7 27.0 %collective-permute-start.19 = (f32[2048,256]{1,0:T(8,128)}, f32[2048,256]{1,0:T(8,128)}, u32[]{:S(2)}, u32[]{:S(2)}) collective-permute-start(f32[2048,256]{1,0:T(8,128)} %add.296.refs_6_.refs_0_), channel_id=1, source_target_pairs={{1,0},{0,1},{3,2},{2,3},{5,4},{4,5},{7,6},{6,7},{9,8},{8,9},{11,10... | collective-permute-start | bytes 6291464 | tf_op jit(solution)/shard_map/ppermute | solution.py:786
  394.6 36.8 %collective-permute-start.35 = (bf16[4,192,768]{2,1,0:T(8,128)(2,1)}, bf16[4,192,768]{2,1,0:T(8,128)(2,1)S(1)}, u32[]{:S(2)}, u32[]{:S(2)}) collective-permute-start(bf16[4,192,768]{2,1,0:T(8,128)(2,1)} %fusion), channel_id=1, source_target_pairs={{2,0},{3,1},{0,2},{1,3},{6,4},{7,5},{4,6},{5,7},{10,8},{11,9},{8,1... | collective-permute-start | bytes 3538952 | tf_op jit(solution)/shard_map/ppermute | solution.py:774
  402.6 24.6 %collective-permute-start.40 = (bf16[2,192,768]{2,1,0:T(8,128)(2,1)S(1)}, bf16[2,192,768]{2,1,0:T(8,128)(2,1)S(1)}, u32[]{:S(2)}, u32[]{:S(2)}) collective-permute-start(bf16[2,192,768]{2,1,0:T(8,128)(2,1)S(1)} %fusion.12), channel_id=1, source_target_pairs={{8,0},{12,4},{0,8},{4,12},{24,16},{28,20},{16,24},{20,28},{9,1},{1... | collective-permute-start | bytes 1769480 | tf_op jit(solution)/shard_map/ppermute | solution.py:817
  425.7 49.5 %collective-permute-start.20 = (f32[8,256]{1,0:T(8,128)}, f32[8,256]{1,0:T(8,128)S(1)}, u32[]{:S(2)}, u32[]{:S(2)}) collective-permute-start(f32[8,256]{1,0:T(8,128)} %get-tuple-element.189), channel_id=1, source_target_pairs={{2,0},{3,1},{6,4},{7,5},{10,8},{11,9},{14,12},{15,13},{18,16},{19,... | collective-permute-start | bytes 24584 | tf_op jit(solution)/shard_map/ppermute | solution.py:783
  428.8 121.6 %collective-permute-start.41 = (bf16[1,192,768]{2,1,0:T(8,128)(2,1)}, bf16[1,192,768]{2,1,0:T(8,128)(2,1)}, u32[]{:S(2)}, u32[]{:S(2)}) collective-permute-start(bf16[1,192,768]{2,1,0:T(8,128)(2,1)} %dynamic-slice_convert_fusion.2), channel_id=1, source_target_pairs={{16,0},{20,4},{24,8},{28,12},{0,16},{4,20},{8,24},{12,28},{17,1},{... | collective-permute-start | bytes 884744 | tf_op jit(solution)/shard_map/ppermute | solution.py:817
  434.8 122.6 %collective-permute-start.36 = (bf16[2,192,768]{2,1,0:T(8,128)(2,1)}, bf16[2,192,768]{2,1,0:T(8,128)(2,1)}, u32[]{:S(2)}, u32[]{:S(2)}) collective-permute-start(bf16[2,192,768]{2,1,0:T(8,128)(2,1)} %fusion.10), channel_id=1, source_target_pairs={{8,0},{12,4},{0,8},{4,12},{24,16},{28,20},{16,24},{20,28},{9,1},{1... | collective-permute-start | bytes 1769480 | tf_op jit(solution)/shard_map/ppermute | solution.py:817
  441.2 34.9 %collective-permute-start.25 = (bf16[1536,256]{1,0:T(8,128)(2,1)S(1)}, bf16[1536,256]{1,0:T(8,128)(2,1)S(1)}, u32[]{:S(2)}, u32[]{:S(2)}) collective-permute-start(bf16[1536,256]{1,0:T(8,128)(2,1)S(1)} %convolution_convert_fusion.11.refs_11_), channel_id=1, source_target_pairs={{2,0},{3,1},{0,2},{1,3},{6,4},{7,5},{4,6},{5,7},{10,8},{11,9},{8,1... | collective-permute-start | bytes 2359304 | tf_op jit(solution)/shard_map/ppermute | solution.py:774
  473.1 33.3 %collective-permute-start.23 = (bf16[1024,1536]{1,0:T(8,128)(2,1)}, bf16[1024,1536]{1,0:T(8,128)(2,1)}, u32[]{:S(2)}, u32[]{:S(2)}) collective-permute-start(bf16[1024,1536]{1,0:T(8,128)(2,1)} %get-tuple-element.198), channel_id=1, source_target_pairs={{1,0},{0,1},{3,2},{2,3},{5,4},{4,5},{7,6},{6,7},{9,8},{8,9},{11,10... | collective-permute-start | bytes 9437192 | tf_op jit(solution)/shard_map/ppermute | solution.py:786
  475.2 28.8 %collective-permute-start.24 = (bf16[4,192,768]{2,1,0:T(8,128)(2,1)S(1)}, bf16[4,192,768]{2,1,0:T(8,128)(2,1)S(1)}, u32[]{:S(2)}, u32[]{:S(2)}) collective-permute-start(bf16[4,192,768]{2,1,0:T(8,128)(2,1)S(1)} %fusion.2), channel_id=1, source_target_pairs={{4,0},{0,4},{12,8},{8,12},{20,16},{16,20},{28,24},{24,28},{5,1},{1... | collective-permute-start | bytes 3538952 | tf_op jit(solution)/shard_map/ppermute | solution.py:790
  477.9 57.2 %collective-permute-start.27 = (bf16[4,192,256]{2,1,0:T(8,128)(2,1)S(1)}, bf16[4,192,256]{2,1,0:T(8,128)(2,1)S(1)}, u32[]{:S(2)}, u32[]{:S(2)}) collective-permute-start(bf16[4,192,256]{2,1,0:T(8,128)(2,1)S(1)} %fusion.13), channel_id=1, source_target_pairs={{4,0},{0,4},{12,8},{8,12},{20,16},{16,20},{28,24},{24,28},{5,1},{1... | collective-permute-start | bytes 1179656 | tf_op jit(solution)/shard_map/ppermute | solution.py:790
  559.3 20.5 %collective-permute-start.38 = (bf16[2,192,768]{2,1,0:T(8,128)(2,1)S(1)}, bf16[2,192,768]{2,1,0:T(8,128)(2,1)S(1)}, u32[]{:S(2)}, u32[]{:S(2)}) collective-permute-start(bf16[2,192,768]{2,1,0:T(8,128)(2,1)S(1)} %fusion.11), channel_id=1, source_target_pairs={{8,0},{12,4},{0,8},{4,12},{24,16},{28,20},{16,24},{20,28},{9,1},{1... | collective-permute-start | bytes 1769480 | tf_op jit(solution)/shard_map/ppermute | solution.py:817
  569.8 19.3 %collective-permute-start.37 = (bf16[1,192,768]{2,1,0:T(8,128)(2,1)S(1)}, bf16[1,192,768]{2,1,0:T(8,128)(2,1)S(1)}, u32[]{:S(2)}, u32[]{:S(2)}) collective-permute-start(bf16[1,192,768]{2,1,0:T(8,128)(2,1)S(1)} %dynamic-slice_convert_fusion.4), channel_id=1, source_target_pairs={{16,0},{20,4},{24,8},{28,12},{0,16},{4,20},{8,24},{12,28},{17,1},{... | collective-permute-start | bytes 884744 | tf_op jit(solution)/shard_map/ppermute | solution.py:817
  580.7 13.6 %collective-permute-start.39 = (bf16[1,192,768]{2,1,0:T(8,128)(2,1)S(1)}, bf16[1,192,768]{2,1,0:T(8,128)(2,1)S(1)}, u32[]{:S(2)}, u32[]{:S(2)}) collective-permute-start(bf16[1,192,768]{2,1,0:T(8,128)(2,1)S(1)} %dynamic-slice_convert_fusion.3), channel_id=1, source_target_pairs={{16,0},{20,4},{24,8},{28,12},{0,16},{4,20},{8,24},{12,28},{17,1},{... | collective-permute-start | bytes 884744 | tf_op jit(solution)/shard_map/ppermute | solution.py:817
  581.1 15.9 %collective-permute-start.33 = (f32[1612,128]{1,0:T(8,128)S(1)}, f32[1612,128]{1,0:T(8,128)}, u32[]{:S(2)}, u32[]{:S(2)}) collective-permute-start(f32[1612,128]{1,0:T(8,128)S(1)} %pad_maximum_fusion.1), channel_id=1, source_target_pairs={{1,0},{0,1},{3,2},{2,3},{5,4},{4,5},{7,6},{6,7},{9,8},{8,9},{11,10... | collective-permute-start | bytes 2476040 | tf_op jit(solution)/shard_map/ppermute | solution.py:1386
  (81 other events, 713.4 us)
